TPU v7x, 32 devices: a whole 2x2x4 slice. The times are simulated.
32 devices in a mesh: fsdp: 8 (over z, x), ctx: 2 (over y), tp: 2 (over core).
Axes of the slice: x: 2, y: 2, z: 4, core: 2. Of those that a mesh axis runs over, the one named last changes fastest.
Arguments:
- latents: float32 [64, 256, 16], P(('fsdp', 'ctx')), may hold values from -6 to 6
- noise: float32 [64, 256, 16], P(('fsdp', 'ctx')), may hold values from -6 to 6
- timesteps: int32 [64], P(('fsdp', 'ctx')), may hold values from 0 to 999
- labels: int32 [64], P(('fsdp', 'ctx')), may hold values from 0 to 999
- owners: int32 [1152], replicated, may hold values from 0 to 15, as said below
- tiles_low: bfloat16 [2, 1152, 128, 128], P('tp', ('fsdp', 'ctx')), may hold values from -0.5 to 0.5
- tiles_master: float32 [2, 1152, 128, 128], P('tp', ('fsdp', 'ctx')), may hold values from -0.5 to 0.5
- tiles_first: float32 [2, 1152, 128, 128], P('tp', ('fsdp', 'ctx')), may hold values from -0.0024414062 to 0.0024414062
- tiles_second: float32 [2, 1152, 128, 128], P('tp', ('fsdp', 'ctx')), may hold values from 2.3689173e-08 to 9.475669e-08
- bases: float32 [2, 1152, 2, 128], P('tp', ('fsdp', 'ctx')), may hold values from -5 to 5
- else_low: bfloat16 [4464640], P(('fsdp', 'ctx', 'tp')), may hold values from -1 to 1
- else_master: float32 [4464640], P(('fsdp', 'ctx', 'tp')), may hold values from -1 to 1
- else_first: float32 [4464640], P(('fsdp', 'ctx', 'tp')), may hold values from -0.0036939091 to 0.0036939091
- else_second: float32 [4464640], P(('fsdp', 'ctx', 'tp')), may hold values from 2.3689174e-08 to 3.0322142e-06
Outputs:
- loss: float32 [], replicated
- grad_norm: float32 [], replicated
- tiles_master_new: float32 [2, 1152, 128, 128], P('tp', ('fsdp', 'ctx'))
- tiles_first_new: float32 [2, 1152, 128, 128], P('tp', ('fsdp', 'ctx'))
- tiles_second_new: float32 [2, 1152, 128, 128], P('tp', ('fsdp', 'ctx'))
- tiles_low_new: bfloat16 [2, 1152, 128, 128], P('tp', ('fsdp', 'ctx'))
- else_master_new: float32 [4464640], P(('fsdp', 'ctx', 'tp'))
- else_first_new: float32 [4464640], P(('fsdp', 'ctx', 'tp'))
- else_second_new: float32 [4464640], P(('fsdp', 'ctx', 'tp'))
- else_low_new: bfloat16 [4464640], P(('fsdp', 'ctx', 'tp'))
Inputs may be any that keep to these rules, and one draw needn't show every extreme that they name: `owners`: each owner is named by exactly 72 tiles.
All inputs are finite; a program needn't handle non-finite values.
Results may differ from a plain program's by a relative error of at most 0.0034.
Values may be sent and summed in bfloat16 or wider, within the bound.
No kernel may reach another device: no remote copies, remote signals or barrier semaphores. Data moves between devices by JAX's collectives and lax.ppermute only.
A program may use at most 448 MiB of HBM per device.

v0:
```python
import math

import jax
import jax.numpy as jnp
from jax import lax
from jax.sharding import PartitionSpec as P

D = 1024
HD = 64
F = 4096
P_SIZE = 16
TFREQ = 256
NCLS = 1000
GRID = 16
L = 2
B = 128


HIGHEST = lax.Precision.HIGHEST
EPS_NORM = 1e-06
RATE = 0.02
DECAY = 0.1


def matmul(left_op, right_op):
    return jnp.dot(left_op, right_op, precision=HIGHEST)


def contract(formula, left_op, right_op):
    return jnp.einsum(formula, left_op, right_op, precision=HIGHEST)


def product(left_op, right_op):
    return jnp.dot(left_op, right_op, preferred_element_type=jnp.float32)


def over_rows(left_op, right_op):
    return lax.dot_general(
        left_op, right_op, (((0,), (0,)), ((), ())), preferred_element_type=jnp.float32
    )


def against(left_op, right_op):
    return lax.dot_general(
        left_op, right_op, (((1,), (1,)), ((), ())), preferred_element_type=jnp.float32
    )


def normed(stream):
    centred = stream - jnp.mean(stream, -1, keepdims=True)
    return centred * lax.rsqrt(jnp.mean(centred * centred, -1, keepdims=True) + EPS_NORM)


def modulate(stream, offset, factor):
    return normed(stream) * (1.0 + factor) + offset


def gelu_tanh(values):
    return jax.nn.gelu(values, approximate=True)


def time_features(time_steps):
    half_count = TFREQ // 2
    freqs = jnp.exp(-math.log(10000.0) * jnp.arange(half_count, dtype=jnp.float32) / half_count)
    angles = time_steps.astype(jnp.float32)[:, None] * freqs[None, :]
    return jnp.concatenate([jnp.cos(angles), jnp.sin(angles)], -1)


def position_table(token_ids):
    quarter = D // 4
    omegas = 1.0 / 10000.0 ** (jnp.arange(quarter, dtype=jnp.float32) / quarter)
    row_angle = (token_ids // GRID).astype(jnp.float32)[:, None] * omegas[None, :]
    col_angle = (token_ids % GRID).astype(jnp.float32)[:, None] * omegas[None, :]
    return jnp.concatenate(
        [jnp.sin(row_angle), jnp.cos(row_angle), jnp.sin(col_angle), jnp.cos(col_angle)], -1
    )


def signal_level(time_steps):
    phase = (time_steps.astype(jnp.float32) / 1000.0 + 0.008) / 1.008 * (math.pi / 2)
    return jnp.cos(phase) ** 2


def shard_shapes(tp_parts):
    head_width = D // tp_parts
    hidden_width = F // tp_parts
    return [
        (D, 3 * head_width),
        (head_width, D),
        (D, hidden_width),
        (hidden_width, D),
        (D, 6 * head_width),
    ]


def untile(tile_set, height, breadth):
    block = tile_set.shape[-1]
    return (
        tile_set.reshape(height // block, breadth // block, block, block)
        .transpose(0, 2, 1, 3)
        .reshape(height, breadth)
    )


def retile(matrix):
    height, breadth = matrix.shape
    return matrix.reshape(height // B, B, breadth // B, B).transpose(0, 2, 1, 3).reshape(-1, B, B)


def unpack_layers(tile_set, tp_parts):
    layer_list = []
    cursor = 0
    for layer_no in range(L):
        matrices = []
        for height, breadth in shard_shapes(tp_parts):
            amount = height * breadth // (B * B)
            matrices.append(untile(tile_set[cursor : cursor + amount], height, breadth))
            cursor += amount
        layer_list.append(matrices)
    return layer_list


def pack_layers(layer_list):
    return jnp.concatenate([retile(matrix) for matrices in layer_list for matrix in matrices], 0)


def else_shapes():
    return [(P_SIZE, D), (NCLS, D), (TFREQ, D), (D, D), (D, 2 * D), (D, P_SIZE)]


def split_else(flat_params):
    components = []
    cursor = 0
    for height, breadth in else_shapes():
        components.append(flat_params[cursor : cursor + height * breadth].reshape(height, breadth))
        cursor += height * breadth
    return components


def reflection(vectors):
    outer_prod = vectors[..., :, None] * vectors[..., None, :]
    return (
        jnp.eye(vectors.shape[-1], dtype=jnp.float32)
        - 2.0 * outer_prod / jnp.sum(vectors * vectors, -1)[..., None, None]
    )


def rotate(left_basis, middle, right_basis):
    return contract(
        "...ab,...bc->...ac", contract("...ab,...bc->...ac", left_basis, middle), right_basis
    )


def adam_finish(turned, master_state, first_state, second_state, left_basis, right_basis):
    first_new = 0.5 * first_state + 0.5 * turned
    second_new = 0.5 * second_state + 0.5 * turned * turned
    direction = first_new / (jnp.sqrt(second_new) + 1e-08)
    return (master_state - RATE * rotate(left_basis, direction, right_basis), first_new, second_new)


def adamw_flat(grad_clipped, master_state, first_state, second_state):
    first_new = 0.5 * first_state + 0.5 * grad_clipped
    second_new = 0.5 * second_state + 0.5 * grad_clipped * grad_clipped
    master_new = master_state - RATE * (
        first_new / (jnp.sqrt(second_new) + 1e-08) + DECAY * master_state
    )
    return (master_new, first_new, second_new)


def rows_in(value_low):
    return lax.all_gather(value_low, "tp", axis=0, tiled=True)


def rows_out(left_op, weight, contract_dim):
    return lax.psum_scatter(
        lax.dot_general(
            left_op, weight, (((1,), (contract_dim,)), ((), ())), preferred_element_type=jnp.float32
        ),
        "tp",
        scatter_dimension=0,
        tiled=True,
    )


def global_totals(loss_part, squares):
    return lax.psum((loss_part, squares), ("fsdp", "ctx", "tp"))


def attend(queries, key_rows, value_rows):
    scores = jnp.einsum(
        "iqhe,ikhe->ihqk", queries, key_rows, preferred_element_type=jnp.float32
    ) * HD ** (-0.5)
    highest_score = jnp.max(scores, -1, keepdims=True)
    exponent = jnp.exp(scores - highest_score)
    row_total = jnp.sum(exponent, -1, keepdims=True)
    probabilities = (exponent / row_total).astype(jnp.bfloat16)
    attended = jnp.einsum(
        "ihqk,ikhe->iqhe", probabilities, value_rows, preferred_element_type=jnp.float32
    )
    return (attended, highest_score + jnp.log(row_total))


def attend_back(queries, key_rows, value_rows, log_total, grad_attended):
    scores = jnp.einsum(
        "iqhe,ikhe->ihqk", queries, key_rows, preferred_element_type=jnp.float32
    ) * HD ** (-0.5)
    probabilities = jnp.exp(scores - log_total)
    grad_prob = jnp.einsum(
        "iqhe,ikhe->ihqk", grad_attended, value_rows, preferred_element_type=jnp.float32
    )
    grad_scores = (
        probabilities * (grad_prob - jnp.sum(probabilities * grad_prob, -1, keepdims=True))
    ).astype(jnp.bfloat16)
    grad_queries = jnp.einsum(
        "ihqk,ikhe->iqhe", grad_scores, key_rows, preferred_element_type=jnp.float32
    ) * HD ** (-0.5)
    grad_keys = jnp.einsum(
        "ihqk,iqhe->ikhe", grad_scores, queries, preferred_element_type=jnp.float32
    ) * HD ** (-0.5)
    grad_values = jnp.einsum(
        "ihqk,iqhe->ikhe",
        probabilities.astype(jnp.bfloat16),
        grad_attended,
        preferred_element_type=jnp.float32,
    )
    return (grad_queries, grad_keys, grad_values)


def layer_forward(stream, modes, matrices, images, local_len):
    w_qkv, w_proj, w_up, w_down = matrices[:4]
    shift_attn, scale_attn, gate_attn, shift_mlp, scale_mlp, gate_mlp = jnp.split(modes, 6, -1)
    normed_in = rows_in(modulate(stream, shift_attn, scale_attn).astype(jnp.bfloat16))
    projected = product(normed_in, w_qkv).astype(jnp.bfloat16)
    head_width = w_proj.shape[0]
    head_count = head_width // HD
    queries = projected[:, :head_width].reshape(images, local_len, head_count, HD)
    key_rows = projected[:, head_width : 2 * head_width].reshape(images, local_len, head_count, HD)
    value_rows = projected[:, 2 * head_width :].reshape(images, local_len, head_count, HD)
    attended, log_total = attend(queries, key_rows, value_rows)
    attended = attended.reshape(images * local_len, head_width).astype(jnp.bfloat16)
    branch = rows_out(attended, w_proj, 0)
    middle = stream + gate_attn * branch
    normed_mid = rows_in(modulate(middle, shift_mlp, scale_mlp).astype(jnp.bfloat16))
    hidden = product(normed_mid, w_up)
    activation = gelu_tanh(hidden).astype(jnp.bfloat16)
    mlp_out = rows_out(activation, w_down, 0)
    kept_state = (
        stream,
        normed_in,
        queries,
        key_rows,
        value_rows,
        log_total,
        attended,
        branch,
        middle,
        normed_mid,
        hidden,
        mlp_out,
    )
    return (middle + gate_mlp * mlp_out, kept_state)


def layer_backward(upstream, kept_state, modes, matrices, images, local_len):
    w_qkv, w_proj, w_up, w_down = matrices[:4]
    (
        stream,
        normed_in,
        queries,
        key_rows,
        value_rows,
        log_total,
        attended,
        branch,
        middle,
        normed_mid,
        hidden,
        mlp_out,
    ) = kept_state
    shift_attn, scale_attn, gate_attn, shift_mlp, scale_mlp, gate_mlp = jnp.split(modes, 6, -1)
    grad_mlp = rows_in((gate_mlp * upstream).astype(jnp.bfloat16))
    activation, gelu_back = jax.vjp(gelu_tanh, hidden)
    grad_down = over_rows(activation.astype(jnp.bfloat16), grad_mlp)
    grad_hidden = gelu_back(against(grad_mlp, w_down))[0].astype(jnp.bfloat16)
    grad_up = over_rows(normed_mid, grad_hidden)
    grad_normed_mid = rows_out(grad_hidden, w_up, 1)
    grad_middle, grad_shift_mlp, grad_scale_mlp = jax.vjp(modulate, middle, shift_mlp, scale_mlp)[
        1
    ](grad_normed_mid)
    grad_middle = grad_middle + upstream
    grad_branch = rows_in((gate_attn * grad_middle).astype(jnp.bfloat16))
    grad_proj = over_rows(attended, grad_branch)
    head_width = w_proj.shape[0]
    head_count = head_width // HD
    grad_attended = (
        against(grad_branch, w_proj).astype(jnp.bfloat16).reshape(images, local_len, head_count, HD)
    )
    grad_queries, grad_keys, grad_values = attend_back(
        queries, key_rows, value_rows, log_total, grad_attended
    )
    rows_here = images * local_len
    grad_qkv = jnp.concatenate(
        [
            grad_queries.reshape(rows_here, head_width),
            grad_keys.reshape(rows_here, head_width),
            grad_values.reshape(rows_here, head_width),
        ],
        1,
    ).astype(jnp.bfloat16)
    grad_w_qkv = over_rows(normed_in, grad_qkv)
    grad_normed_in = rows_out(grad_qkv, w_qkv, 1)
    grad_stream, grad_shift_attn, grad_scale_attn = jax.vjp(
        modulate, stream, shift_attn, scale_attn
    )[1](grad_normed_in)
    grad_modes = jnp.concatenate(
        [
            grad_shift_attn,
            grad_scale_attn,
            grad_middle * branch,
            grad_shift_mlp,
            grad_scale_mlp,
            upstream * mlp_out,
        ],
        -1,
    )
    return (grad_stream + grad_middle, [grad_w_qkv, grad_proj, grad_up, grad_down], grad_modes)


def on_device(
    latents,
    noise,
    timesteps,
    labels,
    owners,
    tiles_low,
    tiles_master,
    tiles_first,
    tiles_second,
    bases,
    else_low,
    else_master,
    else_first,
    else_second,
):
    tp_parts = lax.axis_size("tp")
    tp_index = lax.axis_index("tp")
    ctx_parts = lax.axis_size("ctx")
    fsdp_parts = lax.axis_size("fsdp")
    images = latents.shape[0]
    local_len = latents.shape[1]
    sp_rows = images * local_len // tp_parts
    first_row = tp_index * sp_rows
    element_count = images * fsdp_parts * ctx_parts * local_len * P_SIZE
    ordering = jnp.argsort(owners, stable=True)
    inverse = jnp.argsort(ordering)
    gathered = lax.all_gather(tiles_low, ("fsdp", "ctx"), axis=1, tiled=True)[0][inverse]
    layer_list = unpack_layers(gathered, tp_parts)
    patch_weight, class_table, time_first, time_second, final_weight, head_weight = split_else(
        lax.all_gather(else_low, ("fsdp", "ctx", "tp"), axis=0, tiled=True)
    )
    features_low = time_features(timesteps).astype(jnp.bfloat16)
    onehot = (labels[:, None] == jnp.arange(NCLS)[None, :]).astype(jnp.bfloat16)
    time_hidden = product(features_low, time_first)
    time_act = jax.nn.silu(time_hidden).astype(jnp.bfloat16)
    condition = product(time_act, time_second) + product(onehot, class_table)
    cond_act = jax.nn.silu(condition).astype(jnp.bfloat16)
    mod_shards = jnp.stack([product(cond_act, matrices[4]) for matrices in layer_list])
    mod_full = lax.all_gather(mod_shards, "tp", axis=2, tiled=True)
    final_modes = product(cond_act, final_weight)
    row_index = first_row + jnp.arange(sp_rows)
    selector = ((row_index // local_len)[:, None] == jnp.arange(images)[None, :]).astype(
        jnp.float32
    )
    mode_rows = contract("ri,lid->lrd", selector, mod_full)
    final_rows = matmul(selector, final_modes)
    signal = signal_level(timesteps)
    noisy_input = (
        jnp.sqrt(signal)[:, None, None] * latents + jnp.sqrt(1.0 - signal)[:, None, None] * noise
    )
    noisy_rows = lax.dynamic_slice_in_dim(
        noisy_input.reshape(images * local_len, P_SIZE), first_row, sp_rows, 0
    ).astype(jnp.bfloat16)
    target = lax.dynamic_slice_in_dim(
        noise.reshape(images * local_len, P_SIZE), first_row, sp_rows, 0
    )
    stream = product(noisy_rows, patch_weight) + position_table(row_index % local_len)
    kept_list = []
    for layer_no in range(L):
        stream, kept_state = layer_forward(
            stream, mode_rows[layer_no], layer_list[layer_no], images, local_len
        )
        kept_list.append(kept_state)
    shift_out, scale_out = jnp.split(final_rows, 2, -1)
    head_in, head_back = jax.vjp(modulate, stream, shift_out, scale_out)
    head_low = head_in.astype(jnp.bfloat16)
    mismatch = product(head_low, head_weight) - target
    loss_part = jnp.sum(mismatch * mismatch) / element_count
    grad_pred = (2.0 * mismatch / element_count).astype(jnp.bfloat16)
    grad_head = over_rows(head_low, grad_pred)
    upstream, grad_shift_out, grad_scale_out = head_back(against(grad_pred, head_weight))
    grad_final = matmul(selector.T, jnp.concatenate([grad_shift_out, grad_scale_out], -1))
    grad_layers = [None] * L
    grad_modes = [None] * L
    for layer_no in reversed(range(L)):
        upstream, grad_layers[layer_no], grad_modes[layer_no] = layer_backward(
            upstream,
            kept_list[layer_no],
            mode_rows[layer_no],
            layer_list[layer_no],
            images,
            local_len,
        )
    grad_patch = over_rows(noisy_rows, upstream.astype(jnp.bfloat16))
    mode_image = contract("ri,lrd->lid", selector, jnp.stack(grad_modes))
    mode_image = lax.psum_scatter(
        mode_image.astype(jnp.bfloat16), "tp", scatter_dimension=2, tiled=True
    ).astype(jnp.float32)
    cond_wide = cond_act.astype(jnp.float32)
    grad_cond_act = matmul(grad_final, final_weight.astype(jnp.float32).T)
    for layer_no in range(L):
        grad_layers[layer_no].append(contract("id,ie->de", cond_wide, mode_image[layer_no]))
        grad_cond_act = grad_cond_act + matmul(
            mode_image[layer_no], layer_list[layer_no][4].astype(jnp.float32).T
        )
    grad_condition = jax.vjp(jax.nn.silu, condition)[1](grad_cond_act)[0]
    grad_table = contract("ic,id->cd", onehot.astype(jnp.float32), grad_condition)
    grad_second = contract("ic,id->cd", time_act.astype(jnp.float32), grad_condition)
    grad_time_hidden = jax.vjp(jax.nn.silu, time_hidden)[1](
        matmul(grad_condition, time_second.astype(jnp.float32).T)
    )[0]
    grad_first = contract("ic,id->cd", features_low.astype(jnp.float32), grad_time_hidden)
    grad_final_weight = contract("ic,id->cd", cond_wide, grad_final)
    flat_grad = jnp.concatenate(
        [
            component.reshape(-1)
            for component in (
                grad_patch,
                grad_table,
                grad_first,
                grad_second,
                grad_final_weight,
                grad_head,
            )
        ]
    )
    tile_grads = pack_layers(grad_layers)[ordering]
    owned = lax.psum_scatter(tile_grads, ("fsdp", "ctx"), scatter_dimension=0, tiled=True)
    else_grad = lax.psum_scatter(flat_grad, ("fsdp", "ctx", "tp"), scatter_dimension=0, tiled=True)
    squares = jnp.sum(owned * owned) + jnp.sum(else_grad * else_grad)
    left_basis = reflection(bases[0, :, 0, :])
    right_basis = reflection(bases[0, :, 1, :])
    loss_total, square_total = global_totals(loss_part, squares)
    grad_norm = jnp.sqrt(square_total)
    clip_factor = jnp.minimum(1.0, 1.0 / grad_norm)
    turned = rotate(left_basis, clip_factor * owned, right_basis)
    master_new, first_new, second_new = adam_finish(
        turned, tiles_master[0], tiles_first[0], tiles_second[0], left_basis, right_basis
    )
    else_master_new, else_first_new, else_second_new = adamw_flat(
        clip_factor * else_grad, else_master, else_first, else_second
    )
    return (
        loss_total,
        grad_norm,
        master_new[None],
        first_new[None],
        second_new[None],
        master_new.astype(jnp.bfloat16)[None],
        else_master_new,
        else_first_new,
        else_second_new,
        else_master_new.astype(jnp.bfloat16),
    )


def solution(mesh):
    return jax.shard_map(
        on_device,
        mesh=mesh,
        in_specs=(
            P(("fsdp", "ctx"), None, None),
            P(("fsdp", "ctx"), None, None),
            P(("fsdp", "ctx")),
            P(("fsdp", "ctx")),
            P(),
            P("tp", ("fsdp", "ctx"), None, None),
            P("tp", ("fsdp", "ctx"), None, None),
            P("tp", ("fsdp", "ctx"), None, None),
            P("tp", ("fsdp", "ctx"), None, None),
            P("tp", ("fsdp", "ctx"), None, None),
            P(("fsdp", "ctx", "tp")),
            P(("fsdp", "ctx", "tp")),
            P(("fsdp", "ctx", "tp")),
            P(("fsdp", "ctx", "tp")),
        ),
        out_specs=(
            P(),
            P(),
            P("tp", ("fsdp", "ctx"), None, None),
            P("tp", ("fsdp", "ctx"), None, None),
            P("tp", ("fsdp", "ctx"), None, None),
            P("tp", ("fsdp", "ctx"), None, None),
            P(("fsdp", "ctx", "tp")),
            P(("fsdp", "ctx", "tp")),
            P(("fsdp", "ctx", "tp")),
            P(("fsdp", "ctx", "tp")),
        ),
        check_vma=False,
    )
```

profile of v0, /device:TPU:0, one launch (start us, length us, event | category | flops | bytes accessed | tf_op | source)
XLA Modules:
  0.0 2683.9 jit_solution(17024690424159067126)
XLA Ops:
  31.2 105.9 %all-gather.30.cloned.1.call-done = bf16[32,1,139520]{2,1,0:T(2,128)(2,1)} async-done(((bf16[1,1,139520]{2,1,0:T(2,128)(2,1)}), bf16[32,1,139520]{2,1,0:T(2,128)(2,1)}) %all-gather.30.cloned.1.call-update) | async-done | bytes 8929296 | tf_op jit(solution)/shard_map/all_gather | solution.py:359
  137.1 190.0 %reduce = bf16[32,139520]{1,0:T(8,128)(2,1)} reduce(bf16[32,1,139520]{2,1,0:T(2,128)(2,1)} %all-gather.30.cloned.1.call-done, bf16[]{:T(256)} %constant.168), dimensions={1}, to_apply=%all-gather.reduce_sub_computation | reduce | bytes 17858562 | tf_op jit(solution)/shard_map/all_gather | solution.py:359
  327.1 17.1 reshape.586
  361.2 167.4 %all-gather.12.cloned.1.call-done = bf16[1,1152,128,128]{3,2,0,1:T(8,128)(2,1)} async-done(((bf16[1,72,128,128]{3,2,0,1:T(8,128)(2,1)}), bf16[1,1152,128,128]{3,2,0,1:T(8,128)(2,1)}) %all-gather.12.cloned.1.call-update) | async-done | bytes 37748752 | tf_op jit(solution)/shard_map/all_gather | solution.py:356
  528.6 28.4 %gather_fusion = bf16[1152,128,128]{2,1,0:T(8,128)(2,1)} fusion(bf16[1152,128,128]{2,1,0:T(8,128)(2,1)} %bitcast.440, s32[2048]{0:T(1024)S(1)} %pad_clamp_fusion.1), kind=kCustom, calls=%fused_computation | custom fusion | bytes 75502080 | tf_op jit(solution)/shard_map/gather | solution.py:356
  569.4 9.1 copy.197
  583.1 13.5 convolution_bitcast_fusion
  596.6 14.2 slice_bitcast_fusion
  663.4 10.4 reduce-scatter.13.cloned.1.call-done
  682.5 11.5 fusion.256
  722.8 13.5 reduce-scatter.15.cloned.1.call-done
  789.1 13.3 reduce-scatter.17.cloned.1.call-done
  874.0 12.0 all-gather.22.cloned.1.call-done
  885.9 12.9 fusion.17
  907.3 13.3 reduce-scatter.21.cloned.1.call-done
  929.9 11.9 all-gather.24.cloned.1.call-done
  975.1 13.1 reduce-scatter.23.cloned.1.call-done
  1000.9 12.0 all-gather.26.cloned.1.call-done
  1012.9 12.7 fusion.10
  1034.1 13.3 reduce-scatter.25.cloned.1.call-done
  1056.5 11.9 all-gather.28.cloned.1.call-done
  1162.4 11.0 fusion.23
  1243.2 10.1 copy.257
  1353.0 11.6 constant_dynamic-update-slice_fusion.15
  1389.5 11.7 constant_dynamic-update-slice_fusion.10
  1401.1 54.0 %gather_fusion.1 = f32[1152,128,128]{2,1,0:T(8,128)} fusion(f32[1152,128,128]{2,1,0:T(8,128)} %constant_dynamic-update-slice_fusion.10, s32[2048]{0:T(1024)S(1)} %copy-done.112), kind=kCustom, calls=%fused_computation.1 | custom fusion | bytes 150999552 | tf_op jit(solution)/shard_map/gather | solution.py:446
  1456.8 76.9 %all-reduce.4.cloned.1.call-done = f32[4464640]{0:T(1024)} async-done(((f32[4464640]{0:T(1024)}), f32[4464640]{0:T(1024)}) %all-reduce.4.cloned.1.call-update) | async-done | bytes 17858576
  1535.7 1043.4 %reduce-scatter.29.cloned.1.call-done = f32[72,128,128]{2,1,0:T(8,128)} async-done(((f32[1152,128,128]{2,1,0:T(8,128)}), f32[72,128,128]{2,1,0:T(8,128)}) %reduce-scatter.29.cloned.1.call-update) | async-done | bytes 4718608 | tf_op jit(solution)/shard_map/reduce_scatter | solution.py:447
  2584.7 39.4 %all-reduce.1 = (f32[]{:T(128)}, f32[]{:T(128)}) all-reduce(f32[]{:T(128)S(6)} %div.232, f32[]{:T(128)S(6)} %add.340), channel_id=1, replica_groups=mesh['fsdp'=8,'ctx'=2,'tp'=2] {'fsdp','ctx','tp'}, use_global_device_ids=true, to_apply=%region_21.22 | all-reduce | flops 2 | bytes 16 | tf_op jit(solution)/shard_map/psum | solution.py:186
  2641.0 11.0 fusion.41
  2651.9 9.7 fusion.160
  2661.6 8.4 bitcast_subtract_fusion
  (632 shorter events, 668.8 us)
Async XLA Ops:
  7.2 130.0 %all-gather.30.cloned.1.call-start = ((), (), s32[]{:S(2)}) async-start(), calls=%async_computation.28 | async-start | bytes 18416640 | tf_op jit(solution)/shard_map/all_gather | solution.py:359
  11.5 517.1 %all-gather.12.cloned.1.call-start = ((), (), s32[]{:S(2)}) async-start(), calls=%async_computation.10 | async-start | bytes 40108032 | tf_op jit(solution)/shard_map/all_gather | solution.py:356
  12.2 619.0 %all-gather.14.cloned.1.call-start = ((), (), s32[]{:S(2)}) async-start(), calls=%async_computation.11 | async-start | bytes 3145728 | tf_op jit(solution)/shard_map/all_gather | solution.py:171
  14.6 342.1 %copy-start.92 = (bf16[4,2,8,256]{3,2,0,1:T(8,128)(2,1)}, bf16[4,2,8,256]{3,2,0,1:T(8,128)(2,1)S(1)}, u32[]{:S(2)}) copy-start(bf16[4,2,8,256]{3,2,0,1:T(8,128)(2,1)S(1)} %copy.299) | copy-start | bytes 98308
  20.4 306.7 %copy-start.113 = (s32[1152]{0:T(1024)}, s32[1152]{0:T(1024)S(1)}, u32[]{:S(2)}) copy-start(s32[1152]{0:T(1024)S(1)} %get-tuple-element.12) | copy-start | bytes 13828
  25.5 557.6 %copy-start.100 = (s32[512]{0:T(512)}, s32[512]{0:T(512)S(1)}, u32[]{:S(2)}) copy-start(s32[512]{0:T(512)S(1)} %add_select_fusion) | copy-start | bytes 6148
  25.6 333.7 %copy-start.129 = (bf16[4,128]{1,0:T(4,128)(2,1)}, bf16[4,128]{1,0:T(4,128)(2,1)S(1)}, u32[]{:S(2)}) copy-start(bf16[4,128]{1,0:T(4,128)(2,1)S(1)} %get-tuple-element.84) | copy-start | bytes 3076
  25.7 333.7 %copy-start.131 = (bf16[4,128]{1,0:T(4,128)(2,1)}, bf16[4,128]{1,0:T(4,128)(2,1)S(1)}, u32[]{:S(2)}) copy-start(bf16[4,128]{1,0:T(4,128)(2,1)S(1)} %get-tuple-element.85) | copy-start | bytes 3076
  359.0 251.9 %copy-start.11 = (f32[512,1024]{1,0:T(8,128)}, f32[512,1024]{1,0:T(8,128)S(1)}, u32[]{:S(2)}) copy-start(f32[512,1024]{1,0:T(8,128)S(1)} %get-tuple-element.89) | copy-start | bytes 6291460
  359.0 251.8 %copy-start.103 = (f32[512]{0:T(512)}, f32[512]{0:T(512)S(1)}, u32[]{:S(2)}) copy-start(f32[512]{0:T(512)S(1)} %broadcast_multiply_fusion.4) | copy-start | bytes 6148
  359.4 197.6 %copy-start.121 = (f32[512]{0:T(512)}, f32[512]{0:T(512)S(1)}, u32[]{:S(2)}) copy-start(f32[512]{0:T(512)S(1)} %multiply_reduce_fusion.14) | copy-start | bytes 6148
  359.4 251.5 %copy-start.117 = (f32[512]{0:T(512)}, f32[512]{0:T(512)S(1)}, u32[]{:S(2)}) copy-start(f32[512]{0:T(512)S(1)} %fusion.214) | copy-start | bytes 6148
  361.2 218.3 %copy-start.67 = (f32[4,1024]{1,0:T(4,128)}, f32[4,1024]{1,0:T(4,128)S(1)}, u32[]{:S(2)}) copy-start(f32[4,1024]{1,0:T(4,128)S(1)} %convolution_add_fusion.1) | copy-start | bytes 49156
  616.9 56.8 %reduce-scatter.13.cloned.1.call-start = ((), (), s32[]{:S(2)}) async-start(), calls=%async_computation.12 | async-start | bytes 6291456 | tf_op jit(solution)/shard_map/reduce_scatter | solution.py:175
  663.3 41.2 %all-gather.16.cloned.1.call-start = ((), (), s32[]{:S(2)}) async-start(), calls=%async_computation.13 | async-start | bytes 3145728 | tf_op jit(solution)/shard_map/all_gather | solution.py:171
  682.5 53.8 %reduce-scatter.15.cloned.1.call-start = ((), (), s32[]{:S(2)}) async-start(), calls=%async_computation.14 | async-start | bytes 6291456 | tf_op jit(solution)/shard_map/reduce_scatter | solution.py:175
  722.7 33.8 %all-gather.18.cloned.1.call-start = ((), (), s32[]{:S(2)}) async-start(), calls=%async_computation.15 | async-start | bytes 3145728 | tf_op jit(solution)/shard_map/all_gather | solution.py:171
  744.5 57.9 %reduce-scatter.17.cloned.1.call-start = ((), (), s32[]{:S(2)}) async-start(), calls=%async_computation.16 | async-start | bytes 6291456 | tf_op jit(solution)/shard_map/reduce_scatter | solution.py:175
  789.0 34.2 %all-gather.20.cloned.1.call-start = ((), (), s32[]{:S(2)}) async-start(), calls=%async_computation.17 | async-start | bytes 3145728 | tf_op jit(solution)/shard_map/all_gather | solution.py:171
  810.1 51.7 %reduce-scatter.19.cloned.1.call-start = ((), (), s32[]{:S(2)}) async-start(), calls=%async_computation.18 | async-start | bytes 6291456 | tf_op jit(solution)/shard_map/reduce_scatter | solution.py:175
  841.8 44.2 %all-gather.22.cloned.1.call-start = ((), (), s32[]{:S(2)}) async-start(), calls=%async_computation.19 | async-start | bytes 3145728 | tf_op jit(solution)/shard_map/all_gather | solution.py:171
  873.9 46.7 %reduce-scatter.21.cloned.1.call-start = ((), (), s32[]{:S(2)}) async-start(), calls=%async_computation.20 | async-start | bytes 6291456 | tf_op jit(solution)/shard_map/reduce_scatter | solution.py:175
  907.2 34.6 %all-gather.24.cloned.1.call-start = ((), (), s32[]{:S(2)}) async-start(), calls=%async_computation.21 | async-start | bytes 3145728 | tf_op jit(solution)/shard_map/all_gather | solution.py:171
  929.9 58.4 %reduce-scatter.23.cloned.1.call-start = ((), (), s32[]{:S(2)}) async-start(), calls=%async_computation.22 | async-start | bytes 6291456 | tf_op jit(solution)/shard_map/reduce_scatter | solution.py:175
  974.9 38.0 %all-gather.26.cloned.1.call-start = ((), (), s32[]{:S(2)}) async-start(), calls=%async_computation.23 | async-start | bytes 3145728 | tf_op jit(solution)/shard_map/all_gather | solution.py:171
  1000.9 46.5 %reduce-scatter.25.cloned.1.call-start = ((), (), s32[]{:S(2)}) async-start(), calls=%async_computation.24 | async-start | bytes 6291456 | tf_op jit(solution)/shard_map/reduce_scatter | solution.py:175
  1034.0 34.4 %all-gather.28.cloned.1.call-start = ((), (), s32[]{:S(2)}) async-start(), calls=%async_computation.25 | async-start | bytes 3145728 | tf_op jit(solution)/shard_map/all_gather | solution.py:171
  1056.4 93.6 %reduce-scatter.27.cloned.1.call-start = ((), (), s32[]{:S(2)}) async-start(), calls=%async_computation.26 | async-start | bytes 6291456 | tf_op jit(solution)/shard_map/reduce_scatter | solution.py:175
  1101.7 93.7 %reduce-scatter.31.cloned.1.call-start = ((), (), s32[]{:S(2)}) async-start(), calls=%async_computation.29 | async-start | bytes 2359296
  1185.1 348.7 %all-reduce.4.cloned.1.call-start = ((), (), s32[]{:S(2)}) async-start(), calls=%async_computation.30 | async-start | bytes 35717120
  1238.7 1340.4 %reduce-scatter.29.cloned.1.call-start = ((), (), s32[]{:S(2)}) async-start(), calls=%async_computation.27 | async-start | bytes 80216064 | tf_op jit(solution)/shard_map/reduce_scatter | solution.py:447
  1533.8 1107.2 %slice-start.16 = ((s8[4718592]{0:T(1024)(128)(4,1)}), s8[524288]{0:T(1024)(128)(4,1)S(1)}, s32[]{:S(2)}) async-start(s8[4718592]{0:T(1024)(128)(4,1)} %bitcast.478), calls=%async_computation.47 | async-start | bytes 1048576
  (151 other events, 1020.1 us)
Sparse Core Ops, SparseCore 0:
  11.6 125.4 all-gather.29
  139.9 388.6 all-gather.11
  617.0 8.7 all-gather.13
  663.4 10.2 reduce-scatter.12
  682.6 11.8 all-gather.15
  722.9 13.3 reduce-scatter.14
  744.7 11.8 all-gather.17
  789.2 13.2 reduce-scatter.16
  810.2 11.8 all-gather.19
  841.9 13.3 reduce-scatter.18
  874.0 11.8 all-gather.21
  907.3 13.2 reduce-scatter.20
  930.0 11.8 all-gather.23
  975.0 13.1 reduce-scatter.22
  1001.0 11.8 all-gather.25
  1034.1 13.2 reduce-scatter.24
  1056.5 11.8 all-gather.27
  1101.9 13.1 reduce-scatter.26
  1185.2 10.2 reduce-scatter.30
  1238.9 294.8 all-reduce.3
  1539.8 1039.3 reduce-scatter.28
where the time goes:
time: 2690 us; the launch traced here: 2680 us
  waiting for transfers between devices  1530 us (57%)
  local copies, waits for them, and re-layouts  486 us (18%)
  other arithmetic  312 us (12%)
  matrix products  289 us (11%)
  blocking collectives  41.4 us (2%)
    reduce_scatter x1, waiting for transfers between devices, on_device(): lax.psum_scatter(tile_grads, ('fsdp', 'ctx'), scatter_dimension=0, tiled=...  1040 us
    all_gather x1, other arithmetic, on_device(): lax.all_gather(else_low, ('fsdp', 'ctx', 'tp'), axis=0, tiled=True)  190 us
    unnamed x366, local copies, waits for them, and re-layouts  176 us
    all_gather x1, waiting for transfers between devices, on_device(): lax.all_gather(tiles_low, ('fsdp', 'ctx'), axis=1, tiled=True)[0][inverse]  167 us
    all_gather x1, waiting for transfers between devices, on_device(): lax.all_gather(else_low, ('fsdp', 'ctx', 'tp'), axis=0, tiled=True)  106 us
    unnamed x23, waiting for transfers between devices  85.7 us
    dot_general x12, matrix products, contract(): return jnp.einsum(formula, left_op, right_op, precision=HIGHEST)  78.4 us
    reduce_scatter x8, waiting for transfers between devices, rows_out(): lax.psum_scatter(lax.dot_general(left_op, weight, (((1,), (contract_dim,)...  76.9 us
  transfers between devices with their start and end apart: 21, of which 16 were waited for; matrix products, arithmetic and copies ran while one was open for 22% of the time, Pallas kernels for 0%

commit v1 on v0

--- a/solution.py
+++ b/solution.py
@@ -3,6 +3,8 @@
 import jax
 import jax.numpy as jnp
 from jax import lax
+from jax.experimental import pallas as pl
+from jax.experimental.pallas import tpu as pltpu
 from jax.sharding import PartitionSpec as P
 
 D = 1024
@@ -167,23 +169,225 @@
     return (master_new, first_new, second_new)
 
 
+def is_box():
+    return (lax.axis_size("fsdp"), lax.axis_size("ctx"), lax.axis_size("tp")) == (8, 2, 2)
+
+
+def swap_tp(value):
+    return lax.ppermute(value, "tp", [(0, 1), (1, 0)])
+
+
+def swap_y(value):
+    return lax.ppermute(value, "ctx", [(0, 1), (1, 0)])
+
+
+def swap_f(value, bit):
+    return lax.ppermute(value, "fsdp", [(place, place ^ bit) for place in range(8)])
+
+
+def swap_x(value):
+    return swap_f(value, 1)
+
+
+def move_z(value, step, sources):
+    return lax.ppermute(
+        value,
+        "fsdp",
+        [(2 * from_z + x, 2 * (from_z + step) + x) for from_z in sources for x in range(2)],
+    )
+
+
+def place_z():
+    return lax.axis_index("fsdp") // 2
+
+
+def low(value):
+    return value.astype(jnp.bfloat16)
+
+
+def wide(value):
+    return value.astype(jnp.float32)
+
+
+def along_z(own):
+    z = place_z()
+    above, below = [own], [own]
+    for hop in range(1, 4):
+        above.append(move_z(above[-1], 1, range(hop - 1, 3)))
+        below.append(move_z(below[-1], -1, range(1, 5 - hop)))
+    return [
+        own,
+        jnp.where(z % 2 == 1, above[1], below[1]),
+        jnp.where(z >= 2, above[2], below[2]),
+        jnp.where(
+            z == 0, below[3], jnp.where(z == 3, above[3], jnp.where(z == 1, below[1], above[1]))
+        ),
+    ]
+
+
+def sum_z(blocks):
+    z = place_z()
+    up = move_z(low(blocks[3]), 1, range(0, 1))
+    down = move_z(low(blocks[3]), -1, range(3, 4))
+    up = move_z(low(blocks[2] + up), 1, range(0, 2))
+    down = move_z(low(blocks[2] + down), -1, range(2, 4))
+    up = move_z(low(jnp.where(z == 1, blocks[3], blocks[1]) + up), 1, range(0, 3))
+    down = move_z(low(jnp.where(z == 2, blocks[3], blocks[1]) + down), -1, range(1, 4))
+    return blocks[0] + up + down
+
+
+def slot_ranges(slots):
+    side = slots * 5 // 18
+    return slots - 2 * side, side
+
+
+def gather_tiles(own):
+    main, side = slot_ranges(own.shape[0])
+    half = main // 2
+    first, second, third = own[:main], own[main : main + side], own[main + side :]
+    second = jnp.concatenate([second, swap_x(second)], 0)
+    third = jnp.concatenate([third, swap_y(third)], 0)
+    pieces = []
+    for block in along_z(first):
+        by_x, by_y = swap_x(block), swap_y(block)
+        pieces += [block, by_y, by_x, swap_y(by_x[:half]), swap_x(by_y[half:])]
+    for block in along_z(second):
+        pieces += [block, swap_y(block)]
+    for block in along_z(third):
+        pieces += [block, swap_x(block)]
+    return jnp.concatenate(pieces, 0)
+
+
+def place_of_slot(owner, slot, slots):
+    main, side = slot_ranges(slots)
+    rel_f = jnp.bitwise_xor(owner // 2, lax.axis_index("fsdp"))
+    rel_y = jnp.bitwise_xor(owner % 2, lax.axis_index("ctx"))
+    rel_z, rel_x = rel_f // 2, rel_f % 2
+    one = ((rel_z * 2 + rel_x) * 2 + rel_y) * main + slot
+    two = 16 * main + ((rel_z * 2 + rel_y) * 2 + rel_x) * side + slot - main
+    three = 16 * (main + side) + ((rel_z * 2 + rel_x) * 2 + rel_y) * side + slot - main - side
+    return jnp.where(slot < main, one, jnp.where(slot < main + side, two, three))
+
+
+def scatter_tiles(parts, slots):
+    main, side = slot_ranges(slots)
+    half = main // 2
+    first = parts[: 16 * main].reshape(4, 2, 2, main, B, B)
+    second = parts[16 * main : 16 * (main + side)].reshape(4, 2, 2, side, B, B)
+    third = parts[16 * (main + side) :].reshape(4, 2, 2, side, B, B)
+    blocks = [None] * 4
+    two = [None] * 4
+    three = [None] * 4
+    for rel in (3, 2, 1, 0):
+        two[rel] = wide(second[rel, 0]) + swap_y(second[rel, 1])
+        three[rel] = wide(third[rel, 0]) + swap_x(third[rel, 1])
+    for rel in (3, 2, 1, 0):
+        by_y = swap_y(first[rel, 1, 1, :half])
+        by_x = swap_x(first[rel, 1, 1, half:])
+        from_x = jnp.concatenate(
+            [
+                swap_x(low(wide(first[rel, 1, 0, :half]) + by_y)),
+                swap_x(first[rel, 1, 0, half:]),
+            ],
+            0,
+        )
+        from_y = jnp.concatenate(
+            [
+                swap_y(first[rel, 0, 1, :half]),
+                swap_y(low(wide(first[rel, 0, 1, half:]) + by_x)),
+            ],
+            0,
+        )
+        blocks[rel] = wide(first[rel, 0, 0]) + from_x + from_y
+    two = sum_z(two)
+    three = sum_z(three)
+    two = two[0] + swap_x(low(two[1]))
+    three = three[0] + swap_y(low(three[1]))
+    return jnp.concatenate([sum_z(blocks), two, three], 0)
+
+
+def gather_images(value):
+    if not is_box():
+        return lax.all_gather(value, ("fsdp", "ctx"), axis=0, tiled=True)
+    value = jnp.concatenate(along_z(value), 0)
+    by_x, by_y = swap_x(value), swap_y(value)
+    return jnp.concatenate([value, by_x, by_y, swap_x(by_y)], 0)
+
+
+def gather_else(flat):
+    if not is_box():
+        return lax.all_gather(flat, ("fsdp", "ctx", "tp"), axis=0, tiled=True)
+    z, x = place_z(), lax.axis_index("fsdp") % 2
+    y, core = lax.axis_index("ctx"), lax.axis_index("tp")
+    own = flat.reshape(1, -1, 128)
+    line = along_z(own)
+    line = [
+        jnp.where(
+            z == place,
+            line[0],
+            jnp.where(z == place ^ 1, line[1], jnp.where(z == place ^ 2, line[2], line[3])),
+        )
+        for place in range(4)
+    ]
+    line = jnp.concatenate(line, 0)
+    by_x, by_y = swap_x(line), swap_y(line)
+    half = line.shape[1] // 2
+    both = jnp.concatenate([swap_y(by_x[:, :half]), swap_x(by_y[:, half:])], 1)
+    y_low = [jnp.where(y == 0, line, by_y), jnp.where(y == 0, by_x, both)]
+    y_high = [jnp.where(y == 0, by_y, line), jnp.where(y == 0, both, by_x)]
+    chip = jnp.stack(
+        [
+            jnp.stack([jnp.where(x == 0, y_low[0], y_low[1]), jnp.where(x == 0, y_high[0], y_high[1])], 1),
+            jnp.stack([jnp.where(x == 0, y_low[1], y_low[0]), jnp.where(x == 0, y_high[1], y_high[0])], 1),
+        ],
+        1,
+    )
+    other = swap_tp(chip)
+    return jnp.stack(
+        [jnp.where(core == 0, chip, other), jnp.where(core == 0, other, chip)], 3
+    ).reshape(-1)
+
+
+def total(value):
+    if not is_box():
+        return lax.psum(value, ("fsdp", "ctx", "tp"))
+    value = value + swap_tp(value)
+    value = value + swap_y(value)
+    for bit in (1, 2, 4):
+        value = value + swap_f(value, bit)
+    return value
+
+
+def tp_sum(value):
+    if lax.axis_size("tp") == 2:
+        return value + swap_tp(value)
+    return lax.psum(value, "tp")
+
+
+def columns_in(value):
+    if lax.axis_size("tp") == 2:
+        other = swap_tp(value)
+        at_zero = lax.axis_index("tp") == 0
+        return jnp.concatenate(
+            [jnp.where(at_zero, value, other), jnp.where(at_zero, other, value)], -1
+        )
+    return lax.all_gather(value, "tp", axis=value.ndim - 1, tiled=True)
+
+
 def rows_in(value_low):
+    if lax.axis_size("tp") == 2:
+        return jnp.concatenate([value_low, swap_tp(value_low)], 0)
     return lax.all_gather(value_low, "tp", axis=0, tiled=True)
 
 
 def rows_out(left_op, weight, contract_dim):
-    return lax.psum_scatter(
-        lax.dot_general(
-            left_op, weight, (((1,), (contract_dim,)), ((), ())), preferred_element_type=jnp.float32
-        ),
-        "tp",
-        scatter_dimension=0,
-        tiled=True,
-    )
-
-
-def global_totals(loss_part, squares):
-    return lax.psum((loss_part, squares), ("fsdp", "ctx", "tp"))
+    partial = lax.dot_general(
+        left_op, weight, (((1,), (contract_dim,)), ((), ())), preferred_element_type=jnp.float32
+    )
+    if lax.axis_size("tp") == 2:
+        half = partial.shape[0] // 2
+        return partial[:half] + swap_tp(partial[half:])
+    return lax.psum_scatter(partial, "tp", scatter_dimension=0, tiled=True)
 
 
 def attend(queries, key_rows, value_rows):
@@ -228,22 +432,26 @@
 
 def layer_forward(stream, modes, matrices, images, local_len):
     w_qkv, w_proj, w_up, w_down = matrices[:4]
-    shift_attn, scale_attn, gate_attn, shift_mlp, scale_mlp, gate_mlp = jnp.split(modes, 6, -1)
-    normed_in = rows_in(modulate(stream, shift_attn, scale_attn).astype(jnp.bfloat16))
-    projected = product(normed_in, w_qkv).astype(jnp.bfloat16)
+    own, group = stream.shape[:2]
+    rows = own * group
+    shift_attn, scale_attn, gate_attn, shift_mlp, scale_mlp, gate_mlp = jnp.split(
+        modes[:, None, :], 6, -1
+    )
+    normed_in = rows_in(low(modulate(stream, shift_attn, scale_attn)).reshape(rows, D))
+    projected = low(product(normed_in, w_qkv))
     head_width = w_proj.shape[0]
     head_count = head_width // HD
     queries = projected[:, :head_width].reshape(images, local_len, head_count, HD)
     key_rows = projected[:, head_width : 2 * head_width].reshape(images, local_len, head_count, HD)
     value_rows = projected[:, 2 * head_width :].reshape(images, local_len, head_count, HD)
     attended, log_total = attend(queries, key_rows, value_rows)
-    attended = attended.reshape(images * local_len, head_width).astype(jnp.bfloat16)
-    branch = rows_out(attended, w_proj, 0)
+    attended = low(attended.reshape(images * local_len, head_width))
+    branch = rows_out(attended, w_proj, 0).reshape(own, group, D)
     middle = stream + gate_attn * branch
-    normed_mid = rows_in(modulate(middle, shift_mlp, scale_mlp).astype(jnp.bfloat16))
+    normed_mid = rows_in(low(modulate(middle, shift_mlp, scale_mlp)).reshape(rows, D))
     hidden = product(normed_mid, w_up)
-    activation = gelu_tanh(hidden).astype(jnp.bfloat16)
-    mlp_out = rows_out(activation, w_down, 0)
+    activation = low(gelu_tanh(hidden))
+    mlp_out = rows_out(activation, w_down, 0).reshape(own, group, D)
     kept_state = (
         stream,
         normed_in,
@@ -277,38 +485,42 @@
         hidden,
         mlp_out,
     ) = kept_state
-    shift_attn, scale_attn, gate_attn, shift_mlp, scale_mlp, gate_mlp = jnp.split(modes, 6, -1)
-    grad_mlp = rows_in((gate_mlp * upstream).astype(jnp.bfloat16))
+    own, group = stream.shape[:2]
+    rows = own * group
+    shift_attn, scale_attn, gate_attn, shift_mlp, scale_mlp, gate_mlp = jnp.split(
+        modes[:, None, :], 6, -1
+    )
+    grad_mlp = rows_in(low(gate_mlp * upstream).reshape(rows, D))
     activation, gelu_back = jax.vjp(gelu_tanh, hidden)
-    grad_down = over_rows(activation.astype(jnp.bfloat16), grad_mlp)
-    grad_hidden = gelu_back(against(grad_mlp, w_down))[0].astype(jnp.bfloat16)
-    grad_up = over_rows(normed_mid, grad_hidden)
-    grad_normed_mid = rows_out(grad_hidden, w_up, 1)
+    grad_down = low(over_rows(low(activation), grad_mlp))
+    grad_hidden = low(gelu_back(against(grad_mlp, w_down))[0])
+    grad_up = low(over_rows(normed_mid, grad_hidden))
+    grad_normed_mid = rows_out(grad_hidden, w_up, 1).reshape(own, group, D)
     grad_middle, grad_shift_mlp, grad_scale_mlp = jax.vjp(modulate, middle, shift_mlp, scale_mlp)[
         1
     ](grad_normed_mid)
     grad_middle = grad_middle + upstream
-    grad_branch = rows_in((gate_attn * grad_middle).astype(jnp.bfloat16))
-    grad_proj = over_rows(attended, grad_branch)
+    grad_branch = rows_in(low(gate_attn * grad_middle).reshape(rows, D))
+    grad_proj = low(over_rows(attended, grad_branch))
     head_width = w_proj.shape[0]
     head_count = head_width // HD
-    grad_attended = (
-        against(grad_branch, w_proj).astype(jnp.bfloat16).reshape(images, local_len, head_count, HD)
-    )
+    grad_attended = low(against(grad_branch, w_proj)).reshape(images, local_len, head_count, HD)
     grad_queries, grad_keys, grad_values = attend_back(
         queries, key_rows, value_rows, log_total, grad_attended
     )
     rows_here = images * local_len
-    grad_qkv = jnp.concatenate(
-        [
-            grad_queries.reshape(rows_here, head_width),
-            grad_keys.reshape(rows_here, head_width),
-            grad_values.reshape(rows_here, head_width),
-        ],
-        1,
-    ).astype(jnp.bfloat16)
-    grad_w_qkv = over_rows(normed_in, grad_qkv)
-    grad_normed_in = rows_out(grad_qkv, w_qkv, 1)
+    grad_qkv = low(
+        jnp.concatenate(
+            [
+                grad_queries.reshape(rows_here, head_width),
+                grad_keys.reshape(rows_here, head_width),
+                grad_values.reshape(rows_here, head_width),
+            ],
+            1,
+        )
+    )
+    grad_w_qkv = low(over_rows(normed_in, grad_qkv))
+    grad_normed_in = rows_out(grad_qkv, w_qkv, 1).reshape(own, group, D)
     grad_stream, grad_shift_attn, grad_scale_attn = jax.vjp(
         modulate, stream, shift_attn, scale_attn
     )[1](grad_normed_in)
@@ -316,14 +528,60 @@
         [
             grad_shift_attn,
             grad_scale_attn,
-            grad_middle * branch,
+            jnp.sum(grad_middle * branch, 1, keepdims=True),
             grad_shift_mlp,
             grad_scale_mlp,
-            upstream * mlp_out,
+            jnp.sum(upstream * mlp_out, 1, keepdims=True),
         ],
         -1,
-    )
+    )[:, 0]
     return (grad_stream + grad_middle, [grad_w_qkv, grad_proj, grad_up, grad_down], grad_modes)
+
+
+def update_kernel(clip, grad, master, first, second, bases, master_out, first_out, second_out, low_out):
+    eye = lax.broadcasted_iota(jnp.int32, (B, B), 0) == lax.broadcasted_iota(jnp.int32, (B, B), 1)
+    for tile in range(grad.shape[0]):
+        left_row = bases[tile, 0:1, :]
+        right_row = bases[tile, 1:2, :]
+        left_col = jnp.sum(jnp.where(eye, left_row, 0.0), 1, keepdims=True)
+        left_rate = 2.0 / jnp.sum(left_row * left_row, 1, keepdims=True)
+        right_rate = 2.0 / jnp.sum(right_row * right_row, 1, keepdims=True)
+        left_scaled = left_col * left_rate
+        right_scaled = right_row * right_rate
+
+        def turn(middle):
+            middle = middle - left_scaled * jnp.sum(left_col * middle, 0, keepdims=True)
+            return middle - jnp.sum(middle * right_row, 1, keepdims=True) * right_scaled
+
+        turned = turn(clip[0, 0] * grad[tile])
+        first_new = 0.5 * first[tile] + 0.5 * turned
+        second_new = 0.5 * second[tile] + 0.5 * turned * turned
+        direction = first_new / (jnp.sqrt(second_new) + 1e-08)
+        master_new = master[tile] - RATE * turn(direction)
+        master_out[tile] = master_new
+        first_out[tile] = first_new
+        second_out[tile] = second_new
+        low_out[tile] = master_new.astype(jnp.bfloat16)
+
+
+def update_tiles(clip_factor, grad, master, first, second, bases):
+    slots = grad.shape[0]
+    amount = 3
+    tile_spec = pl.BlockSpec((amount, B, B), lambda step: (step, 0, 0))
+    whole = jax.ShapeDtypeStruct(grad.shape, jnp.float32)
+    return pl.pallas_call(
+        update_kernel,
+        grid=(slots // amount,),
+        in_specs=[pl.BlockSpec(memory_space=pltpu.SMEM)]
+        + [tile_spec] * 4
+        + [pl.BlockSpec((amount, 2, B), lambda step: (step, 0, 0))],
+        out_specs=[tile_spec] * 4,
+        out_shape=[whole, whole, whole, jax.ShapeDtypeStruct(grad.shape, jnp.bfloat16)],
+        compiler_params=pltpu.CompilerParams(vmem_limit_bytes=32 * 1024 * 1024),
+        cost_estimate=pl.CostEstimate(
+            flops=slots * B * B * 30, bytes_accessed=slots * B * B * 30, transcendentals=slots * B * B
+        ),
+    )(clip_factor.reshape(1, 1), grad, master, first, second, bases)
 
 
 def on_device(
@@ -342,63 +600,76 @@
     else_first,
     else_second,
 ):
+    box = is_box()
     tp_parts = lax.axis_size("tp")
     tp_index = lax.axis_index("tp")
     ctx_parts = lax.axis_size("ctx")
     fsdp_parts = lax.axis_size("fsdp")
     images = latents.shape[0]
     local_len = latents.shape[1]
+    slots = tiles_low.shape[1]
     sp_rows = images * local_len // tp_parts
     first_row = tp_index * sp_rows
+    own = max(1, sp_rows // local_len)
+    group = sp_rows // own
+    first_image = first_row // local_len
     element_count = images * fsdp_parts * ctx_parts * local_len * P_SIZE
     ordering = jnp.argsort(owners, stable=True)
     inverse = jnp.argsort(ordering)
-    gathered = lax.all_gather(tiles_low, ("fsdp", "ctx"), axis=1, tiled=True)[0][inverse]
+    patch_weight, class_table, time_first, time_second, final_weight, head_weight = split_else(
+        gather_else(else_low)
+    )
+    if box:
+        places = place_of_slot(inverse // slots, inverse % slots, slots)
+        tile_at = jnp.argsort(places)
+        gathered = gather_tiles(tiles_low[0])[places]
+    else:
+        gathered = lax.all_gather(tiles_low, ("fsdp", "ctx"), axis=1, tiled=True)[0][inverse]
     layer_list = unpack_layers(gathered, tp_parts)
-    patch_weight, class_table, time_first, time_second, final_weight, head_weight = split_else(
-        lax.all_gather(else_low, ("fsdp", "ctx", "tp"), axis=0, tiled=True)
-    )
-    features_low = time_features(timesteps).astype(jnp.bfloat16)
-    onehot = (labels[:, None] == jnp.arange(NCLS)[None, :]).astype(jnp.bfloat16)
+    features_low = low(time_features(timesteps))
+    onehot = low(labels[:, None] == jnp.arange(NCLS)[None, :])
     time_hidden = product(features_low, time_first)
-    time_act = jax.nn.silu(time_hidden).astype(jnp.bfloat16)
+    time_act = low(jax.nn.silu(time_hidden))
     condition = product(time_act, time_second) + product(onehot, class_table)
-    cond_act = jax.nn.silu(condition).astype(jnp.bfloat16)
-    mod_shards = jnp.stack([product(cond_act, matrices[4]) for matrices in layer_list])
-    mod_full = lax.all_gather(mod_shards, "tp", axis=2, tiled=True)
-    final_modes = product(cond_act, final_weight)
+    cond_act = low(jax.nn.silu(condition))
+    mod_full = columns_in(
+        jnp.stack([product(cond_act, matrices[4]) for matrices in layer_list])
+    )
+    mode_rows = lax.dynamic_slice_in_dim(mod_full, first_image, own, 1)
+    final_rows = lax.dynamic_slice_in_dim(product(cond_act, final_weight), first_image, own, 0)
     row_index = first_row + jnp.arange(sp_rows)
-    selector = ((row_index // local_len)[:, None] == jnp.arange(images)[None, :]).astype(
-        jnp.float32
-    )
-    mode_rows = contract("ri,lid->lrd", selector, mod_full)
-    final_rows = matmul(selector, final_modes)
     signal = signal_level(timesteps)
     noisy_input = (
         jnp.sqrt(signal)[:, None, None] * latents + jnp.sqrt(1.0 - signal)[:, None, None] * noise
     )
-    noisy_rows = lax.dynamic_slice_in_dim(
-        noisy_input.reshape(images * local_len, P_SIZE), first_row, sp_rows, 0
-    ).astype(jnp.bfloat16)
+    noisy_rows = low(
+        lax.dynamic_slice_in_dim(
+            noisy_input.reshape(images * local_len, P_SIZE), first_row, sp_rows, 0
+        )
+    )
     target = lax.dynamic_slice_in_dim(
         noise.reshape(images * local_len, P_SIZE), first_row, sp_rows, 0
     )
-    stream = product(noisy_rows, patch_weight) + position_table(row_index % local_len)
+    stream = (product(noisy_rows, patch_weight) + position_table(row_index % local_len)).reshape(
+        own, group, D
+    )
     kept_list = []
     for layer_no in range(L):
         stream, kept_state = layer_forward(
             stream, mode_rows[layer_no], layer_list[layer_no], images, local_len
         )
         kept_list.append(kept_state)
-    shift_out, scale_out = jnp.split(final_rows, 2, -1)
+    shift_out, scale_out = jnp.split(final_rows[:, None, :], 2, -1)
     head_in, head_back = jax.vjp(modulate, stream, shift_out, scale_out)
-    head_low = head_in.astype(jnp.bfloat16)
+    head_low = low(head_in).reshape(sp_rows, D)
     mismatch = product(head_low, head_weight) - target
     loss_part = jnp.sum(mismatch * mismatch) / element_count
-    grad_pred = (2.0 * mismatch / element_count).astype(jnp.bfloat16)
+    grad_pred = low(2.0 * mismatch / element_count)
     grad_head = over_rows(head_low, grad_pred)
-    upstream, grad_shift_out, grad_scale_out = head_back(against(grad_pred, head_weight))
-    grad_final = matmul(selector.T, jnp.concatenate([grad_shift_out, grad_scale_out], -1))
+    upstream, grad_shift_out, grad_scale_out = head_back(
+        against(grad_pred, head_weight).reshape(own, group, D)
+    )
+    grad_final = jnp.concatenate([grad_shift_out, grad_scale_out], -1)[:, 0]
     grad_layers = [None] * L
     grad_modes = [None] * L
     for layer_no in reversed(range(L)):
@@ -410,51 +681,87 @@
             images,
             local_len,
         )
-    grad_patch = over_rows(noisy_rows, upstream.astype(jnp.bfloat16))
-    mode_image = contract("ri,lrd->lid", selector, jnp.stack(grad_modes))
-    mode_image = lax.psum_scatter(
-        mode_image.astype(jnp.bfloat16), "tp", scatter_dimension=2, tiled=True
-    ).astype(jnp.float32)
-    cond_wide = cond_act.astype(jnp.float32)
-    grad_cond_act = matmul(grad_final, final_weight.astype(jnp.float32).T)
+    grad_patch = over_rows(noisy_rows, low(upstream).reshape(sp_rows, D))
+    own_modes = jnp.concatenate(grad_modes + [grad_final], -1)
+    image_grads = tp_sum(
+        lax.dynamic_update_slice_in_dim(
+            jnp.zeros((images, own_modes.shape[1]), jnp.float32), own_modes, first_image, 0
+        )
+    )
+    grad_final = image_grads[:, 12 * D :]
+    mode_width = 6 * D // tp_parts
+    mode_image = [
+        lax.dynamic_slice_in_dim(
+            image_grads, layer_no * 6 * D + tp_index * mode_width, mode_width, 1
+        )
+        for layer_no in range(L)
+    ]
+    cond_wide = wide(cond_act)
+    grad_cond_act = 0.0
     for layer_no in range(L):
-        grad_layers[layer_no].append(contract("id,ie->de", cond_wide, mode_image[layer_no]))
+        grad_layers[layer_no].append(low(contract("id,ie->de", cond_wide, mode_image[layer_no])))
         grad_cond_act = grad_cond_act + matmul(
-            mode_image[layer_no], layer_list[layer_no][4].astype(jnp.float32).T
-        )
+            mode_image[layer_no], wide(layer_list[layer_no][4]).T
+        )
+    grad_cond_act = tp_sum(grad_cond_act) + matmul(grad_final, wide(final_weight).T)
     grad_condition = jax.vjp(jax.nn.silu, condition)[1](grad_cond_act)[0]
-    grad_table = contract("ic,id->cd", onehot.astype(jnp.float32), grad_condition)
-    grad_second = contract("ic,id->cd", time_act.astype(jnp.float32), grad_condition)
     grad_time_hidden = jax.vjp(jax.nn.silu, time_hidden)[1](
-        matmul(grad_condition, time_second.astype(jnp.float32).T)
+        matmul(grad_condition, wide(time_second).T)
     )[0]
-    grad_first = contract("ic,id->cd", features_low.astype(jnp.float32), grad_time_hidden)
-    grad_final_weight = contract("ic,id->cd", cond_wide, grad_final)
-    flat_grad = jnp.concatenate(
+    if box:
+        tile_grads = pack_layers(grad_layers)[tile_at]
+        owned = scatter_tiles(tile_grads, slots)
+    else:
+        tile_grads = wide(pack_layers(grad_layers))[ordering]
+        owned = lax.psum_scatter(tile_grads, ("fsdp", "ctx"), scatter_dimension=0, tiled=True)
+    label_column = jnp.broadcast_to(wide(labels)[:, None], (images, 128))
+    every = gather_images(
+        jnp.concatenate(
+            [
+                label_column,
+                wide(features_low),
+                grad_time_hidden,
+                grad_condition,
+                wide(time_act),
+                cond_wide,
+                grad_final,
+            ],
+            1,
+        )
+    )
+    cuts = [128, 128 + TFREQ]
+    for length in (D, D, D, D):
+        cuts.append(cuts[-1] + length)
+    all_labels, all_features, all_hidden, all_condition, all_time, all_cond, all_final = jnp.split(
+        every, cuts, 1
+    )
+    all_onehot = wide(all_labels[:, :1] == jnp.arange(NCLS, dtype=jnp.float32)[None, :])
+    token_grads = total(jnp.concatenate([grad_patch, grad_head.reshape(P_SIZE, D)], 0))
+    row_grads = jnp.concatenate(
         [
-            component.reshape(-1)
-            for component in (
-                grad_patch,
-                grad_table,
-                grad_first,
-                grad_second,
-                grad_final_weight,
-                grad_head,
-            )
-        ]
-    )
-    tile_grads = pack_layers(grad_layers)[ordering]
-    owned = lax.psum_scatter(tile_grads, ("fsdp", "ctx"), scatter_dimension=0, tiled=True)
-    else_grad = lax.psum_scatter(flat_grad, ("fsdp", "ctx", "tp"), scatter_dimension=0, tiled=True)
+            token_grads[:P_SIZE],
+            contract("ic,id->cd", all_onehot, all_condition),
+            contract("ic,id->cd", all_features, all_hidden),
+            contract("ic,id->cd", all_time, all_condition),
+            contract("ic,id->cd", all_cond, all_final).reshape(2 * D, D),
+            token_grads[P_SIZE:],
+        ],
+        0,
+    )
+    share = else_low.shape[0]
+    device = (lax.axis_index("fsdp") * ctx_parts + lax.axis_index("ctx")) * tp_parts + tp_index
+    begin = device * share
+    row_count = min(share // D + 2, row_grads.shape[0])
+    begin_row = jnp.minimum(begin // D, row_grads.shape[0] - row_count)
+    near = lax.dynamic_slice_in_dim(row_grads, begin_row, row_count, 0).reshape(-1)
+    else_grad = lax.dynamic_slice_in_dim(near, begin - begin_row * D, share, 0)
     squares = jnp.sum(owned * owned) + jnp.sum(else_grad * else_grad)
-    left_basis = reflection(bases[0, :, 0, :])
-    right_basis = reflection(bases[0, :, 1, :])
-    loss_total, square_total = global_totals(loss_part, squares)
-    grad_norm = jnp.sqrt(square_total)
+    totals = total(jnp.stack([loss_part, squares]))
+    loss_total = totals[0]
+    grad_norm = jnp.sqrt(totals[1])
     clip_factor = jnp.minimum(1.0, 1.0 / grad_norm)
-    turned = rotate(left_basis, clip_factor * owned, right_basis)
-    master_new, first_new, second_new = adam_finish(
-        turned, tiles_master[0], tiles_first[0], tiles_second[0], left_basis, right_basis
+    master_new, first_new, second_new, low_new = update_tiles(
+        clip_factor, owned, tiles_master[0], tiles_first[0], tiles_second[0], bases[0]
     )
     else_master_new, else_first_new, else_second_new = adamw_flat(
         clip_factor * else_grad, else_master, else_first, else_second
@@ -465,11 +772,11 @@
         master_new[None],
         first_new[None],
         second_new[None],
-        master_new.astype(jnp.bfloat16)[None],
+        low_new[None],
         else_master_new,
         else_first_new,
         else_second_new,
-        else_master_new.astype(jnp.bfloat16),
+        low(else_master_new),
     )
 
 

time: 2690 us -> 1710 us (0.64)
  waiting for transfers between devices: 1530 us -> 489 us
  starting transfers between devices: 1.88 us -> 197 us
  other arithmetic: 312 us -> 221 us
  matrix products: 289 us -> 227 us
  local copies, waits for them, and re-layouts: 486 us -> 541 us
  blocking collectives: 41.4 us -> 0 us
    reduce_scatter x9 -> x0, waiting for transfers between devices: 1120 us -> none  [the longest x1 1040 us: on_device(): lax.psum_scatter(tile_grads, ('fsdp', 'ctx'), scatter_dimension=0, tiled=...]
    ppermute x0 -> x145, waiting for transfers between devices: none -> 489 us  [the longest x40 181 us: swap_f(): lax.ppermute(value, 'fsdp', [(place, place ^ bit) for place in range(8)])]
    all_gather x10 -> x0, waiting for transfers between devices: 327 us -> none  [the longest x1 167 us: on_device(): lax.all_gather(tiles_low, ('fsdp', 'ctx'), axis=1, tiled=True)[0][inverse]]
    ppermute x0 -> x145, starting transfers between devices: none -> 197 us  [the longest x48 101 us: move_z(): lax.ppermute(value, 'fsdp', [(2 * from_z + x, 2 * (from_z + step) + x) fo...]
    all_gather x1 -> x0, other arithmetic: 190 us -> none  [on_device(): lax.all_gather(else_low, ('fsdp', 'ctx', 'tp'), axis=0, tiled=True)]
    unnamed x23 -> x0, waiting for transfers between devices: 85.7 us -> none
    slice x13 -> x3, local copies, waits for them, and re-layouts: 23.2 us -> 80.6 us  [split_else(): flat_params[cursor:cursor + height * breadth].reshape(height, breadth)]
    dot_general x12 -> x6, matrix products: 78.4 us -> 31.1 us  [contract(): return jnp.einsum(formula, left_op, right_op, precision=HIGHEST)]
  transfers between devices with their start and end apart: 21 -> 145, of which waited for: 16 -> 53; matrix products, arithmetic and copies ran while one was open for 22% -> 36% of each run, Pallas kernels for 0% -> 0%
where the time goes in v1:
time: 1710 us; the launch traced here: 1700 us
  local copies, waits for them, and re-layouts  541 us (32%)
  waiting for transfers between devices  489 us (29%)
  matrix products  227 us (13%)
  other arithmetic  221 us (13%)
  starting transfers between devices  197 us (12%)
    ppermute x40, waiting for transfers between devices, swap_f(): lax.ppermute(value, 'fsdp', [(place, place ^ bit) for place in range(8)])  181 us
    ppermute x35, waiting for transfers between devices, swap_y(): return lax.ppermute(value, 'ctx', [(0, 1), (1, 0)])  177 us
    unnamed x575, local copies, waits for them, and re-layouts  143 us
    ppermute x48, waiting for transfers between devices, move_z(): lax.ppermute(value, 'fsdp', [(2 * from_z + x, 2 * (from_z + step) + x) fo...  108 us
    ppermute x48, starting transfers between devices, move_z(): lax.ppermute(value, 'fsdp', [(2 * from_z + x, 2 * (from_z + step) + x) fo...  101 us
    slice x3, local copies, waits for them, and re-layouts, split_else(): flat_params[cursor:cursor + height * breadth].reshape(height, breadth)  80.6 us
    ppermute x40, starting transfers between devices, swap_f(): lax.ppermute(value, 'fsdp', [(place, place ^ bit) for place in range(8)])  58 us
    convert_element_type x20, other arithmetic, low(): return value.astype(jnp.bfloat16)  51.3 us
  transfers between devices with their start and end apart: 145, of which 53 were waited for; matrix products, arithmetic and copies ran while one was open for 36% of the time, Pallas kernels for 0%

profile of v1, /device:TPU:0, one launch (start us, length us, event | category | flops | bytes accessed | tf_op | source)
XLA Modules:
  0.0 1698.3 jit_solution(79312084000802131)
XLA Ops:
  12.4 17.0 %collective-permute-done.12 = bf16[32,128,128]{2,1,0:T(8,128)(2,1)S(1)} collective-permute-done((bf16[32,128,128]{2,1,0:T(8,128)(2,1)}, bf16[32,128,128]{2,1,0:T(8,128)(2,1)S(1)}, u32[]{:S(2)}, u32[]{:S(2)}) %collective-permute-start.12) | collective-permute-done | bytes 1048608 | tf_op jit(solution)/shard_map/ppermute | solution.py:185
  81.0 10.6 collective-permute-done.3
  111.5 18.6 %collective-permute-done.24 = bf16[32,128,128]{2,1,0:T(8,128)(2,1)S(1)} collective-permute-done((bf16[32,128,128]{2,1,0:T(8,128)(2,1)S(1)}, bf16[32,128,128]{2,1,0:T(8,128)(2,1)S(1)}, u32[]{:S(2)}, u32[]{:S(2)}) %collective-permute-start.24) | collective-permute-done | bytes 1048608 | tf_op jit(solution)/shard_map/ppermute | solution.py:185
  151.9 48.7 %collective-permute-done.33 = bf16[20,128,128]{2,1,0:T(8,128)(2,1)S(1)} collective-permute-done((bf16[20,128,128]{2,1,0:T(8,128)(2,1)S(1)}, bf16[20,128,128]{2,1,0:T(8,128)(2,1)S(1)}, u32[]{:S(2)}, u32[]{:S(2)}) %collective-permute-start.33) | collective-permute-done | bytes 655392 | tf_op jit(solution)/shard_map/ppermute | solution.py:185
  214.4 26.5 %collective-permute-done.31 = bf16[16,128,128]{2,1,0:T(8,128)(2,1)S(1)} collective-permute-done((bf16[16,128,128]{2,1,0:T(8,128)(2,1)S(1)}, bf16[16,128,128]{2,1,0:T(8,128)(2,1)S(1)}, u32[]{:S(2)}, u32[]{:S(2)}) %collective-permute-start.31) | collective-permute-done | bytes 524320 | tf_op jit(solution)/shard_map/ppermute | solution.py:181
  300.8 10.2 copy.210
  311.0 10.9 collective-permute-done.40
  338.2 20.3 %collective-permute-done.43 = bf16[40,128,128]{2,1,0:T(8,128)(2,1)} collective-permute-done((bf16[40,128,128]{2,1,0:T(8,128)(2,1)}, bf16[40,128,128]{2,1,0:T(8,128)(2,1)}, u32[]{:S(2)}, u32[]{:S(2)}) %collective-permute-start.43) | collective-permute-done | bytes 1310752 | tf_op jit(solution)/shard_map/ppermute | solution.py:181
  424.9 15.5 slice.358
  450.8 19.3 %collective-permute-done.54 = bf16[40,128,128]{2,1,0:T(8,128)(2,1)S(1)} collective-permute-done((bf16[40,128,128]{2,1,0:T(8,128)(2,1)S(1)}, bf16[40,128,128]{2,1,0:T(8,128)(2,1)S(1)}, u32[]{:S(2)}, u32[]{:S(2)}) %collective-permute-start.54) | collective-permute-done | bytes 1310752 | tf_op jit(solution)/shard_map/ppermute | solution.py:185
  471.3 28.4 %gather_fusion = bf16[1152,128,128]{2,1,0:T(8,128)(2,1)} fusion(bf16[1152,128,128]{2,1,0:T(8,128)(2,1)} %constant_dynamic-update-slice_fusion, s32[2048]{0:T(1024)S(1)} %copy-done.198), kind=kCustom, calls=%fused_computation | custom fusion | bytes 75502080 | tf_op jit(solution)/shard_map/gather | solution.py:625
  590.8 11.3 fusion.291
  702.3 13.8 slice.403
  716.2 51.3 %slice.405 = bf16[279040,16]{1,0:T(8,128)(2,1)} reshape(bf16[4,2,2,2,1090,128]{5,4,3,2,1,0:T(8,128)(2,1)} %copy.213) | data formatting | bytes 17858560 | tf_op jit(solution)/shard_map/slice | solution.py:137
  795.0 14.7 fusion.13
  895.2 9.4 convert_bitcast_fusion.2
  918.9 9.3 fusion.6
  972.2 11.5 convert_bitcast_fusion.4
  1126.1 28.6 %gather_fusion.1 = bf16[1152,128,128]{2,1,0:T(8,128)(2,1)} fusion(bf16[1152,128,128]{2,1,0:T(8,128)(2,1)} %constant_dynamic-update-slice_fusion.56, s32[2048]{0:T(1024)S(1)} %copy-done.196), kind=kCustom, calls=%fused_computation.1 | custom fusion | bytes 75502080 | tf_op jit(solution)/shard_map/gather | solution.py:712
  1197.7 13.0 fusion.290
  1229.1 9.4 collective-permute-done.79
  1264.1 9.3 collective-permute-done.81
  1312.1 30.9 %collective-permute-done.138 = f32[16,6528]{1,0:T(8,128)} collective-permute-done((f32[16,6528]{1,0:T(8,128)}, f32[16,6528]{1,0:T(8,128)}, u32[]{:S(2)}, u32[]{:S(2)}) %collective-permute-start.138) | collective-permute-done | bytes 417824 | tf_op jit(solution)/shard_map/ppermute | solution.py:181
  1356.7 29.7 %collective-permute-done.92 = bf16[16,128,128]{2,1,0:T(8,128)(2,1)} collective-permute-done((bf16[16,128,128]{2,1,0:T(8,128)(2,1)}, bf16[16,128,128]{2,1,0:T(8,128)(2,1)}, u32[]{:S(2)}, u32[]{:S(2)}) %collective-permute-start.92) | collective-permute-done | bytes 524320 | tf_op jit(solution)/shard_map/ppermute | solution.py:185
  1419.7 22.0 %collective-permute-done.90 = bf16[16,128,128]{2,1,0:T(8,128)(2,1)} collective-permute-done((bf16[16,128,128]{2,1,0:T(8,128)(2,1)}, bf16[16,128,128]{2,1,0:T(8,128)(2,1)}, u32[]{:S(2)}, u32[]{:S(2)}) %collective-permute-start.90) | collective-permute-done | bytes 524320 | tf_op jit(solution)/shard_map/ppermute | solution.py:181
  1455.1 9.3 reshape.864
  1505.2 24.1 %collective-permute-done.108 = bf16[2,20,128,128]{3,2,1,0:T(8,128)(2,1)} collective-permute-done((bf16[2,20,128,128]{3,2,1,0:T(8,128)(2,1)}, bf16[2,20,128,128]{3,2,1,0:T(8,128)(2,1)}, u32[]{:S(2)}, u32[]{:S(2)}) %collective-permute-start.108) | collective-permute-done | bytes 1310752 | tf_op jit(solution)/shard_map/ppermute | solution.py:193
  1539.1 18.3 %collective-permute-done.119 = bf16[2,20,128,128]{3,2,1,0:T(8,128)(2,1)} collective-permute-done((bf16[2,20,128,128]{3,2,1,0:T(8,128)(2,1)}, bf16[2,20,128,128]{3,2,1,0:T(8,128)(2,1)}, u32[]{:S(2)}, u32[]{:S(2)}) %collective-permute-start.119) | collective-permute-done | bytes 1310752 | tf_op jit(solution)/shard_map/ppermute | solution.py:193
  1570.3 9.5 collective-permute-done.98
  1591.9 15.9 collective-permute-done.109
  1617.6 13.3 collective-permute-done.120
  1682.0 14.9 shard_map.213
  (1179 shorter events, 1094.2 us)
Async XLA Ops:
  134.9 66.4 %collective-permute-start.7 = (bf16[4,1090,128]{2,0,1:T(4,128)(2,1)S(1)}, bf16[4,1090,128]{2,0,1:T(4,128)(2,1)S(1)}, u32[]{:S(2)}, u32[]{:S(2)}) collective-permute-start(bf16[4,1090,128]{2,0,1:T(4,128)(2,1)S(1)} %copy.202), channel_id=1, source_target_pairs={{0,4},{4,0},{8,12},{12,8},{16,20},{20,16},{24,28},{28,24},{1,5},{5... | collective-permute-start | bytes 3348488 | tf_op jit(solution)/shard_map/ppermute | solution.py:185
  141.8 67.9 %collective-permute-start.6 = (bf16[4,1090,128]{2,0,1:T(4,128)(2,1)S(1)}, bf16[4,1090,128]{2,0,1:T(4,128)(2,1)S(1)}, u32[]{:S(2)}, u32[]{:S(2)}) collective-permute-start(bf16[4,1090,128]{2,0,1:T(4,128)(2,1)S(1)} %copy.202), channel_id=1, source_target_pairs={{0,2},{2,0},{1,3},{3,1},{4,6},{6,4},{5,7},{7,5},{8,10},{10,8},{9,1... | collective-permute-start | bytes 3348488 | tf_op jit(solution)/shard_map/ppermute | solution.py:181
  147.7 60.4 %collective-permute-start.29 = (bf16[32,128,128]{2,1,0:T(8,128)(2,1)S(1)}, bf16[32,128,128]{2,1,0:T(8,128)(2,1)S(1)}, u32[]{:S(2)}, u32[]{:S(2)}) collective-permute-start(bf16[32,128,128]{2,1,0:T(8,128)(2,1)S(1)} %get-tuple-element.87), channel_id=1, source_target_pairs={{0,2},{2,0},{1,3},{3,1},{4,6},{6,4},{5,7},{7,5},{8,10},{10,8},{9,1... | collective-permute-start | bytes 3145736 | tf_op jit(solution)/shard_map/ppermute | solution.py:181
  149.7 57.0 %collective-permute-start.30 = (bf16[32,128,128]{2,1,0:T(8,128)(2,1)S(1)}, bf16[32,128,128]{2,1,0:T(8,128)(2,1)S(1)}, u32[]{:S(2)}, u32[]{:S(2)}) collective-permute-start(bf16[32,128,128]{2,1,0:T(8,128)(2,1)S(1)} %get-tuple-element.87), channel_id=1, source_target_pairs={{0,4},{4,0},{8,12},{12,8},{16,20},{20,16},{24,28},{28,24},{1,5},{5... | collective-permute-start | bytes 3145736 | tf_op jit(solution)/shard_map/ppermute | solution.py:185
  150.2 50.5 %collective-permute-start.33 = (bf16[20,128,128]{2,1,0:T(8,128)(2,1)S(1)}, bf16[20,128,128]{2,1,0:T(8,128)(2,1)S(1)}, u32[]{:S(2)}, u32[]{:S(2)}) collective-permute-start(bf16[20,128,128]{2,1,0:T(8,128)(2,1)S(1)} %get-tuple-element.162), channel_id=1, source_target_pairs={{0,4},{4,0},{8,12},{12,8},{16,20},{20,16},{24,28},{28,24},{1,5},{5... | collective-permute-start | bytes 1966088 | tf_op jit(solution)/shard_map/ppermute | solution.py:185
  270.6 64.5 %collective-permute-start.46 = (bf16[40,128,128]{2,1,0:T(8,128)(2,1)}, bf16[40,128,128]{2,1,0:T(8,128)(2,1)}, u32[]{:S(2)}, u32[]{:S(2)}) collective-permute-start(bf16[40,128,128]{2,1,0:T(8,128)(2,1)} %pad_maximum_fusion.28), channel_id=1, source_target_pairs={{0,8},{4,12},{8,16},{12,20},{16,24},{20,28},{1,9},{5,13},{9,17},{1... | collective-permute-start | bytes 3932168 | tf_op jit(solution)/shard_map/ppermute | solution.py:193
  278.0 58.9 %collective-permute-start.47 = (bf16[40,128,128]{2,1,0:T(8,128)(2,1)}, bf16[40,128,128]{2,1,0:T(8,128)(2,1)}, u32[]{:S(2)}, u32[]{:S(2)}) collective-permute-start(bf16[40,128,128]{2,1,0:T(8,128)(2,1)} %pad_maximum_fusion.28), channel_id=1, source_target_pairs={{8,0},{12,4},{16,8},{20,12},{24,16},{28,20},{9,1},{13,5},{17,9},{2... | collective-permute-start | bytes 3932168 | tf_op jit(solution)/shard_map/ppermute | solution.py:193
  321.9 81.0 %collective-permute-start.10 = (bf16[4,2,2,1090,128]{4,0,3,2,1:T(4,128)(2,1)}, bf16[4,2,2,1090,128]{4,0,3,2,1:T(4,128)(2,1)}, u32[]{:S(2)}, u32[]{:S(2)}) collective-permute-start(bf16[4,2,2,1090,128]{4,0,3,2,1:T(4,128)(2,1)} %copy.210), channel_id=1, source_target_pairs={{0,1},{1,0},{2,3},{3,2},{4,5},{5,4},{6,7},{7,6},{8,9},{9,8},{10,11... | collective-permute-start | bytes 13393928 | tf_op jit(solution)/shard_map/ppermute | solution.py:177
  335.1 59.6 %collective-permute-start.49 = (bf16[40,128,128]{2,1,0:T(8,128)(2,1)}, bf16[40,128,128]{2,1,0:T(8,128)(2,1)}, u32[]{:S(2)}, u32[]{:S(2)}) collective-permute-start(bf16[40,128,128]{2,1,0:T(8,128)(2,1)} %collective-permute-done.46), channel_id=1, source_target_pairs={{8,16},{12,20},{16,24},{20,28},{9,17},{13,21},{17,25},{21,29},{10,... | collective-permute-start | bytes 3932168 | tf_op jit(solution)/shard_map/ppermute | solution.py:193
  336.9 56.5 %collective-permute-start.50 = (bf16[40,128,128]{2,1,0:T(8,128)(2,1)}, bf16[40,128,128]{2,1,0:T(8,128)(2,1)}, u32[]{:S(2)}, u32[]{:S(2)}) collective-permute-start(bf16[40,128,128]{2,1,0:T(8,128)(2,1)} %collective-permute-done.47), channel_id=1, source_target_pairs={{8,0},{12,4},{16,8},{20,12},{9,1},{13,5},{17,9},{21,13},{10,2},{14... | collective-permute-start | bytes 3932168 | tf_op jit(solution)/shard_map/ppermute | solution.py:193
  393.4 48.2 %collective-permute-start.52 = (bf16[40,128,128]{2,1,0:T(8,128)(2,1)}, bf16[40,128,128]{2,1,0:T(8,128)(2,1)}, u32[]{:S(2)}, u32[]{:S(2)}) collective-permute-start(bf16[40,128,128]{2,1,0:T(8,128)(2,1)} %collective-permute-done.50), channel_id=1, source_target_pairs={{8,0},{12,4},{9,1},{13,5},{10,2},{14,6},{11,3},{15,7}} | collective-permute-start | bytes 3932168 | tf_op jit(solution)/shard_map/ppermute | solution.py:193
  702.0 68.9 %collective-permute-start.63 = (f32[512,1024]{1,0:T(8,128)}, f32[512,1024]{1,0:T(8,128)}, u32[]{:S(2)}, u32[]{:S(2)}) collective-permute-start(f32[512,1024]{1,0:T(8,128)} %slice.515), channel_id=1, source_target_pairs={{0,1},{1,0},{2,3},{3,2},{4,5},{5,4},{6,7},{7,6},{8,9},{9,8},{10,11... | collective-permute-start | bytes 6291464 | tf_op jit(solution)/shard_map/ppermute | solution.py:177
  1073.0 113.0 %collective-permute-start.126 = (f32[32,1024]{1,0:T(8,128)S(1)}, f32[32,1024]{1,0:T(8,128)S(1)}, u32[]{:S(2)}, u32[]{:S(2)}) collective-permute-start(f32[32,1024]{1,0:T(8,128)S(1)} %fusion.274), channel_id=1, source_target_pairs={{0,2},{2,0},{1,3},{3,1},{4,6},{6,4},{5,7},{7,5},{8,10},{10,8},{9,1... | collective-permute-start | bytes 393224 | tf_op jit(solution)/shard_map/ppermute | solution.py:181
  1100.3 63.0 %collective-permute-start.130 = (f32[4,1024]{1,0:T(4,128)S(1)}, f32[4,1024]{1,0:T(4,128)}, u32[]{:S(2)}, u32[]{:S(2)}) collective-permute-start(f32[4,1024]{1,0:T(4,128)S(1)} %fusion.164), channel_id=1, source_target_pairs={{0,1},{1,0},{2,3},{3,2},{4,5},{5,4},{6,7},{7,6},{8,9},{9,8},{10,11... | collective-permute-start | bytes 49160 | tf_op jit(solution)/shard_map/ppermute | solution.py:177
  1287.9 100.4 %collective-permute-start.104 = (bf16[2,20,128,128]{3,2,1,0:T(8,128)(2,1)}, bf16[2,20,128,128]{3,2,1,0:T(8,128)(2,1)S(1)}, u32[]{:S(2)}, u32[]{:S(2)}) collective-permute-start(bf16[2,20,128,128]{3,2,1,0:T(8,128)(2,1)} %get-tuple-element.141), channel_id=1, source_target_pairs={{0,2},{2,0},{1,3},{3,1},{4,6},{6,4},{5,7},{7,5},{8,10},{10,8},{9,1... | collective-permute-start | bytes 3932168 | tf_op jit(solution)/shard_map/ppermute | solution.py:181
  1295.9 47.2 %collective-permute-start.138 = (f32[16,6528]{1,0:T(8,128)}, f32[16,6528]{1,0:T(8,128)}, u32[]{:S(2)}, u32[]{:S(2)}) collective-permute-start(f32[16,6528]{1,0:T(8,128)} %pad_maximum_fusion.35), channel_id=1, source_target_pairs={{0,2},{2,0},{1,3},{3,1},{4,6},{6,4},{5,7},{7,5},{8,10},{10,8},{9,1... | collective-permute-start | bytes 1253384 | tf_op jit(solution)/shard_map/ppermute | solution.py:181
  1343.1 62.5 %collective-permute-start.115 = (bf16[2,20,128,128]{3,2,1,0:T(8,128)(2,1)}, bf16[2,20,128,128]{3,2,1,0:T(8,128)(2,1)}, u32[]{:S(2)}, u32[]{:S(2)}) collective-permute-start(bf16[2,20,128,128]{3,2,1,0:T(8,128)(2,1)} %get-tuple-element.145), channel_id=1, source_target_pairs={{0,4},{4,0},{8,12},{12,8},{16,20},{20,16},{24,28},{28,24},{1,5},{5... | collective-permute-start | bytes 3932168 | tf_op jit(solution)/shard_map/ppermute | solution.py:185
  1386.3 57.0 %collective-permute-start.106 = (bf16[2,20,128,128]{3,2,1,0:T(8,128)(2,1)}, bf16[2,20,128,128]{3,2,1,0:T(8,128)(2,1)}, u32[]{:S(2)}, u32[]{:S(2)}) collective-permute-start(bf16[2,20,128,128]{3,2,1,0:T(8,128)(2,1)} %get-tuple-element.139), channel_id=1, source_target_pairs={{0,2},{2,0},{1,3},{3,1},{4,6},{6,4},{5,7},{7,5},{8,10},{10,8},{9,1... | collective-permute-start | bytes 3932168 | tf_op jit(solution)/shard_map/ppermute | solution.py:181
  1387.7 59.1 %collective-permute-start.105 = (bf16[2,20,128,128]{3,2,1,0:T(8,128)(2,1)}, bf16[2,20,128,128]{3,2,1,0:T(8,128)(2,1)}, u32[]{:S(2)}, u32[]{:S(2)}) collective-permute-start(bf16[2,20,128,128]{3,2,1,0:T(8,128)(2,1)} %get-tuple-element.140), channel_id=1, source_target_pairs={{0,2},{2,0},{1,3},{3,1},{4,6},{6,4},{5,7},{7,5},{8,10},{10,8},{9,1... | collective-permute-start | bytes 3932168 | tf_op jit(solution)/shard_map/ppermute | solution.py:181
  1393.4 59.2 %collective-permute-start.107 = (bf16[2,20,128,128]{3,2,1,0:T(8,128)(2,1)}, bf16[2,20,128,128]{3,2,1,0:T(8,128)(2,1)}, u32[]{:S(2)}, u32[]{:S(2)}) collective-permute-start(bf16[2,20,128,128]{3,2,1,0:T(8,128)(2,1)} %fusion.92), channel_id=1, source_target_pairs={{0,8},{4,12},{1,9},{5,13},{2,10},{6,14},{3,11},{7,15}} | collective-permute-start | bytes 3932168 | tf_op jit(solution)/shard_map/ppermute | solution.py:193
  1405.5 58.9 %collective-permute-start.110 = (bf16[2,20,128,128]{3,2,1,0:T(8,128)(2,1)}, bf16[2,20,128,128]{3,2,1,0:T(8,128)(2,1)}, u32[]{:S(2)}, u32[]{:S(2)}) collective-permute-start(bf16[2,20,128,128]{3,2,1,0:T(8,128)(2,1)} %fusion.92), channel_id=1, source_target_pairs={{24,16},{28,20},{25,17},{29,21},{26,18},{30,22},{27,19},{31,23}} | collective-permute-start | bytes 3932168 | tf_op jit(solution)/shard_map/ppermute | solution.py:193
  1478.3 51.0 %collective-permute-start.108 = (bf16[2,20,128,128]{3,2,1,0:T(8,128)(2,1)}, bf16[2,20,128,128]{3,2,1,0:T(8,128)(2,1)}, u32[]{:S(2)}, u32[]{:S(2)}) collective-permute-start(bf16[2,20,128,128]{3,2,1,0:T(8,128)(2,1)} %get-tuple-element.134), channel_id=1, source_target_pairs={{0,8},{4,12},{8,16},{12,20},{1,9},{5,13},{9,17},{13,21},{2,10},{6,... | collective-permute-start | bytes 3932168 | tf_op jit(solution)/shard_map/ppermute | solution.py:193
  1480.6 53.1 %collective-permute-start.111 = (bf16[2,20,128,128]{3,2,1,0:T(8,128)(2,1)}, bf16[2,20,128,128]{3,2,1,0:T(8,128)(2,1)}, u32[]{:S(2)}, u32[]{:S(2)}) collective-permute-start(bf16[2,20,128,128]{3,2,1,0:T(8,128)(2,1)} %get-tuple-element.135), channel_id=1, source_target_pairs={{16,8},{20,12},{24,16},{28,20},{17,9},{21,13},{25,17},{29,21},{18,... | collective-permute-start | bytes 3932168 | tf_op jit(solution)/shard_map/ppermute | solution.py:193
  1488.1 69.3 %collective-permute-start.119 = (bf16[2,20,128,128]{3,2,1,0:T(8,128)(2,1)}, bf16[2,20,128,128]{3,2,1,0:T(8,128)(2,1)}, u32[]{:S(2)}, u32[]{:S(2)}) collective-permute-start(bf16[2,20,128,128]{3,2,1,0:T(8,128)(2,1)} %get-tuple-element.136), channel_id=1, source_target_pairs={{0,8},{4,12},{8,16},{12,20},{1,9},{5,13},{9,17},{13,21},{2,10},{6,... | collective-permute-start | bytes 3932168 | tf_op jit(solution)/shard_map/ppermute | solution.py:193
  1490.5 71.4 %collective-permute-start.122 = (bf16[2,20,128,128]{3,2,1,0:T(8,128)(2,1)}, bf16[2,20,128,128]{3,2,1,0:T(8,128)(2,1)}, u32[]{:S(2)}, u32[]{:S(2)}) collective-permute-start(bf16[2,20,128,128]{3,2,1,0:T(8,128)(2,1)} %get-tuple-element.137), channel_id=1, source_target_pairs={{16,8},{20,12},{24,16},{28,20},{17,9},{21,13},{25,17},{29,21},{18,... | collective-permute-start | bytes 3932168 | tf_op jit(solution)/shard_map/ppermute | solution.py:193
  1501.2 67.4 %collective-permute-start.103 = (bf16[2,20,128,128]{3,2,1,0:T(8,128)(2,1)}, bf16[2,20,128,128]{3,2,1,0:T(8,128)(2,1)S(1)}, u32[]{:S(2)}, u32[]{:S(2)}) collective-permute-start(bf16[2,20,128,128]{3,2,1,0:T(8,128)(2,1)} %get-tuple-element.138), channel_id=1, source_target_pairs={{0,2},{2,0},{1,3},{3,1},{4,6},{6,4},{5,7},{7,5},{8,10},{10,8},{9,1... | collective-permute-start | bytes 3932168 | tf_op jit(solution)/shard_map/ppermute | solution.py:181
  1529.3 50.5 %collective-permute-start.98 = (bf16[32,128,128]{2,1,0:T(8,128)(2,1)S(1)}, bf16[32,128,128]{2,1,0:T(8,128)(2,1)S(1)}, u32[]{:S(2)}, u32[]{:S(2)}) collective-permute-start(bf16[32,128,128]{2,1,0:T(8,128)(2,1)S(1)} %get-tuple-element.104), channel_id=1, source_target_pairs={{0,8},{4,12},{8,16},{12,20},{1,9},{5,13},{9,17},{13,21},{2,10},{6,... | collective-permute-start | bytes 3145736 | tf_op jit(solution)/shard_map/ppermute | solution.py:193
  1533.8 50.5 %collective-permute-start.101 = (bf16[32,128,128]{2,1,0:T(8,128)(2,1)S(1)}, bf16[32,128,128]{2,1,0:T(8,128)(2,1)S(1)}, u32[]{:S(2)}, u32[]{:S(2)}) collective-permute-start(bf16[32,128,128]{2,1,0:T(8,128)(2,1)S(1)} %get-tuple-element.105), channel_id=1, source_target_pairs={{16,8},{20,12},{24,16},{28,20},{17,9},{21,13},{25,17},{29,21},{18,... | collective-permute-start | bytes 3145736 | tf_op jit(solution)/shard_map/ppermute | solution.py:193
  1557.4 50.5 %collective-permute-start.109 = (bf16[2,20,128,128]{3,2,1,0:T(8,128)(2,1)S(1)}, bf16[2,20,128,128]{3,2,1,0:T(8,128)(2,1)S(1)}, u32[]{:S(2)}, u32[]{:S(2)}) collective-permute-start(bf16[2,20,128,128]{3,2,1,0:T(8,128)(2,1)S(1)} %get-tuple-element.130), channel_id=1, source_target_pairs={{0,8},{4,12},{8,16},{12,20},{16,24},{20,28},{1,9},{5,13},{9,17},{1... | collective-permute-start | bytes 3932168 | tf_op jit(solution)/shard_map/ppermute | solution.py:193
  1561.9 50.4 %collective-permute-start.112 = (bf16[2,20,128,128]{3,2,1,0:T(8,128)(2,1)S(1)}, bf16[2,20,128,128]{3,2,1,0:T(8,128)(2,1)S(1)}, u32[]{:S(2)}, u32[]{:S(2)}) collective-permute-start(bf16[2,20,128,128]{3,2,1,0:T(8,128)(2,1)S(1)} %get-tuple-element.131), channel_id=1, source_target_pairs={{8,0},{12,4},{16,8},{20,12},{24,16},{28,20},{9,1},{13,5},{17,9},{2... | collective-permute-start | bytes 3932168 | tf_op jit(solution)/shard_map/ppermute | solution.py:193
  1568.7 47.2 %collective-permute-start.114 = (bf16[2,20,128,128]{3,2,1,0:T(8,128)(2,1)S(1)}, bf16[2,20,128,128]{3,2,1,0:T(8,128)(2,1)S(1)}, u32[]{:S(2)}, u32[]{:S(2)}) collective-permute-start(bf16[2,20,128,128]{3,2,1,0:T(8,128)(2,1)S(1)} %copy-done.102), channel_id=1, source_target_pairs={{0,4},{4,0},{8,12},{12,8},{16,20},{20,16},{24,28},{28,24},{1,5},{5... | collective-permute-start | bytes 3932168 | tf_op jit(solution)/shard_map/ppermute | solution.py:185
  1579.8 51.1 %collective-permute-start.120 = (bf16[2,20,128,128]{3,2,1,0:T(8,128)(2,1)S(1)}, bf16[2,20,128,128]{3,2,1,0:T(8,128)(2,1)S(1)}, u32[]{:S(2)}, u32[]{:S(2)}) collective-permute-start(bf16[2,20,128,128]{3,2,1,0:T(8,128)(2,1)S(1)} %get-tuple-element.132), channel_id=1, source_target_pairs={{0,8},{4,12},{8,16},{12,20},{16,24},{20,28},{1,9},{5,13},{9,17},{1... | collective-permute-start | bytes 3932168 | tf_op jit(solution)/shard_map/ppermute | solution.py:193
  (364 other events, 6261.5 us)

commit v2 on v1

v2 whole, which is shorter than its diff:
```python
import math

import jax
import jax.numpy as jnp
from jax import lax
from jax.experimental import pallas as pl
from jax.experimental.pallas import tpu as pltpu
from jax.sharding import PartitionSpec as P

D = 1024
HD = 64
F = 4096
P_SIZE = 16
TFREQ = 256
NCLS = 1000
GRID = 16
L = 2
B = 128


HIGHEST = lax.Precision.HIGHEST
EPS_NORM = 1e-06
RATE = 0.02
DECAY = 0.1


def matmul(left_op, right_op):
    return jnp.dot(left_op, right_op, precision=HIGHEST)


def contract(formula, left_op, right_op):
    return jnp.einsum(formula, left_op, right_op, precision=HIGHEST)


def product(left_op, right_op):
    return jnp.dot(left_op, right_op, preferred_element_type=jnp.float32)


def over_rows(left_op, right_op):
    return lax.dot_general(
        left_op, right_op, (((0,), (0,)), ((), ())), preferred_element_type=jnp.float32
    )


def against(left_op, right_op):
    return lax.dot_general(
        left_op, right_op, (((1,), (1,)), ((), ())), preferred_element_type=jnp.float32
    )


def normed(stream):
    centred = stream - jnp.mean(stream, -1, keepdims=True)
    return centred * lax.rsqrt(jnp.mean(centred * centred, -1, keepdims=True) + EPS_NORM)


def modulate(stream, offset, factor):
    return normed(stream) * (1.0 + factor) + offset


def gelu_tanh(values):
    return jax.nn.gelu(values, approximate=True)


def time_features(time_steps):
    half_count = TFREQ // 2
    freqs = jnp.exp(-math.log(10000.0) * jnp.arange(half_count, dtype=jnp.float32) / half_count)
    angles = time_steps.astype(jnp.float32)[:, None] * freqs[None, :]
    return jnp.concatenate([jnp.cos(angles), jnp.sin(angles)], -1)


def position_table(token_ids):
    quarter = D // 4
    omegas = 1.0 / 10000.0 ** (jnp.arange(quarter, dtype=jnp.float32) / quarter)
    row_angle = (token_ids // GRID).astype(jnp.float32)[:, None] * omegas[None, :]
    col_angle = (token_ids % GRID).astype(jnp.float32)[:, None] * omegas[None, :]
    return jnp.concatenate(
        [jnp.sin(row_angle), jnp.cos(row_angle), jnp.sin(col_angle), jnp.cos(col_angle)], -1
    )


def signal_level(time_steps):
    phase = (time_steps.astype(jnp.float32) / 1000.0 + 0.008) / 1.008 * (math.pi / 2)
    return jnp.cos(phase) ** 2


def shard_shapes(tp_parts):
    head_width = D // tp_parts
    hidden_width = F // tp_parts
    return [
        (D, 3 * head_width),
        (head_width, D),
        (D, hidden_width),
        (hidden_width, D),
        (D, 6 * head_width),
    ]


def untile(tile_set, height, breadth):
    block = tile_set.shape[-1]
    return (
        tile_set.reshape(height // block, breadth // block, block, block)
        .transpose(0, 2, 1, 3)
        .reshape(height, breadth)
    )


def retile(matrix):
    height, breadth = matrix.shape
    return matrix.reshape(height // B, B, breadth // B, B).transpose(0, 2, 1, 3).reshape(-1, B, B)


def unpack_layers(tile_set, tp_parts):
    layer_list = []
    cursor = 0
    for layer_no in range(L):
        matrices = []
        for height, breadth in shard_shapes(tp_parts):
            amount = height * breadth // (B * B)
            matrices.append(untile(tile_set[cursor : cursor + amount], height, breadth))
            cursor += amount
        layer_list.append(matrices)
    return layer_list


def pack_layers(layer_list):
    return jnp.concatenate([retile(matrix) for matrices in layer_list for matrix in matrices], 0)


def else_shapes():
    return [(P_SIZE, D), (NCLS, D), (TFREQ, D), (D, D), (D, 2 * D), (D, P_SIZE)]


def split_else(flat_params):
    components = []
    cursor = 0
    for height, breadth in else_shapes():
        components.append(flat_params[cursor : cursor + height * breadth].reshape(height, breadth))
        cursor += height * breadth
    return components


def reflection(vectors):
    outer_prod = vectors[..., :, None] * vectors[..., None, :]
    return (
        jnp.eye(vectors.shape[-1], dtype=jnp.float32)
        - 2.0 * outer_prod / jnp.sum(vectors * vectors, -1)[..., None, None]
    )


def rotate(left_basis, middle, right_basis):
    return contract(
        "...ab,...bc->...ac", contract("...ab,...bc->...ac", left_basis, middle), right_basis
    )


def adam_finish(turned, master_state, first_state, second_state, left_basis, right_basis):
    first_new = 0.5 * first_state + 0.5 * turned
    second_new = 0.5 * second_state + 0.5 * turned * turned
    direction = first_new / (jnp.sqrt(second_new) + 1e-08)
    return (master_state - RATE * rotate(left_basis, direction, right_basis), first_new, second_new)


def adamw_flat(grad_clipped, master_state, first_state, second_state):
    first_new = 0.5 * first_state + 0.5 * grad_clipped
    second_new = 0.5 * second_state + 0.5 * grad_clipped * grad_clipped
    master_new = master_state - RATE * (
        first_new / (jnp.sqrt(second_new) + 1e-08) + DECAY * master_state
    )
    return (master_new, first_new, second_new)


def is_box():
    return (lax.axis_size("fsdp"), lax.axis_size("ctx"), lax.axis_size("tp")) == (8, 2, 2)


def swap_tp(value):
    return lax.ppermute(value, "tp", [(0, 1), (1, 0)])


def swap_y(value):
    return lax.ppermute(value, "ctx", [(0, 1), (1, 0)])


def swap_f(value, bit):
    return lax.ppermute(value, "fsdp", [(place, place ^ bit) for place in range(8)])


def swap_x(value):
    return swap_f(value, 1)


def place_z():
    return lax.axis_index("fsdp") // 2


def low(value):
    return value.astype(jnp.bfloat16)


def wide(value):
    return value.astype(jnp.float32)


def after(value, *earlier):
    return lax.optimization_barrier((value, *earlier))[0]


class Lanes:
    def __init__(self):
        self.done = ()

    def step(self, sends, *earlier):
        values = lax.optimization_barrier(tuple(value for _, value in sends) + self.done + earlier)
        self.done = tuple(swap(value) for (swap, _), value in zip(sends, values))
        return list(self.done)


def move_z(step, sources):
    pairs = [(2 * z + x, 2 * (z + step) + x) for z in sources for x in range(2)]
    return lambda value: lax.ppermute(value, "fsdp", pairs)


def to_z(rel):
    return lambda value: swap_f(value, 2 * rel)


class ZLine:
    def __init__(self, own):
        self.above, self.below = [own], [own]

    def sends(self):
        hop = len(self.above)
        return [
            (move_z(1, range(hop - 1, 3)), self.above[-1]),
            (move_z(-1, range(1, 5 - hop)), self.below[-1]),
        ]

    def take(self, arrived):
        self.above.append(arrived[0])
        self.below.append(arrived[1])

    def block(self, rel):
        z = place_z()
        above, below = self.above, self.below
        if rel == 0:
            return above[0]
        if rel == 1:
            return jnp.where(z % 2 == 1, above[1], below[1])
        if rel == 2:
            return jnp.where(z >= 2, above[2], below[2])
        return jnp.where(
            z == 0, below[3], jnp.where(z == 3, above[3], jnp.where(z == 1, below[1], above[1]))
        )


class ZSum:
    def __init__(self):
        self.last = None
        self.up = self.down = None

    def sends(self, rel, block):
        z = place_z()
        if rel == 3:
            self.last = block
            up, down = block, block
        elif rel == 2:
            up, down = block + self.up, block + self.down
        else:
            up = jnp.where(z == 1, self.last, block) + self.up
            down = jnp.where(z == 2, self.last, block) + self.down
        return [
            (move_z(1, range(0, 4 - rel)), low(up)),
            (move_z(-1, range(rel, 4)), low(down)),
        ]

    def take(self, arrived):
        self.up, self.down = arrived

    def total(self, block):
        return block + self.up + self.down


def early_slots(slots):
    return slots - slots * 13 // 36


def gather_tiles(own, early, place_early, place_late, else_low, targets):
    half = early // 2
    lanes = Lanes()
    line, late_line = ZLine(own[:early]), ZLine(own[early:])
    rest = None
    token = ()
    for rel in range(4):
        block = line.block(rel)
        sends = [(swap_x, block), (swap_y, block)]
        waits = token
        if rel == 2:
            waits += (flat,)
        elif rel == 3:
            waits += rest
        if rel < 3:
            by_x, by_y, *arrived = lanes.step(sends + line.sends(), *waits)
            line.take(arrived)
        else:
            by_x, by_y, *arrived = lanes.step(sends + late_line.sends(), *waits)
            late_line.take(arrived)
        sends = [(swap_y, by_x[:half]), (swap_x, by_y[half:])]
        if rel == 0:
            first, second, *arrived = lanes.step(
                sends + [(to_z(other), else_low.reshape(1, -1, 128)) for other in (1, 2, 3)],
                targets,
            )
            flat = gather_else(else_low, lanes, arrived)
            rest = cut_else(flat)
        elif rel == 1:
            first, second = lanes.step(sends)
        else:
            first, second, *arrived = lanes.step(sends + late_line.sends())
            late_line.take(arrived)
        at = 4 * rel * early
        group = [
            (block, at),
            (by_y, at + early),
            (by_x, at + 2 * early),
            (first, at + 3 * early),
            (second, at + 3 * early + half),
        ]
        token = (place_early(group),)
    line = jnp.concatenate([late_line.block(rel) for rel in range(4)], 0)
    count = line.shape[0]
    half = count // 2
    by_x, by_y = lanes.step([(swap_x, line), (swap_y, line)])
    token = place_late([(line, 0)])
    first, second = lanes.step([(swap_y, by_x[:half]), (swap_x, by_y[half:])], token)
    place_late([(by_y, count), (by_x, 2 * count)])
    place_late([(first, 3 * count), (second, 3 * count + half)])
    return rest


def relative(owner):
    rel_f = jnp.bitwise_xor(owner // 2, lax.axis_index("fsdp"))
    return rel_f // 2, rel_f % 2, jnp.bitwise_xor(owner % 2, lax.axis_index("ctx"))


def early_place(owner, slot, slots):
    rel_z, rel_x, rel_y = relative(owner)
    return ((rel_z * 2 + rel_x) * 2 + rel_y) * slots + slot


def late_place(owner, slot, slots):
    rel_z, rel_x, rel_y = relative(owner)
    return ((rel_x * 2 + rel_y) * 4 + rel_z) * slots + slot


def scatter_late(parts, slots, lanes):
    count = 4 * slots
    half = count // 2
    keep, to_y, to_x, both = (parts[part * count : (part + 1) * count] for part in range(4))
    by_y, by_x = lanes.step([(swap_y, both[:half]), (swap_x, both[half:])])
    to_x = jnp.concatenate([low(wide(to_x[:half]) + by_y), to_x[half:]], 0)
    to_y = jnp.concatenate([to_y[:half], low(wide(to_y[half:]) + by_x)], 0)
    from_x, from_y = lanes.step([(swap_x, to_x), (swap_y, to_y)])
    keep = wide(keep) + from_x + from_y
    return [keep[rel * slots : (rel + 1) * slots] for rel in range(4)]


def scatter_early(parts, slots, lanes, late, images_part):
    half = slots // 2

    def block(part, begin, end):
        return parts[part * slots + begin : part * slots + end]

    def diagonal(rel):
        return [
            (swap_y, block(4 * rel + 3, 0, half)),
            (swap_x, block(4 * rel + 3, half, slots)),
        ]

    def sides(rel, arrived):
        by_y, by_x = arrived
        return [
            (
                swap_x,
                jnp.concatenate(
                    [
                        low(wide(block(4 * rel + 2, 0, half)) + by_y),
                        block(4 * rel + 2, half, slots),
                    ],
                    0,
                ),
            ),
            (
                swap_y,
                jnp.concatenate(
                    [
                        block(4 * rel + 1, 0, half),
                        low(wide(block(4 * rel + 1, half, slots)) + by_x),
                    ],
                    0,
                ),
            ),
        ]

    def kept(rel, arrived):
        return wide(block(4 * rel, 0, slots)) + arrived[0] + arrived[1]

    line, late_line = ZSum(), ZSum()
    arrived = lanes.step(diagonal(3) + late_line.sends(3, late[3]))
    diagonal_3 = arrived[:2]
    late_line.take(arrived[2:])
    arrived = lanes.step(diagonal(2) + late_line.sends(2, late[2]))
    diagonal_2 = arrived[:2]
    late_line.take(arrived[2:])
    arrived = lanes.step(sides(3, diagonal_3) + late_line.sends(1, late[1]))
    late_line.take(arrived[2:])
    owned_late = late_line.total(late[0])
    kept_3 = kept(3, arrived)
    arrived = lanes.step(diagonal(1) + [(to_z(rel), images_part) for rel in (1, 2, 3)])
    diagonal_1 = arrived[:2]
    images = jnp.concatenate([images_part] + arrived[2:], 0)
    arrived = lanes.step(sides(2, diagonal_2) + line.sends(3, kept_3) + [(swap_y, images)])
    line.take(arrived[2:4])
    kept_2 = kept(2, arrived)
    images = jnp.concatenate([images, arrived[4]], 0)
    arrived = lanes.step(diagonal(0) + [(swap_x, images)])
    diagonal_0 = arrived[:2]
    images = jnp.concatenate([images, arrived[2]], 0)
    arrived = lanes.step(sides(1, diagonal_1) + line.sends(2, kept_2))
    line.take(arrived[2:4])
    arrived_0 = lanes.step(sides(0, diagonal_0) + line.sends(1, kept(1, arrived)))
    line.take(arrived_0[2:4])
    return line.total(kept(0, arrived_0)), owned_late, images


def gather_images(value):
    if not is_box():
        return lax.all_gather(value, ("fsdp", "ctx"), axis=0, tiled=True)
    value = jnp.concatenate([value] + [swap_f(value, 2 * rel) for rel in (1, 2, 3)], 0)
    by_x, by_y = swap_x(value), swap_y(value)
    return jnp.concatenate([value, by_y, by_x, swap_x(by_y)], 0)


def gather_else(flat, lanes, line):
    if not is_box():
        return lax.all_gather(flat, ("fsdp", "ctx", "tp"), axis=0, tiled=True)
    z, x = place_z(), lax.axis_index("fsdp") % 2
    y, core = lax.axis_index("ctx"), lax.axis_index("tp")
    own = flat.reshape(1, -1, 128)
    line = [own] + line
    line = [
        jnp.where(
            z == place,
            line[0],
            jnp.where(z == place ^ 1, line[1], jnp.where(z == place ^ 2, line[2], line[3])),
        )
        for place in range(4)
    ]
    line = jnp.concatenate(line, 0)
    by_x, by_y = lanes.step([(swap_x, line), (swap_y, line)])
    half = line.shape[1] // 2
    both = jnp.concatenate(lanes.step([(swap_y, by_x[:, :half]), (swap_x, by_y[:, half:])]), 1)
    y_low = [jnp.where(y == 0, line, by_y), jnp.where(y == 0, by_x, both)]
    y_high = [jnp.where(y == 0, by_y, line), jnp.where(y == 0, both, by_x)]
    chip = jnp.stack(
        [
            jnp.stack([jnp.where(x == 0, y_low[0], y_low[1]), jnp.where(x == 0, y_high[0], y_high[1])], 1),
            jnp.stack([jnp.where(x == 0, y_low[1], y_low[0]), jnp.where(x == 0, y_high[1], y_high[0])], 1),
        ],
        1,
    )
    other = swap_tp(chip)
    return jnp.stack(
        [jnp.where(core == 0, chip, other), jnp.where(core == 0, other, chip)], 3
    ).reshape(-1)


def cut_else(flat):
    rows = flat.reshape(-1, D)
    counts = [P_SIZE, NCLS, TFREQ, D, 2 * D, P_SIZE]
    ends = [sum(counts[: place + 1]) for place in range(6)]
    parts = [rows[end - count : end] for end, count in zip(ends, counts)]
    parts[4] = parts[4].reshape(D, 2 * D)
    parts[5] = parts[5].reshape(D, P_SIZE)
    return tuple(parts)


def total(value):
    if not is_box():
        return lax.psum(value, ("fsdp", "ctx", "tp"))
    value = value + swap_tp(value)
    value = value + swap_y(value)
    for bit in (1, 2, 4):
        value = value + swap_f(value, bit)
    return value


def tp_sum(value):
    if lax.axis_size("tp") == 2:
        return value + swap_tp(value)
    return lax.psum(value, "tp")


def columns_in(value):
    if lax.axis_size("tp") == 2:
        other = swap_tp(value)
        at_zero = lax.axis_index("tp") == 0
        return jnp.concatenate(
            [jnp.where(at_zero, value, other), jnp.where(at_zero, other, value)], -1
        )
    return lax.all_gather(value, "tp", axis=value.ndim - 1, tiled=True)


def rows_in(value_low):
    if lax.axis_size("tp") == 2:
        return [value_low, swap_tp(value_low)]
    return [lax.all_gather(value_low, "tp", axis=0, tiled=True)]


def each_half(work, row_sets):
    if len(row_sets) == 2:
        other = work(row_sets[1])
        sent = swap_tp(other[-1])
        own = work(row_sets[0])
        return [own[:-1], other[:-1]], [own[-1], sent]
    whole = work(row_sets[0])
    return [whole[:-1]], [lax.psum_scatter(whole[-1], "tp", scatter_dimension=0, tiled=True)]


BIG = 56 * 1024 * 1024


def against_value(left_op, right_op):
    return lax.dot_general(
        left_op, right_op, (((1,), (1,)), ((), ())), preferred_element_type=jnp.float32
    )


def untile_into(matrix, tile_set):
    rows, columns = matrix.shape[0] // B, matrix.shape[1] // B
    for row in range(rows):
        for column in range(columns):
            matrix[row * B : (row + 1) * B, column * B : (column + 1) * B] = tile_set[
                row * columns + column
            ]


def segments(tp_parts):
    found = []
    begin = 0
    for height, breadth in shard_shapes(tp_parts):
        amount = height * breadth // (B * B)
        found.append((amount, begin))
        begin += amount
    return found


def weight_spec(kind, tp_parts):
    amount, begin = segments(tp_parts)[kind]
    return pl.BlockSpec(
        (amount, B, B), lambda *step: (begin // amount, 0, 0), pipeline_mode=pl.Buffered(1)
    )


def rows_spec(rows, breadth):
    return pl.BlockSpec((rows, breadth), lambda step: (step, 0))


def shaped(rows, breadth, kind):
    return jax.ShapeDtypeStruct((rows, breadth), kind)


def params():
    return pltpu.CompilerParams(vmem_limit_bytes=BIG)


def attend_kernel(normed_in, qkv_tiles, proj_tiles, projected, attended, partial, w_qkv, w_proj):
    @pl.when(pl.program_id(0) == 0)
    def _():
        untile_into(w_qkv, qkv_tiles)
        untile_into(w_proj, proj_tiles)

    values = low(product(normed_in[...], w_qkv[...]))
    projected[...] = values
    width = values.shape[1] // 3
    results = []
    for head in range(width // HD):
        at = head * HD
        query = values[:, at : at + HD]
        key_rows = values[:, width + at : width + at + HD]
        value_rows = values[:, 2 * width + at : 2 * width + at + HD]
        scores = against_value(query, key_rows) * HD ** (-0.5)
        exponent = jnp.exp(scores - jnp.max(scores, -1, keepdims=True))
        probabilities = low(exponent / jnp.sum(exponent, -1, keepdims=True))
        results.append(low(product(probabilities, value_rows)))
    result = jnp.concatenate(results, 1)
    attended[...] = result
    partial[...] = product(result, w_proj[...])


def attend_call(normed_in, store, tp_parts, local_len):
    rows = normed_in.shape[0]
    width = D // tp_parts
    return pl.pallas_call(
        attend_kernel,
        grid=(rows // local_len,),
        in_specs=[
            rows_spec(local_len, D),
            weight_spec(0, tp_parts),
            weight_spec(1, tp_parts),
        ],
        out_specs=[
            rows_spec(local_len, 3 * width),
            rows_spec(local_len, width),
            rows_spec(local_len, D),
        ],
        out_shape=[
            shaped(rows, 3 * width, jnp.bfloat16),
            shaped(rows, width, jnp.bfloat16),
            shaped(rows, D, jnp.float32),
        ],
        scratch_shapes=[
            pltpu.VMEM((D, 3 * width), jnp.bfloat16),
            pltpu.VMEM((width, D), jnp.bfloat16),
        ],
        compiler_params=params(),
        cost_estimate=pl.CostEstimate(
            flops=rows * D * width * 8, bytes_accessed=rows * D * 8, transcendentals=rows * 2048
        ),
    )(normed_in, store, store)


def attend_back_kernel(
    grad_branch, projected, qkv_tiles, proj_tiles, grad_qkv, partial, w_qkv, w_proj
):
    @pl.when(pl.program_id(0) == 0)
    def _():
        untile_into(w_qkv, qkv_tiles)
        untile_into(w_proj, proj_tiles)

    grad_attended = low(against_value(grad_branch[...], w_proj[...]))
    values = projected[...]
    width = values.shape[1] // 3
    grads = [[], [], []]
    for head in range(width // HD):
        at = head * HD
        query = values[:, at : at + HD]
        key_rows = values[:, width + at : width + at + HD]
        value_rows = values[:, 2 * width + at : 2 * width + at + HD]
        grad_here = grad_attended[:, at : at + HD]
        scores = against_value(query, key_rows) * HD ** (-0.5)
        exponent = jnp.exp(scores - jnp.max(scores, -1, keepdims=True))
        probabilities = exponent / jnp.sum(exponent, -1, keepdims=True)
        grad_prob = against_value(grad_here, value_rows)
        grad_scores = low(
            probabilities
            * (grad_prob - jnp.sum(probabilities * grad_prob, -1, keepdims=True))
        )
        grads[0].append(low(product(grad_scores, key_rows) * HD ** (-0.5)))
        grads[1].append(low(over_rows(grad_scores, query) * HD ** (-0.5)))
        grads[2].append(low(over_rows(low(probabilities), grad_here)))
    result = jnp.concatenate(grads[0] + grads[1] + grads[2], 1)
    grad_qkv[...] = result
    partial[...] = against_value(result, w_qkv[...])


def attend_back_call(grad_branch, projected, store, tp_parts, local_len):
    rows = grad_branch.shape[0]
    width = D // tp_parts
    return pl.pallas_call(
        attend_back_kernel,
        grid=(rows // local_len,),
        in_specs=[
            rows_spec(local_len, D),
            rows_spec(local_len, 3 * width),
            weight_spec(0, tp_parts),
            weight_spec(1, tp_parts),
        ],
        out_specs=[rows_spec(local_len, 3 * width), rows_spec(local_len, D)],
        out_shape=[shaped(rows, 3 * width, jnp.bfloat16), shaped(rows, D, jnp.float32)],
        scratch_shapes=[
            pltpu.VMEM((D, 3 * width), jnp.bfloat16),
            pltpu.VMEM((width, D), jnp.bfloat16),
        ],
        compiler_params=params(),
        cost_estimate=pl.CostEstimate(
            flops=rows * D * width * 10, bytes_accessed=rows * D * 8, transcendentals=rows * 2048
        ),
    )(grad_branch, projected, store, store)


def mlp_kernel(normed_mid, up_tiles, down_tiles, hidden, partial, w_up, w_down):
    @pl.when(pl.program_id(0) == 0)
    def _():
        untile_into(w_up, up_tiles)
        untile_into(w_down, down_tiles)

    values = product(normed_mid[...], w_up[...])
    hidden[...] = values
    partial[...] = product(low(gelu_tanh(values)), w_down[...])


def mlp_call(normed_mid, store, tp_parts, local_len):
    rows = normed_mid.shape[0]
    width = F // tp_parts
    return pl.pallas_call(
        mlp_kernel,
        grid=(rows // local_len,),
        in_specs=[
            rows_spec(local_len, D),
            weight_spec(2, tp_parts),
            weight_spec(3, tp_parts),
        ],
        out_specs=[rows_spec(local_len, width), rows_spec(local_len, D)],
        out_shape=[shaped(rows, width, jnp.float32), shaped(rows, D, jnp.float32)],
        scratch_shapes=[
            pltpu.VMEM((D, width), jnp.bfloat16),
            pltpu.VMEM((width, D), jnp.bfloat16),
        ],
        compiler_params=params(),
        cost_estimate=pl.CostEstimate(
            flops=rows * D * width * 4,
            bytes_accessed=rows * D * 12 + 4 * D * width,
            transcendentals=rows * width,
        ),
    )(normed_mid, store, store)


def mlp_back_kernel(
    grad_mlp, hidden, up_tiles, down_tiles, activation, grad_hidden, partial, w_up, w_down
):
    @pl.when(pl.program_id(0) == 0)
    def _():
        untile_into(w_up, up_tiles)
        untile_into(w_down, down_tiles)

    values = hidden[...]
    factor = math.sqrt(2.0 / math.pi)
    square = values * values
    bent = jnp.tanh(factor * (values + 0.044715 * (square * values)))
    half_up = 0.5 * (1.0 + bent)
    activation[...] = low(values * half_up)
    slope = half_up + 0.5 * values * (1.0 - bent * bent) * (
        factor * (1.0 + 3.0 * 0.044715 * square)
    )
    grad = low(against_value(grad_mlp[...], w_down[...]) * slope)
    grad_hidden[...] = grad
    partial[...] = against_value(grad, w_up[...])


def mlp_back_call(grad_mlp, hidden, store, tp_parts, local_len):
    rows = grad_mlp.shape[0]
    width = F // tp_parts
    return pl.pallas_call(
        mlp_back_kernel,
        grid=(rows // local_len,),
        in_specs=[
            rows_spec(local_len, D),
            rows_spec(local_len, width),
            weight_spec(2, tp_parts),
            weight_spec(3, tp_parts),
        ],
        out_specs=[
            rows_spec(local_len, width),
            rows_spec(local_len, width),
            rows_spec(local_len, D),
        ],
        out_shape=[
            shaped(rows, width, jnp.bfloat16),
            shaped(rows, width, jnp.bfloat16),
            shaped(rows, D, jnp.float32),
        ],
        scratch_shapes=[
            pltpu.VMEM((D, width), jnp.bfloat16),
            pltpu.VMEM((width, D), jnp.bfloat16),
        ],
        compiler_params=params(),
        cost_estimate=pl.CostEstimate(
            flops=rows * D * width * 4,
            bytes_accessed=rows * D * 16 + 4 * D * width,
            transcendentals=rows * width,
        ),
    )(grad_mlp, hidden, store, store)


def modes_call(cond_act, store, tp_parts):
    rows = cond_act.shape[0]
    width = 6 * D // tp_parts

    def kernel(left, tile_set, out):
        for column in range(width // B):
            total_here = 0.0
            for row in range(D // B):
                total_here = total_here + product(
                    left[:, row * B : (row + 1) * B], tile_set[row * (width // B) + column]
                )
            out[:, column * B : (column + 1) * B] = total_here

    return pl.pallas_call(
        kernel,
        grid=(1,),
        in_specs=[rows_spec(rows, D), weight_spec(4, tp_parts)],
        out_specs=rows_spec(rows, width),
        out_shape=shaped(rows, width, jnp.float32),
        compiler_params=params(),
    )(cond_act, store)


def three_parts(value):
    first = low(value)
    rest = value - wide(first)
    second = low(rest)
    return jnp.concatenate([first, second, low(rest - wide(second))], 0)


def against_low(value, weight):
    rows = value.shape[0]
    summed = against(three_parts(value), weight)
    return summed[:rows] + summed[rows : 2 * rows] + summed[2 * rows :]


def modes_back_call(grads, store, tp_parts):
    rows = grads.shape[0]
    width = 6 * D // tp_parts
    parts = three_parts(grads)

    def kernel(left, tile_set, out):
        for row in range(D // B):
            total_here = 0.0
            for column in range(width // B):
                total_here = total_here + against_value(
                    left[:, column * B : (column + 1) * B],
                    tile_set[row * (width // B) + column],
                )
            out[:, row * B : (row + 1) * B] = total_here

    summed = pl.pallas_call(
        kernel,
        grid=(1,),
        in_specs=[rows_spec(3 * rows, width), weight_spec(4, tp_parts)],
        out_specs=rows_spec(3 * rows, D),
        out_shape=shaped(3 * rows, D, jnp.float32),
        compiler_params=params(),
    )(parts, store)
    return summed[:rows] + summed[rows : 2 * rows] + summed[2 * rows :]


def weight_grad_call(lefts, rights, places, first_tile, held):
    height, breadth = lefts[0].shape[1], rights[0].shape[1]
    width = 512 if breadth % 512 == 0 else breadth
    steps = breadth // width
    count = len(lefts)
    row_tiles, column_tiles, all_columns = height // B, width // B, breadth // B
    amount = row_tiles * column_tiles
    given = [array for _, _, array in held if array is not None]

    def kernel(place, *refs):
        left_refs, right_refs = refs[:count], refs[count : 2 * count]
        outs = refs[2 * count + len(given) : 2 * count + len(given) + len(held)]
        turned, ready, sem = refs[-2 - count : -2], refs[-2], refs[-1]
        step = pl.program_id(0)
        slot = lax.rem(step, 2)

        @pl.when(step == 0)
        def _():
            for turned_here, left in zip(turned, left_refs):
                turned_here[...] = left[...].T

        def drain(which):
            pltpu.make_async_copy(
                ready.at[which], outs[0].at[pl.ds(0, amount)], sem.at[which]
            ).wait()

        @pl.when(step >= 2)
        def _():
            drain(slot)

        block = product(turned[0][...], right_refs[0][...])
        for turned_here, right in zip(turned[1:], right_refs[1:]):
            block = block + product(turned_here[...], right[...])
        block = low(block)
        for row in range(row_tiles):
            for column in range(column_tiles):
                ready[slot, row * column_tiles + column] = block[
                    row * B : (row + 1) * B, column * B : (column + 1) * B
                ]

        def send(index, carry):
            row, column = index // column_tiles, index % column_tiles
            where_to = place[first_tile + row * all_columns + step * column_tiles + column]
            for number, (begin, _, _) in enumerate(held):
                end = held[number + 1][0] if number + 1 < len(held) else 1 << 30
                copy = pltpu.make_async_copy(
                    ready.at[slot, index], outs[number].at[where_to - begin], sem.at[slot]
                )
                if len(held) == 1:
                    copy.start()
                else:
                    pl.when((where_to >= begin) & (where_to < end))(copy.start)
            return carry

        lax.fori_loop(0, amount, send, 0)

        @pl.when(step == steps - 1)
        def _():
            drain(slot)
            if steps > 1:
                drain(1 - slot)

    rows = [left.shape[0] for left in lefts]
    anywhere = pl.BlockSpec(memory_space=pl.ANY)
    in_specs = [
        pl.BlockSpec((size, height), lambda step, place: (0, 0), pipeline_mode=pl.Buffered(1))
        for size in rows
    ] + [pl.BlockSpec((size, width), lambda step, place: (0, step)) for size in rows]
    in_specs += [anywhere] * len(given)
    operands = [places, *lefts, *rights, *given]
    aliases = {}
    for number, (_, _, array) in enumerate(held):
        if array is not None:
            aliases[1 + 2 * count + len(aliases)] = number
    results = pl.pallas_call(
        kernel,
        grid_spec=pltpu.PrefetchScalarGridSpec(
            num_scalar_prefetch=1,
            grid=(steps,),
            in_specs=in_specs,
            out_specs=[anywhere] * len(held),
            scratch_shapes=[pltpu.VMEM((height, size), jnp.bfloat16) for size in rows]
            + [pltpu.VMEM((2, amount, B, B), jnp.bfloat16), pltpu.SemaphoreType.DMA((2,))],
        ),
        out_shape=[
            jax.ShapeDtypeStruct((places_here, B, B), jnp.bfloat16) for _, places_here, _ in held
        ],
        input_output_aliases=aliases,
        compiler_params=params(),
        cost_estimate=pl.CostEstimate(
            flops=2 * sum(rows) * height * breadth,
            bytes_accessed=2 * (sum(rows) * (height + breadth) + height * breadth),
            transcendentals=0,
        ),
    )(*operands)
    return [
        (begin, places_here, array) for (begin, places_here, _), array in zip(held, results)
    ]


def place_call(pieces, targets, held):
    count = len(pieces)
    given = [array for _, _, array in held if array is not None]

    def kernel(target, *refs):
        outs = refs[count + len(given) : count + len(given) + len(held)]
        token = refs[count + len(given) + len(held)]
        buffers, loaded, stored = refs[-2 - count : -2], refs[-2], refs[-1]
        token[...] = jnp.zeros_like(token)
        for number in range(count):
            pltpu.make_async_copy(refs[number], buffers[number], loaded.at[number]).start()
        for number, (piece, begin) in enumerate(pieces):
            pltpu.make_async_copy(refs[number], buffers[number], loaded.at[number]).wait()

            def send(index, carry):
                where_to = target[begin + index]
                left = True
                for out_number, (first, amount, _) in enumerate(held):
                    last = out_number == len(held) - 1
                    inside = (where_to >= first) & (where_to < first + amount - 1)
                    at = where_to - first
                    if last:
                        at = jnp.where(inside, at, amount - 1)
                        inside = left
                    else:
                        left = jnp.logical_not(inside)
                    copy = pltpu.make_async_copy(
                        buffers[number].at[index], outs[out_number].at[at], stored.at[number]
                    )
                    if len(held) == 1:
                        copy.start()
                    else:
                        pl.when(inside)(copy.start)
                return carry

            lax.fori_loop(0, piece.shape[0], send, 0)
        for number, (piece, begin) in enumerate(pieces):
            pltpu.make_async_copy(
                buffers[number], outs[0].at[pl.ds(0, piece.shape[0])], stored.at[number]
            ).wait()

    anywhere = pl.BlockSpec(memory_space=pl.ANY)
    operands = [targets] + [piece for piece, _ in pieces] + given
    aliases = {}
    for number, (_, _, array) in enumerate(held):
        if array is not None:
            aliases[1 + count + len(aliases)] = number
    results = pl.pallas_call(
        kernel,
        grid_spec=pltpu.PrefetchScalarGridSpec(
            num_scalar_prefetch=1,
            grid=(1,),
            in_specs=[anywhere] * (len(operands) - 1),
            out_specs=[anywhere] * len(held) + [pl.BlockSpec((8, B), lambda step, target: (0, 0))],
            scratch_shapes=[pltpu.VMEM(piece.shape, jnp.bfloat16) for piece, _ in pieces]
            + [pltpu.SemaphoreType.DMA((count,))] * 2,
        ),
        out_shape=[jax.ShapeDtypeStruct((amount, B, B), jnp.bfloat16) for _, amount, _ in held]
        + [jax.ShapeDtypeStruct((8, B), jnp.float32)],
        input_output_aliases=aliases,
        compiler_params=params(),
        cost_estimate=pl.CostEstimate(
            flops=0,
            bytes_accessed=sum(4 * piece.shape[0] * B * B for piece, _ in pieces),
            transcendentals=0,
        ),
    )(*operands)
    return [(first, amount, array) for (first, amount, _), array in zip(held, results)], results[-1]


def chips_sum(value):
    for swap in (swap_y, swap_x, lambda part: swap_f(part, 2), lambda part: swap_f(part, 4)):
        value = value + swap(value)
    return value


LOT = 16


def lots(count):
    return (count + LOT - 1) // LOT


def bring_strays(store, strays, count, owned_tiles, ordering, slots, me):
    def body(state):
        lot, held = state
        tiles = lax.dynamic_slice_in_dim(strays, lot * LOT, LOT, 0)
        valid = lot * LOT + jnp.arange(LOT) < count
        here = ordering[tiles]
        mine = valid & (here // slots == me)
        sent = jnp.where(mine[:, None, None], owned_tiles[here % slots], 0)
        sent = chips_sum(sent)
        at = jnp.where(valid, tiles, held.shape[0])
        return lot + 1, held.at[at].set(sent, mode="drop")

    return lax.while_loop(lambda state: state[0] < lots(count), body, (0, store))[1]


def sum_strays(owned, parts, strays, count, ordering, slots, me):
    def body(state):
        lot, held = state
        tiles = lax.dynamic_slice_in_dim(strays, lot * LOT, LOT, 0)
        valid = lot * LOT + jnp.arange(LOT) < count
        summed = chips_sum(wide(lax.dynamic_slice_in_dim(parts, lot * LOT, LOT, 0)))
        here = ordering[tiles]
        at = jnp.where(valid & (here // slots == me), here % slots, slots)
        return lot + 1, held.at[at].set(summed, mode="drop")

    return lax.while_loop(lambda state: state[0] < lots(count), body, (0, owned))[1]


def normed_value(stream):
    centred = stream - jnp.mean(stream, -1, keepdims=True)
    rate = lax.rsqrt(jnp.mean(centred * centred, -1, keepdims=True) + EPS_NORM)
    return centred * rate, rate


def rows_kernel_call(kernel, wide_ins, mode_ins, outs):
    own, group = wide_ins[0].shape[:2]
    rows = pl.BlockSpec((1, group, D), lambda step: (step, 0, 0))
    few = lambda count: pl.BlockSpec((1, count, D), lambda step: (step, 0, 0))
    return pl.pallas_call(
        kernel,
        grid=(own,),
        in_specs=[rows] * len(wide_ins) + [few(modes.shape[1]) for modes in mode_ins],
        out_specs=[rows if count is None else few(count) for count, _ in outs],
        out_shape=[
            jax.ShapeDtypeStruct((own, group if count is None else count, D), kind)
            for count, kind in outs
        ],
        compiler_params=params(),
        cost_estimate=pl.CostEstimate(
            flops=own * group * D * 20,
            bytes_accessed=own * group * D * 4 * (len(wide_ins) + len(outs)),
            transcendentals=own * group,
        ),
    )(*wide_ins, *mode_ins)


def modulate_call(stream, modes, shift, scale):
    def kernel(values, mode, out):
        out[0] = low(
            normed_value(values[0])[0] * (1.0 + mode[0, scale : scale + 1, :])
            + mode[0, shift : shift + 1, :]
        )

    return rows_kernel_call(kernel, [stream], [modes], [(None, jnp.bfloat16)])[0]


def residual_call(stream, terms, modes, gate, next_modes, shift, scale):
    def kernel(*refs):
        values, term_refs = refs[0], refs[1 : 1 + len(terms)]
        mode, mode_next, branch, stream_new, out = refs[1 + len(terms) :]
        summed = term_refs[0][0]
        for term in term_refs[1:]:
            summed = summed + term[0]
        branch[0] = summed
        result = values[0] + mode[0, gate : gate + 1, :] * summed
        stream_new[0] = result
        out[0] = low(
            normed_value(result)[0] * (1.0 + mode_next[0, scale : scale + 1, :])
            + mode_next[0, shift : shift + 1, :]
        )

    shape = stream.shape
    return rows_kernel_call(
        kernel,
        [stream] + [term.reshape(shape) for term in terms],
        [modes, next_modes],
        [(None, jnp.float32), (None, jnp.float32), (None, jnp.bfloat16)],
    )


def back_call(stream, terms, upstream, modes, scale, below):
    shape = stream.shape
    wide_ins = [stream] + [term.reshape(shape) for term in terms]
    if upstream is not None:
        wide_ins.append(upstream)
    mode_ins = [modes]
    outs = [(None, jnp.float32), (3 if below else 2, jnp.float32)]
    if below:
        branch, branch_modes, gate = below
        wide_ins.append(branch)
        mode_ins.append(branch_modes)
        outs.append((None, jnp.bfloat16))

    def kernel(*refs):
        ins, modes_in = refs[: len(wide_ins)], refs[len(wide_ins) : len(wide_ins) + len(mode_ins)]
        results = refs[len(wide_ins) + len(mode_ins) :]
        grad = ins[1][0]
        for term in ins[2 : 1 + len(terms)]:
            grad = grad + term[0]
        normal, rate = normed_value(ins[0][0])
        results[1][0, 0:1, :] = jnp.sum(grad, 0, keepdims=True)
        results[1][0, 1:2, :] = jnp.sum(grad * normal, 0, keepdims=True)
        grad = grad * (1.0 + modes_in[0][0, scale : scale + 1, :])
        grad = rate * (
            grad
            - jnp.mean(grad, -1, keepdims=True)
            - normal * jnp.mean(grad * normal, -1, keepdims=True)
        )
        if upstream is not None:
            grad = grad + ins[1 + len(terms)][0]
        results[0][0] = grad
        if below:
            results[1][0, 2:3, :] = jnp.sum(grad * ins[-1][0], 0, keepdims=True)
            results[2][0] = low(modes_in[1][0, gate : gate + 1, :] * grad)

    return rows_kernel_call(kernel, wide_ins, mode_ins, outs)


def update_kernel(clip, grad, master, first, second, bases, master_out, first_out, second_out, low_out):
    eye = lax.broadcasted_iota(jnp.int32, (B, B), 0) == lax.broadcasted_iota(jnp.int32, (B, B), 1)
    for tile in range(grad.shape[0]):
        left_row = bases[tile, 0:1, :]
        right_row = bases[tile, 1:2, :]
        left_col = jnp.sum(jnp.where(eye, left_row, 0.0), 1, keepdims=True)
        left_rate = 2.0 / jnp.sum(left_row * left_row, 1, keepdims=True)
        right_rate = 2.0 / jnp.sum(right_row * right_row, 1, keepdims=True)
        left_scaled = left_col * left_rate
        right_scaled = right_row * right_rate

        def turn(middle):
            middle = middle - left_scaled * jnp.sum(left_col * middle, 0, keepdims=True)
            return middle - jnp.sum(middle * right_row, 1, keepdims=True) * right_scaled

        turned = turn(clip[0, 0] * grad[tile])
        first_new = 0.5 * first[tile] + 0.5 * turned
        second_new = 0.5 * second[tile] + 0.5 * turned * turned
        direction = first_new / (jnp.sqrt(second_new) + 1e-08)
        master_new = master[tile] - RATE * turn(direction)
        master_out[tile] = master_new
        first_out[tile] = first_new
        second_out[tile] = second_new
        low_out[tile] = master_new.astype(jnp.bfloat16)


def update_tiles(clip_factor, grad, master, first, second, bases):
    slots = grad.shape[0]
    amount = 3
    tile_spec = pl.BlockSpec((amount, B, B), lambda step: (step, 0, 0))
    whole = jax.ShapeDtypeStruct(grad.shape, jnp.float32)
    return pl.pallas_call(
        update_kernel,
        grid=(slots // amount,),
        in_specs=[pl.BlockSpec(memory_space=pltpu.SMEM)]
        + [tile_spec] * 4
        + [pl.BlockSpec((amount, 2, B), lambda step: (step, 0, 0))],
        out_specs=[tile_spec] * 4,
        out_shape=[whole, whole, whole, jax.ShapeDtypeStruct(grad.shape, jnp.bfloat16)],
        compiler_params=params(),
        cost_estimate=pl.CostEstimate(
            flops=slots * B * B * 30, bytes_accessed=slots * B * B * 30, transcendentals=slots * B * B
        ),
    )(clip_factor.reshape(1, 1), grad, master, first, second, bases)


def on_device(
    latents,
    noise,
    timesteps,
    labels,
    owners,
    tiles_low,
    tiles_master,
    tiles_first,
    tiles_second,
    bases,
    else_low,
    else_master,
    else_first,
    else_second,
):
    box = is_box()
    tp_parts = lax.axis_size("tp")
    tp_index = lax.axis_index("tp")
    ctx_parts = lax.axis_size("ctx")
    fsdp_parts = lax.axis_size("fsdp")
    images = latents.shape[0]
    local_len = latents.shape[1]
    slots = tiles_low.shape[1]
    sp_rows = images * local_len // tp_parts
    first_row = tp_index * sp_rows
    own = max(1, sp_rows // local_len)
    group = sp_rows // own
    first_image = first_row // local_len
    element_count = images * fsdp_parts * ctx_parts * local_len * P_SIZE
    ordering = jnp.argsort(owners, stable=True)
    inverse = jnp.argsort(ordering)
    all_tiles = inverse.shape[0]
    per_layer = all_tiles // L
    if box:
        early = early_slots(slots)
        me = lax.axis_index("fsdp") * ctx_parts + lax.axis_index("ctx")
        tile = jnp.arange(all_tiles, dtype=jnp.int32)
        owner, slot = inverse // slots, inverse % slots
        is_early = slot < early
        place_early = early_place(owner, slot, early)
        place_late = late_place(owner, slot - early, slots - early)
        gather_places = jnp.where(is_early, place_early, 16 * early + place_late)
        targets = jnp.argsort(gather_places).astype(jnp.int32)
        is_stray = jnp.logical_not(is_early) & (tile < per_layer)
        stray_count = jnp.sum(is_stray.astype(jnp.int32))
        stray_rank = jnp.cumsum(is_stray.astype(jnp.int32)) - 1
        room = 16 * (slots - early)
        strays = jnp.argsort(jnp.where(is_stray, tile, all_tiles + tile)).astype(jnp.int32)
        strays = jnp.concatenate([strays, jnp.zeros((LOT,), jnp.int32)])
        places = jnp.where(
            is_stray,
            room + 16 * (early + 1) + stray_rank,
            jnp.where(is_early, room + early_place(owner, slot, early + 1), place_late),
        ).astype(jnp.int32)
        stores = [(0, per_layer + 1, None), (per_layer, per_layer + 1, None)]
        late_store = None

        def place_early_tiles(tile_group):
            nonlocal stores
            stores, token = place_call(tile_group, targets, stores)
            return token

        def place_late_tiles(tile_group):
            nonlocal late_store
            tile_group = [(piece, 16 * early + at) for piece, at in tile_group]
            if late_store is None:
                late_store = [stores[1]]
            late_store, token = place_call(tile_group, targets, late_store)
            return token

        late_store = None
        else_parts = gather_tiles(
            tiles_low[0], early, place_early_tiles, place_late_tiles, else_low, targets
        )
        store = [
            bring_strays(stores[0][2], strays, stray_count, tiles_low[0], inverse, slots, me),
            late_store[0][2],
        ]
        held = [(0, room, None), (room, 16 * (slots + 1) + LOT, None)]
    else:
        places = jnp.arange(all_tiles, dtype=jnp.int32)
        gathered = lax.all_gather(tiles_low, ("fsdp", "ctx"), axis=1, tiled=True)[0][inverse]
        store = [gathered[:per_layer], gathered[per_layer:]]
        held = [(0, all_tiles, None)]
        else_parts = cut_else(gather_else(else_low, None, None))
    patch_weight, class_table, time_first, time_second, final_weight, head_weight = else_parts
    features_low = low(time_features(timesteps))
    onehot = low(labels[:, None] == jnp.arange(NCLS)[None, :])
    time_hidden = product(features_low, time_first)
    time_act = low(jax.nn.silu(time_hidden))
    condition = product(time_act, time_second) + product(onehot, class_table)
    cond_act = low(jax.nn.silu(condition))
    modes = [
        lax.dynamic_slice_in_dim(
            columns_in(modes_call(cond_act, store[layer_no], tp_parts)), first_image, own, 0
        ).reshape(own, 6, D)
        for layer_no in range(L)
    ]
    final_modes = lax.dynamic_slice_in_dim(
        product(cond_act, final_weight), first_image, own, 0
    ).reshape(own, 2, D)
    row_index = first_row + jnp.arange(sp_rows)
    signal = signal_level(timesteps)
    noisy_input = (
        jnp.sqrt(signal)[:, None, None] * latents + jnp.sqrt(1.0 - signal)[:, None, None] * noise
    )
    noisy_rows = low(
        lax.dynamic_slice_in_dim(
            noisy_input.reshape(images * local_len, P_SIZE), first_row, sp_rows, 0
        )
    )
    target = lax.dynamic_slice_in_dim(
        noise.reshape(images * local_len, P_SIZE), first_row, sp_rows, 0
    )
    stream = (product(noisy_rows, patch_weight) + position_table(row_index % local_len)).reshape(
        own, group, D
    )
    normed_in = modulate_call(stream, modes[0], 0, 1)
    kept = []
    for layer_no in range(L):
        row_sets = rows_in(normed_in.reshape(sp_rows, D))
        halves, terms = each_half(
            lambda rows: attend_call(rows, store[layer_no], tp_parts, local_len), row_sets
        )
        branch, middle, normed_mid = residual_call(
            stream, terms, modes[layer_no], 2, modes[layer_no], 3, 4
        )
        mid_sets = rows_in(normed_mid.reshape(sp_rows, D))
        hidden, terms = each_half(
            lambda rows: mlp_call(rows, store[layer_no], tp_parts, local_len), mid_sets
        )
        last = layer_no == L - 1
        mlp_out, stream_new, normed_in = residual_call(
            middle,
            terms,
            modes[layer_no],
            5,
            final_modes if last else modes[layer_no + 1],
            0,
            1,
        )
        kept.append((stream, row_sets, halves, branch, middle, mid_sets, hidden, mlp_out))
        stream = stream_new
    head_low = normed_in.reshape(sp_rows, D)
    mismatch = product(head_low, head_weight) - target
    loss_part = jnp.sum(mismatch * mismatch) / element_count
    grad_pred = low(2.0 * mismatch / element_count)
    grad_head = over_rows(grad_pred, head_low)
    upstream, final_sums, grad_low = back_call(
        stream,
        [against(grad_pred, head_weight)],
        None,
        final_modes,
        1,
        (kept[-1][7], modes[-1], 5),
    )
    grad_final = final_sums[:, :2].reshape(own, 2 * D)
    gate_sum = final_sums[:, 2:]
    starts = [begin for _, begin in segments(tp_parts)]
    mode_width = 6 * D // tp_parts
    fill = (-3 * images) % 16
    conds = jnp.pad(jnp.concatenate([cond_act] * 3, 0), ((0, fill), (0, 0)))

    def all_images(values):
        return tp_sum(
            lax.dynamic_update_slice_in_dim(
                jnp.zeros((images, values.shape[1]), jnp.float32), values, first_image, 0
            )
        )

    grad_final = all_images(grad_final)
    cond_wide = wide(cond_act)

    def image_part(columns):
        packed = jnp.concatenate(columns, 1)
        packed = jnp.pad(packed, ((0, 0), (0, -packed.shape[1] % 256)))
        part = packed.shape[1] // 2
        return lax.dynamic_slice_in_dim(packed, tp_index * part, part, 1)

    def every_image(columns):
        if not box:
            return gather_images(jnp.concatenate(columns, 1))
        return columns_in(gather_images(image_part(columns)))

    label_column = jnp.broadcast_to(wide(labels)[:, None], (images, 128))
    cuts = [128]
    for length in (TFREQ, D, D):
        cuts.append(cuts[-1] + length)
    early_images = every_image(
        [label_column, wide(features_low), wide(time_act), cond_wide, grad_final]
    )
    all_labels, all_features, all_time, all_cond, all_final = jnp.split(early_images, cuts, 1)
    all_final = all_final[:, : 2 * D]
    head_rows = total(grad_head).T.reshape(P_SIZE, D)
    grad_cond_act = 0.0
    for layer_no in reversed(range(L)):
        stream, row_sets, halves, branch, middle, mid_sets, hidden, mlp_out = kept[layer_no]
        base = layer_no * per_layer
        grad_sets = rows_in(grad_low.reshape(sp_rows, D))
        results, terms = each_half(
            lambda pair: mlp_back_call(pair[0], pair[1], store[layer_no], tp_parts, local_len),
            [(rows, hidden_here[0]) for rows, hidden_here in zip(grad_sets, hidden)],
        )
        held = weight_grad_call(
            [result[0] for result in results], grad_sets, places, base + starts[3], held
        )
        held = weight_grad_call(
            mid_sets, [result[1] for result in results], places, base + starts[2], held
        )
        upstream, mlp_sums, grad_low = back_call(
            middle, terms, upstream, modes[layer_no], 4, (branch, modes[layer_no], 2)
        )
        grad_sets = rows_in(grad_low.reshape(sp_rows, D))
        results, terms = each_half(
            lambda pair: attend_back_call(pair[0], pair[1], store[layer_no], tp_parts, local_len),
            [(rows, half[0]) for rows, half in zip(grad_sets, halves)],
        )
        held = weight_grad_call(
            [half[1] for half in halves], grad_sets, places, base + starts[1], held
        )
        held = weight_grad_call(
            row_sets, [result[0] for result in results], places, base + starts[0], held
        )
        below = None if layer_no == 0 else (kept[layer_no - 1][7], modes[layer_no - 1], 5)
        found = back_call(stream, terms, upstream, modes[layer_no], 1, below)
        grad_modes = jnp.concatenate(
            [found[1][:, :2], mlp_sums[:, 2:], mlp_sums[:, :2], gate_sum], 1
        ).reshape(own, 6 * D)
        mode_image = lax.dynamic_slice_in_dim(
            all_images(grad_modes), tp_index * mode_width, mode_width, 1
        )
        held = weight_grad_call(
            [conds],
            [jnp.pad(three_parts(mode_image), ((0, fill), (0, 0)))],
            places,
            base + starts[4],
            held,
        )
        grad_cond_act = grad_cond_act + modes_back_call(mode_image, store[layer_no], tp_parts)
        upstream = found[0]
        if below:
            grad_low, gate_sum = found[2], found[1][:, 2:]
        if box and layer_no == L - 1:
            grad_low = after(grad_low, held[0][2], held[1][2], early_images, head_rows)
            lanes = Lanes()
            late_sums = scatter_late(held[0][2], slots - early, lanes)
            held = held[1:]
    grad_patch = over_rows(noisy_rows, low(upstream).reshape(sp_rows, D))
    grad_cond_act = tp_sum(grad_cond_act) + against_low(grad_final, final_weight)
    grad_condition = jax.vjp(jax.nn.silu, condition)[1](grad_cond_act)[0]
    grad_time_hidden = jax.vjp(jax.nn.silu, time_hidden)[1](
        against_low(grad_condition, time_second)
    )[0]
    if box:
        patch_sum = tp_sum(grad_patch)
        patch_first = low(patch_sum)
        patch_part = jnp.where(tp_index == 0, patch_first, low(patch_sum - wide(patch_first)))
        parts = lax.dynamic_update_slice_in_dim(
            held[0][2],
            patch_part.reshape(1, B, B),
            early_place(0, early, early + 1),
            0,
        )
        owned, owned_late, images_rows = scatter_early(
            parts, early + 1, lanes, late_sums, image_part([grad_time_hidden, grad_condition])
        )
        late_images = columns_in(images_rows)
        patch_rows = tp_sum(owned[early]).reshape(P_SIZE, D)
        owned = jnp.concatenate([owned[:early], owned_late], 0)
        owned = sum_strays(
            owned, parts[16 * (early + 1) :], strays, stray_count, inverse, slots, me
        )
    else:
        owned = lax.psum_scatter(
            wide(held[0][2])[ordering], ("fsdp", "ctx"), scatter_dimension=0, tiled=True
        )
        patch_rows = lax.psum(grad_patch, ("fsdp", "ctx", "tp"))
        late_images = every_image([grad_time_hidden, grad_condition])
    all_hidden, all_condition = jnp.split(late_images, 2, 1)
    all_onehot = wide(all_labels[:, :1] == jnp.arange(NCLS, dtype=jnp.float32)[None, :])
    share = else_low.shape[0]
    device = (lax.axis_index("fsdp") * ctx_parts + lax.axis_index("ctx")) * tp_parts + tp_index
    begin = device * share
    row_total = else_low.shape[0] * fsdp_parts * ctx_parts * tp_parts // D
    row_count = min(share // D + 2, row_total)
    begin_row = jnp.minimum(begin // D, row_total - row_count)
    row_ids = begin_row + jnp.arange(row_count)
    edge = jnp.zeros((all_cond.shape[0], P_SIZE), jnp.float32)
    factors = jnp.concatenate(
        [edge, all_onehot, all_features, all_time, jnp.repeat(all_cond, 2, axis=1), edge], 1
    )
    factors = lax.dynamic_slice_in_dim(factors, begin_row, row_count, 1)
    first_start = P_SIZE + NCLS
    second_start = first_start + TFREQ
    final_start = second_start + D

    def rows_of(chosen, right):
        return contract("ic,id->cd", jnp.where(chosen[None, :], factors, 0.0), right)

    in_first = (row_ids >= first_start) & (row_ids < second_start)
    in_final = row_ids >= final_start
    odd = (row_ids - final_start) % 2 == 1
    near = rows_of(in_first, all_hidden)
    near = near + rows_of(jnp.logical_not(in_first | in_final), all_condition)
    near = near + rows_of(in_final & jnp.logical_not(odd), all_final[:, :D])
    near = near + rows_of(in_final & odd, all_final[:, D:])
    for begin_here, token_rows in ((0, patch_rows), (row_total - P_SIZE, head_rows)):
        here = row_ids - begin_here
        inside = (here >= 0) & (here < P_SIZE)
        near = jnp.where(
            inside[:, None], token_rows[jnp.clip(here, 0, P_SIZE - 1)], near
        )
    else_grad = lax.dynamic_slice_in_dim(near.reshape(-1), begin - begin_row * D, share, 0)
    squares = jnp.sum(owned * owned) + jnp.sum(else_grad * else_grad)
    totals = total(jnp.stack([loss_part, squares]))
    loss_total = totals[0]
    grad_norm = jnp.sqrt(totals[1])
    clip_factor = jnp.minimum(1.0, 1.0 / grad_norm)
    master_new, first_new, second_new, low_new = update_tiles(
        clip_factor, owned, tiles_master[0], tiles_first[0], tiles_second[0], bases[0]
    )
    else_master_new, else_first_new, else_second_new = adamw_flat(
        clip_factor * else_grad, else_master, else_first, else_second
    )
    return (
        loss_total,
        grad_norm,
        master_new[None],
        first_new[None],
        second_new[None],
        low_new[None],
        else_master_new,
        else_first_new,
        else_second_new,
        low(else_master_new),
    )


def solution(mesh):
    return jax.shard_map(
        on_device,
        mesh=mesh,
        in_specs=(
            P(("fsdp", "ctx"), None, None),
            P(("fsdp", "ctx"), None, None),
            P(("fsdp", "ctx")),
            P(("fsdp", "ctx")),
            P(),
            P("tp", ("fsdp", "ctx"), None, None),
            P("tp", ("fsdp", "ctx"), None, None),
            P("tp", ("fsdp", "ctx"), None, None),
            P("tp", ("fsdp", "ctx"), None, None),
            P("tp", ("fsdp", "ctx"), None, None),
            P(("fsdp", "ctx", "tp")),
            P(("fsdp", "ctx", "tp")),
            P(("fsdp", "ctx", "tp")),
            P(("fsdp", "ctx", "tp")),
        ),
        out_specs=(
            P(),
            P(),
            P("tp", ("fsdp", "ctx"), None, None),
            P("tp", ("fsdp", "ctx"), None, None),
            P("tp", ("fsdp", "ctx"), None, None),
            P("tp", ("fsdp", "ctx"), None, None),
            P(("fsdp", "ctx", "tp")),
            P(("fsdp", "ctx", "tp")),
            P(("fsdp", "ctx", "tp")),
            P(("fsdp", "ctx", "tp")),
        ),
        check_vma=False,
    )
```

time: 1710 us -> 1330 us (0.78)
  Pallas kernels: 14.9 us -> 443 us
  local copies, waits for them, and re-layouts: 541 us -> 179 us
  matrix products: 227 us -> 24.7 us
  waiting for transfers between devices: 489 us -> 391 us
  other arithmetic: 221 us -> 139 us
  starting transfers between devices: 197 us -> 136 us
    pallas_call x0 -> x47, Pallas kernels: none -> 418 us  [the longest x10 91.9 us: weight_grad_call(): pl.pallas_call(kernel, grid_spec=pltpu.PrefetchScalarGridSpec(num_scalar_...]
    unnamed x575 -> x259, local copies, waits for them, and re-layouts: 143 us -> 29.5 us
    reshape x37 -> x9, local copies, waits for them, and re-layouts: 112 us -> 11.3 us  [the longest x1 7.42 us: cut_else(): parts[4] = parts[4].reshape(D, 2 * D)]
    slice x32 -> x31, local copies, waits for them, and re-layouts: 152 us -> 59.5 us  [the longest x1 13.2 us: on_device(): parts[16 * (early + 1):]]
    dot_general x24 -> x0, matrix products: 89 us -> none  [the longest x8 30.5 us: rows_out(): lax.dot_general(left_op, weight, (((1,), (contract_dim,)), ((), ())), pre...]
    ppermute x35 -> x26, waiting for transfers between devices: 177 us -> 89.2 us  [swap_y(): return lax.ppermute(value, 'ctx', [(0, 1), (1, 0)])]
    reduce_sum x29 -> x0, other arithmetic: 64.7 us -> none  [the longest x5 20.3 us: modulate(): return normed(stream) * (1.0 + factor) + offset]
    gather x2, local copies, waits for them, and re-layouts: 57.1 us -> 2.74 us  [on_device(): token_rows[jnp.clip(here, 0, P_SIZE - 1)]]
  transfers between devices with their start and end apart: 145 -> 119, of which waited for: 53 -> 53; matrix products, arithmetic and copies ran while one was open for 36% -> 20% of each run, Pallas kernels for 0% -> 24%
where the time goes in v2:
time: 1330 us; the launch traced here: 1320 us
  Pallas kernels  443 us (33%)
  waiting for transfers between devices  391 us (29%)
  local copies, waits for them, and re-layouts  179 us (13%)
  other arithmetic  139 us (10%)
  starting transfers between devices  136 us (10%)
  matrix products  24.7 us (2%)
    ppermute x40, waiting for transfers between devices, swap_f(): lax.ppermute(value, 'fsdp', [(place, place ^ bit) for place in range(8)])  218 us
    pallas_call x10, Pallas kernels, weight_grad_call(): pl.pallas_call(kernel, grid_spec=pltpu.PrefetchScalarGridSpec(num_scalar_...  91.9 us
    ppermute x26, waiting for transfers between devices, swap_y(): return lax.ppermute(value, 'ctx', [(0, 1), (1, 0)])  89.2 us
    ppermute x24, waiting for transfers between devices, move_z(): return lambda value: lax.ppermute(value, 'fsdp', pairs)  67.9 us
    pallas_call x4, Pallas kernels, attend_back_call(): pl.pallas_call(attend_back_kernel, grid=(rows // local_len,), in_specs=[r...  64.2 us
    pallas_call x4, Pallas kernels, mlp_back_call(): pl.pallas_call(mlp_back_kernel, grid=(rows // local_len,), in_specs=[rows...  55.5 us
    ppermute x40, starting transfers between devices, swap_f(): lax.ppermute(value, 'fsdp', [(place, place ^ bit) for place in range(8)])  53.4 us
    pallas_call x10, Pallas kernels, rows_kernel_call(): pl.pallas_call(kernel, grid=(own,), in_specs=[rows] * len(wide_ins) + [fe...  52.8 us
  transfers between devices with their start and end apart: 119, of which 53 were waited for; matrix products, arithmetic and copies ran while one was open for 20% of the time, Pallas kernels for 24%

profile of v2, /device:TPU:0, one launch (start us, length us, event | category | flops | bytes accessed | tf_op | source)
XLA Modules:
  0.0 1321.4 jit_solution(8166199869987028331)
XLA Ops:
  57.1 13.0 collective-permute-done.13
  81.8 15.3 %collective-permute-done.18 = bf16[4,1090,128]{2,0,1:T(4,128)(2,1)S(1)} collective-permute-done((bf16[4,1090,128]{2,0,1:T(4,128)(2,1)S(1)}, bf16[4,1090,128]{2,0,1:T(4,128)(2,1)S(1)}, u32[]{:S(2)}, u32[]{:S(2)}) %collective-permute-start.18) | collective-permute-done | bytes 1116192 | tf_op jit(solution)/shard_map/ppermute | solution.py:185
  140.2 29.9 %collective-permute-done.24.refs_2_ = bf16[46,128,128]{2,1,0:T(8,128)(2,1)S(1)} collective-permute-done((bf16[46,128,128]{2,1,0:T(8,128)(2,1)S(1)}, bf16[46,128,128]{2,1,0:T(8,128)(2,1)S(1)}, u32[]{:S(2)}, u32[]{:S(2)}) %collective-permute-start.24) | collective-permute-done | bytes 1507360 | tf_op jit(solution)/shard_map/ppermute | solution.py:185
  187.2 12.5 collective-permute-done.26.refs_3_
  207.9 26.5 %collective-permute-done.30.refs_2_ = bf16[46,128,128]{2,1,0:T(8,128)(2,1)} collective-permute-done((bf16[46,128,128]{2,1,0:T(8,128)(2,1)}, bf16[46,128,128]{2,1,0:T(8,128)(2,1)}, u32[]{:S(2)}, u32[]{:S(2)}) %collective-permute-start.30) | collective-permute-done | bytes 1507360 | tf_op jit(solution)/shard_map/ppermute | solution.py:185
  270.5 15.6 %reshape_reshape.3 = bf16[4360,1024]{1,0:T(8,128)(2,1)} reshape(bf16[4,2,2,2,1090,128]{5,4,3,2,1,0:T(8,128)(2,1)} %copy.100) | data formatting | bytes 17858560 | tf_op jit(solution)/shard_map/reshape;reshape | solution.py:478
  369.0 16.3 %collective-permute-done.47 = bf16[26,128,128]{2,1,0:T(8,128)(2,1)} collective-permute-done((bf16[26,128,128]{2,1,0:T(8,128)(2,1)}, bf16[26,128,128]{2,1,0:T(8,128)(2,1)}, u32[]{:S(2)}, u32[]{:S(2)}) %collective-permute-start.47) | collective-permute-done | bytes 852000 | tf_op jit(solution)/shard_map/ppermute | solution.py:220
  418.2 45.1 %collective-permute-done.49.refs_1_ = bf16[104,128,128]{2,1,0:T(8,128)(2,1)S(1)} collective-permute-done((bf16[104,128,128]{2,1,0:T(8,128)(2,1)S(1)}, bf16[104,128,128]{2,1,0:T(8,128)(2,1)S(1)}, u32[]{:S(2)}, u32[]{:S(2)}) %collective-permute-start.49) | collective-permute-done | bytes 3407904 | tf_op jit(solution)/shard_map/ppermute | solution.py:185
  471.9 12.1 shard_map.223
  495.1 11.2 collective-permute-done.51.refs_0_
  518.2 11.9 shard_map.222
  572.4 11.9 shard_map.233
  585.8 12.3 shard_map.232
  616.8 13.8 %shard_map.237 = (bf16[512,2048]{1,0:T(8,128)(2,1)}, bf16[512,2048]{1,0:T(8,128)(2,1)}, f32[512,1024]{1,0:T(8,128)}) custom-call(bf16[512,1024]{1,0:T(8,128)(2,1)} %copy-done.60, f32[512,2048]{1,0:T(8,128)} %get-tuple-element.448.hidden, bf16[577,128,128]{2,1,0:T(8,128)(2,1)} %get-tuple-element.433.tile_set.qkv_tiles.proj_tiles.up_tiles.down_tiles, ...), custom_call_target="tpu_custom_call" | custom-call | flops 4294967296 | bytes 16777216 | tf_op jit(solution)/shard_map/pallas_call | solution.py:753
  630.9 14.0 %shard_map.236 = (bf16[512,2048]{1,0:T(8,128)(2,1)}, bf16[512,2048]{1,0:T(8,128)(2,1)}, f32[512,1024]{1,0:T(8,128)}) custom-call(bf16[512,1024]{1,0:T(8,128)(2,1)} %bitcast.195, f32[512,2048]{1,0:T(8,128)} %get-tuple-element.446.hidden, bf16[577,128,128]{2,1,0:T(8,128)(2,1)} %get-tuple-element.433.tile_set.qkv_tiles.proj_tiles.up_tiles.down_tiles, ...), custom_call_target="tpu_custom_call" | custom-call | flops 4294967296 | bytes 16777216 | tf_op jit(solution)/shard_map/pallas_call | solution.py:753
  656.9 16.2 %shard_map.240 = (bf16[512,1536]{1,0:T(8,128)(2,1)}, f32[512,1024]{1,0:T(8,128)}) custom-call(bf16[512,1024]{1,0:T(8,128)(2,1)} %copy-done.31, bf16[512,1536]{1,0:T(8,128)(2,1)} %get-tuple-element.455.projected, bf16[577,128,128]{2,1,0:T(8,128)(2,1)} %get-tuple-element.433.tile_set.qkv_tiles.proj_tiles.up_tiles.down_tiles, ...), custom_call_target="tpu_custom_call" | custom-call | flops 2684354560 | bytes 4194304 | tf_op jit(solution)/shard_map/pallas_call | solution.py:669
  697.6 12.2 shard_map.242
  709.8 11.5 shard_map.243
  721.3 16.0 %shard_map.239 = (bf16[512,1536]{1,0:T(8,128)(2,1)}, f32[512,1024]{1,0:T(8,128)}) custom-call(bf16[512,1024]{1,0:T(8,128)(2,1)} %bitcast.170, bf16[512,1536]{1,0:T(8,128)(2,1)} %get-tuple-element.453.projected, bf16[577,128,128]{2,1,0:T(8,128)(2,1)} %get-tuple-element.433.tile_set.qkv_tiles.proj_tiles.up_tiles.down_tiles, ...), custom_call_target="tpu_custom_call" | custom-call | flops 2684354560 | bytes 4194304 | tf_op jit(solution)/shard_map/pallas_call | solution.py:669
  782.7 13.8 %shard_map.248 = (bf16[512,2048]{1,0:T(8,128)(2,1)}, bf16[512,2048]{1,0:T(8,128)(2,1)}, f32[512,1024]{1,0:T(8,128)}) custom-call(bf16[512,1024]{1,0:T(8,128)(2,1)} %copy-done.30, f32[512,2048]{1,0:T(8,128)} %get-tuple-element.484.hidden, bf16[577,128,128]{2,1,0:T(8,128)(2,1)} %get-tuple-element.417.tile_set.qkv_tiles.proj_tiles.up_tiles.down_tiles, ...), custom_call_target="tpu_custom_call" | custom-call | flops 4294967296 | bytes 16777216 | tf_op jit(solution)/shard_map/pallas_call | solution.py:753
  796.4 22.7 %collective-permute-done.83 = bf16[52,128,128]{2,1,0:T(8,128)(2,1)} collective-permute-done((bf16[52,128,128]{2,1,0:T(8,128)(2,1)}, bf16[52,128,128]{2,1,0:T(8,128)(2,1)}, u32[]{:S(2)}, u32[]{:S(2)}) %collective-permute-start.83) | collective-permute-done | bytes 1703968 | tf_op jit(solution)/shard_map/ppermute | solution.py:181
  830.6 14.0 %shard_map.247 = (bf16[512,2048]{1,0:T(8,128)(2,1)}, bf16[512,2048]{1,0:T(8,128)(2,1)}, f32[512,1024]{1,0:T(8,128)}) custom-call(bf16[512,1024]{1,0:T(8,128)(2,1)} %bitcast.166, f32[512,2048]{1,0:T(8,128)} %get-tuple-element.482.hidden, bf16[577,128,128]{2,1,0:T(8,128)(2,1)} %get-tuple-element.417.tile_set.qkv_tiles.proj_tiles.up_tiles.down_tiles, ...), custom_call_target="tpu_custom_call" | custom-call | flops 4294967296 | bytes 16777216 | tf_op jit(solution)/shard_map/pallas_call | solution.py:753
  857.7 16.0 %shard_map.251 = (bf16[512,1536]{1,0:T(8,128)(2,1)}, f32[512,1024]{1,0:T(8,128)}) custom-call(bf16[512,1024]{1,0:T(8,128)(2,1)} %copy-done.33, bf16[512,1536]{1,0:T(8,128)(2,1)} %get-tuple-element.491.projected, bf16[577,128,128]{2,1,0:T(8,128)(2,1)} %get-tuple-element.417.tile_set.qkv_tiles.proj_tiles.up_tiles.down_tiles, ...), custom_call_target="tpu_custom_call" | custom-call | flops 2684354560 | bytes 4194304 | tf_op jit(solution)/shard_map/pallas_call | solution.py:669
  873.7 11.8 shard_map.253.refs_4_
  885.6 10.9 shard_map.254.refs_4_
  896.5 16.0 %shard_map.250 = (bf16[512,1536]{1,0:T(8,128)(2,1)}, f32[512,1024]{1,0:T(8,128)}) custom-call(bf16[512,1024]{1,0:T(8,128)(2,1)} %bitcast.177, bf16[512,1536]{1,0:T(8,128)(2,1)} %get-tuple-element.489.projected, bf16[577,128,128]{2,1,0:T(8,128)(2,1)} %get-tuple-element.417.tile_set.qkv_tiles.proj_tiles.up_tiles.down_tiles, ...), custom_call_target="tpu_custom_call" | custom-call | flops 2684354560 | bytes 4194304 | tf_op jit(solution)/shard_map/pallas_call | solution.py:669
  978.7 11.4 collective-permute-done.89
  1052.6 12.2 collective-permute-done.97
  1157.7 12.7 collective-permute-done.110
  1181.6 24.8 %collective-permute-done.112 = bf16[47,128,128]{2,1,0:T(8,128)(2,1)S(1)} collective-permute-done((bf16[47,128,128]{2,1,0:T(8,128)(2,1)S(1)}, bf16[47,128,128]{2,1,0:T(8,128)(2,1)S(1)}, u32[]{:S(2)}, u32[]{:S(2)}) %collective-permute-start.112) | collective-permute-done | bytes 1540128 | tf_op jit(solution)/shard_map/ppermute | solution.py:185
  1228.8 13.2 %slice.455 = bf16[432,128,128]{2,1,0:T(8,128)(2,1)} slice(bf16[1184,128,128]{2,1,0:T(8,128)(2,1)} %constant_dynamic-update-slice_fusion.8), slice={[752:1184], [0:128], [0:128]} | slice | bytes 28311552 | tf_op jit(solution)/shard_map/slice | solution.py:1475
  1294.7 25.3 %shard_map.260 = (f32[72,128,128]{2,1,0:T(8,128)}, f32[72,128,128]{2,1,0:T(8,128)}, f32[72,128,128]{2,1,0:T(8,128)}, bf16[72,128,128]{2,1,0:T(8,128)(2,1)}) custom-call(f32[1,1]{1,0:T(1,128)} %bitcast.58.clip, f32[72,128,128]{2,1,0:T(8,128)} %get-tuple-element.542.grad, f32[72,128,128]{2,1,0:T(8,128)} %bitcast.154, f32[72,128,128]{2,1,0:T(8,128)} %bitcast.155, ...), custom_call_target="tpu_custom_call" | custom-call | flops 35389440 | bytes 35389440 | tf_op jit(solution)/shard_map/pallas_call | solution.py:1189
  (729 shorter events, 792.3 us)
Async XLA Ops:
  2.2 36.1 %collective-permute-start.8 = (bf16[46,128,128]{2,1,0:T(8,128)(2,1)S(1)}, bf16[46,128,128]{2,1,0:T(8,128)(2,1)}, u32[]{:S(2)}, u32[]{:S(2)}) collective-permute-start(bf16[46,128,128]{2,1,0:T(8,128)(2,1)S(1)} %slice_bitcast_fusion.refs_0_), channel_id=1, source_target_pairs={{0,4},{4,0},{8,12},{12,8},{16,20},{20,16},{24,28},{28,24},{1,5},{5... | collective-permute-start | bytes 4521992 | tf_op jit(solution)/shard_map/ppermute | solution.py:185
  5.2 35.2 %collective-permute-start.9 = (bf16[46,128,128]{2,1,0:T(8,128)(2,1)S(1)}, bf16[46,128,128]{2,1,0:T(8,128)(2,1)}, u32[]{:S(2)}, u32[]{:S(2)}) collective-permute-start(bf16[46,128,128]{2,1,0:T(8,128)(2,1)S(1)} %slice_bitcast_fusion.refs_0_), channel_id=1, source_target_pairs={{0,2},{2,0},{1,3},{3,1},{4,6},{6,4},{5,7},{7,5},{8,10},{10,8},{9,1... | collective-permute-start | bytes 4521992 | tf_op jit(solution)/shard_map/ppermute | solution.py:181
  6.7 35.7 %collective-permute-start.10 = (bf16[46,128,128]{2,1,0:T(8,128)(2,1)S(1)}, bf16[46,128,128]{2,1,0:T(8,128)(2,1)S(1)}, u32[]{:S(2)}, u32[]{:S(2)}) collective-permute-start(bf16[46,128,128]{2,1,0:T(8,128)(2,1)S(1)} %slice_bitcast_fusion.refs_0_), channel_id=1, source_target_pairs={{0,8},{4,12},{8,16},{12,20},{16,24},{20,28},{1,9},{5,13},{9,17},{1... | collective-permute-start | bytes 4521992 | tf_op jit(solution)/shard_map/ppermute | solution.py:220
  10.3 35.9 %collective-permute-start.11 = (bf16[46,128,128]{2,1,0:T(8,128)(2,1)S(1)}, bf16[46,128,128]{2,1,0:T(8,128)(2,1)}, u32[]{:S(2)}, u32[]{:S(2)}) collective-permute-start(bf16[46,128,128]{2,1,0:T(8,128)(2,1)S(1)} %slice_bitcast_fusion.refs_0_), channel_id=1, source_target_pairs={{8,0},{12,4},{16,8},{20,12},{24,16},{28,20},{9,1},{13,5},{17,9},{2... | collective-permute-start | bytes 4521992 | tf_op jit(solution)/shard_map/ppermute | solution.py:220
  133.0 115.9 %collective-permute-start.21 = (bf16[4,2,2,1090,128]{4,0,3,2,1:T(4,128)(2,1)}, bf16[4,2,2,1090,128]{4,0,3,2,1:T(4,128)(2,1)}, u32[]{:S(2)}, u32[]{:S(2)}) collective-permute-start(bf16[4,2,2,1090,128]{4,0,3,2,1:T(4,128)(2,1)} %copy.97), channel_id=1, source_target_pairs={{0,1},{1,0},{2,3},{3,2},{4,5},{5,4},{6,7},{7,6},{8,9},{9,8},{10,11... | collective-permute-start | bytes 13393928 | tf_op jit(solution)/shard_map/ppermute | solution.py:177
  134.6 35.5 %collective-permute-start.24 = (bf16[46,128,128]{2,1,0:T(8,128)(2,1)S(1)}, bf16[46,128,128]{2,1,0:T(8,128)(2,1)S(1)}, u32[]{:S(2)}, u32[]{:S(2)}) collective-permute-start(bf16[46,128,128]{2,1,0:T(8,128)(2,1)S(1)} %broadcast_select_fusion.1.refs_0_), channel_id=1, source_target_pairs={{0,4},{4,0},{8,12},{12,8},{16,20},{20,16},{24,28},{28,24},{1,5},{5... | collective-permute-start | bytes 4521992 | tf_op jit(solution)/shard_map/ppermute | solution.py:185
  137.1 35.3 %collective-permute-start.22 = (bf16[46,128,128]{2,1,0:T(8,128)(2,1)S(1)}, bf16[46,128,128]{2,1,0:T(8,128)(2,1)}, u32[]{:S(2)}, u32[]{:S(2)}) collective-permute-start(bf16[46,128,128]{2,1,0:T(8,128)(2,1)S(1)} %copy-done.17), channel_id=1, source_target_pairs={{8,16},{12,20},{16,24},{20,28},{9,17},{13,21},{17,25},{21,29},{10,... | collective-permute-start | bytes 4521992 | tf_op jit(solution)/shard_map/ppermute | solution.py:220
  138.9 42.9 %collective-permute-start.23 = (bf16[46,128,128]{2,1,0:T(8,128)(2,1)}, bf16[46,128,128]{2,1,0:T(8,128)(2,1)}, u32[]{:S(2)}, u32[]{:S(2)}) collective-permute-start(bf16[46,128,128]{2,1,0:T(8,128)(2,1)} %collective-permute-done.11), channel_id=1, source_target_pairs={{8,0},{12,4},{16,8},{20,12},{9,1},{13,5},{17,9},{21,13},{10,2},{14... | collective-permute-start | bytes 4521992 | tf_op jit(solution)/shard_map/ppermute | solution.py:220
  203.3 35.2 %collective-permute-start.28 = (bf16[46,128,128]{2,1,0:T(8,128)(2,1)}, bf16[46,128,128]{2,1,0:T(8,128)(2,1)}, u32[]{:S(2)}, u32[]{:S(2)}) collective-permute-start(bf16[46,128,128]{2,1,0:T(8,128)(2,1)} %collective-permute-done.23), channel_id=1, source_target_pairs={{8,0},{12,4},{9,1},{13,5},{10,2},{14,6},{11,3},{15,7}} | collective-permute-start | bytes 4521992 | tf_op jit(solution)/shard_map/ppermute | solution.py:220
  238.5 60.6 %collective-permute-start.34 = (bf16[23,128,128]{2,1,0:T(8,128)(2,1)}, bf16[23,128,128]{2,1,0:T(8,128)(2,1)}, u32[]{:S(2)}, u32[]{:S(2)}) collective-permute-start(bf16[23,128,128]{2,1,0:T(8,128)(2,1)} %slice.400), channel_id=1, source_target_pairs={{0,2},{2,0},{1,3},{3,1},{4,6},{6,4},{5,7},{7,5},{8,10},{10,8},{9,1... | collective-permute-start | bytes 2261000 | tf_op jit(solution)/shard_map/ppermute | solution.py:181
  239.5 59.7 %collective-permute-start.35 = (bf16[23,128,128]{2,1,0:T(8,128)(2,1)}, bf16[23,128,128]{2,1,0:T(8,128)(2,1)}, u32[]{:S(2)}, u32[]{:S(2)}) collective-permute-start(bf16[23,128,128]{2,1,0:T(8,128)(2,1)} %slice.401), channel_id=1, source_target_pairs={{0,4},{4,0},{8,12},{12,8},{16,20},{20,16},{24,28},{28,24},{1,5},{5... | collective-permute-start | bytes 2261000 | tf_op jit(solution)/shard_map/ppermute | solution.py:185
  241.0 58.2 %collective-permute-start.32 = (bf16[26,128,128]{2,1,0:T(8,128)(2,1)S(1)}, bf16[26,128,128]{2,1,0:T(8,128)(2,1)}, u32[]{:S(2)}, u32[]{:S(2)}) collective-permute-start(bf16[26,128,128]{2,1,0:T(8,128)(2,1)S(1)} %slice_bitcast_fusion.1), channel_id=1, source_target_pairs={{0,8},{4,12},{8,16},{12,20},{16,24},{20,28},{1,9},{5,13},{9,17},{1... | collective-permute-start | bytes 2555912 | tf_op jit(solution)/shard_map/ppermute | solution.py:220
  247.6 51.5 %collective-permute-start.33 = (bf16[26,128,128]{2,1,0:T(8,128)(2,1)S(1)}, bf16[26,128,128]{2,1,0:T(8,128)(2,1)}, u32[]{:S(2)}, u32[]{:S(2)}) collective-permute-start(bf16[26,128,128]{2,1,0:T(8,128)(2,1)S(1)} %slice_bitcast_fusion.1), channel_id=1, source_target_pairs={{8,0},{12,4},{16,8},{20,12},{24,16},{28,20},{9,1},{13,5},{17,9},{2... | collective-permute-start | bytes 2555912 | tf_op jit(solution)/shard_map/ppermute | solution.py:220
  387.7 75.6 %collective-permute-start.49 = (bf16[104,128,128]{2,1,0:T(8,128)(2,1)S(1)}, bf16[104,128,128]{2,1,0:T(8,128)(2,1)S(1)}, u32[]{:S(2)}, u32[]{:S(2)}) collective-permute-start(bf16[104,128,128]{2,1,0:T(8,128)(2,1)S(1)} %pad_maximum_fusion.3.refs_0_), channel_id=1, source_target_pairs={{0,4},{4,0},{8,12},{12,8},{16,20},{20,16},{24,28},{28,24},{1,5},{5... | collective-permute-start | bytes 10223624 | tf_op jit(solution)/shard_map/ppermute | solution.py:185
  389.5 75.4 %collective-permute-start.50 = (bf16[104,128,128]{2,1,0:T(8,128)(2,1)S(1)}, bf16[104,128,128]{2,1,0:T(8,128)(2,1)}, u32[]{:S(2)}, u32[]{:S(2)}) collective-permute-start(bf16[104,128,128]{2,1,0:T(8,128)(2,1)S(1)} %pad_maximum_fusion.3.refs_0_), channel_id=1, source_target_pairs={{0,2},{2,0},{1,3},{3,1},{4,6},{6,4},{5,7},{7,5},{8,10},{10,8},{9,1... | collective-permute-start | bytes 10223624 | tf_op jit(solution)/shard_map/ppermute | solution.py:181
  417.7 53.2 %collective-permute-start.45 = (bf16[512,1024]{1,0:T(8,128)(2,1)}, bf16[512,1024]{1,0:T(8,128)(2,1)S(1)}, u32[]{:S(2)}, u32[]{:S(2)}) collective-permute-start(bf16[512,1024]{1,0:T(8,128)(2,1)} %bitcast.157), channel_id=1, source_target_pairs={{0,1},{1,0},{2,3},{3,2},{4,5},{5,4},{6,7},{7,6},{8,9},{9,8},{10,11... | collective-permute-start | bytes 3145736 | tf_op jit(solution)/shard_map/ppermute | solution.py:177
  467.8 38.5 %collective-permute-start.51 = (bf16[52,128,128]{2,1,0:T(8,128)(2,1)}, bf16[52,128,128]{2,1,0:T(8,128)(2,1)S(1)}, u32[]{:S(2)}, u32[]{:S(2)}) collective-permute-start(bf16[52,128,128]{2,1,0:T(8,128)(2,1)} %slice.406), channel_id=1, source_target_pairs={{0,2},{2,0},{1,3},{3,1},{4,6},{6,4},{5,7},{7,5},{8,10},{10,8},{9,1... | collective-permute-start | bytes 5111816 | tf_op jit(solution)/shard_map/ppermute | solution.py:181
  469.1 38.2 %collective-permute-start.52 = (bf16[52,128,128]{2,1,0:T(8,128)(2,1)}, bf16[52,128,128]{2,1,0:T(8,128)(2,1)S(1)}, u32[]{:S(2)}, u32[]{:S(2)}) collective-permute-start(bf16[52,128,128]{2,1,0:T(8,128)(2,1)} %slice.407), channel_id=1, source_target_pairs={{0,4},{4,0},{8,12},{12,8},{16,20},{20,16},{24,28},{28,24},{1,5},{5... | collective-permute-start | bytes 5111816 | tf_op jit(solution)/shard_map/ppermute | solution.py:185
  483.9 47.0 %collective-permute-start.46 = (f32[512,1024]{1,0:T(8,128)}, f32[512,1024]{1,0:T(8,128)S(1)}, u32[]{:S(2)}, u32[]{:S(2)}) collective-permute-start(f32[512,1024]{1,0:T(8,128)} %get-tuple-element.423), channel_id=1, source_target_pairs={{0,1},{1,0},{2,3},{3,2},{4,5},{5,4},{6,7},{7,6},{8,9},{9,8},{10,11... | collective-permute-start | bytes 6291464 | tf_op jit(solution)/shard_map/ppermute | solution.py:177
  673.2 69.4 %collective-permute-start.61 = (f32[512,1024]{1,0:T(8,128)}, f32[512,1024]{1,0:T(8,128)S(1)}, u32[]{:S(2)}, u32[]{:S(2)}) collective-permute-start(f32[512,1024]{1,0:T(8,128)} %get-tuple-element.456), channel_id=1, source_target_pairs={{0,1},{1,0},{2,3},{3,2},{4,5},{5,4},{6,7},{7,6},{8,9},{9,8},{10,11... | collective-permute-start | bytes 6291464 | tf_op jit(solution)/shard_map/ppermute | solution.py:177
  779.7 39.4 %collective-permute-start.83 = (bf16[52,128,128]{2,1,0:T(8,128)(2,1)}, bf16[52,128,128]{2,1,0:T(8,128)(2,1)}, u32[]{:S(2)}, u32[]{:S(2)}) collective-permute-start(bf16[52,128,128]{2,1,0:T(8,128)(2,1)} %get-tuple-element.505), channel_id=1, source_target_pairs={{0,2},{2,0},{1,3},{3,1},{4,6},{6,4},{5,7},{7,5},{8,10},{10,8},{9,1... | collective-permute-start | bytes 5111816 | tf_op jit(solution)/shard_map/ppermute | solution.py:181
  780.5 39.2 %collective-permute-start.84 = (bf16[52,128,128]{2,1,0:T(8,128)(2,1)}, bf16[52,128,128]{2,1,0:T(8,128)(2,1)}, u32[]{:S(2)}, u32[]{:S(2)}) collective-permute-start(bf16[52,128,128]{2,1,0:T(8,128)(2,1)} %get-tuple-element.506), channel_id=1, source_target_pairs={{0,4},{4,0},{8,12},{12,8},{16,20},{20,16},{24,28},{28,24},{1,5},{5... | collective-permute-start | bytes 5111816 | tf_op jit(solution)/shard_map/ppermute | solution.py:185
  796.4 48.1 %collective-permute-start.77 = (f32[512,1024]{1,0:T(8,128)}, f32[512,1024]{1,0:T(8,128)S(1)}, u32[]{:S(2)}, u32[]{:S(2)}) collective-permute-start(f32[512,1024]{1,0:T(8,128)} %get-tuple-element.485), channel_id=1, source_target_pairs={{0,1},{1,0},{2,3},{3,2},{4,5},{5,4},{6,7},{7,6},{8,9},{9,8},{10,11... | collective-permute-start | bytes 6291464 | tf_op jit(solution)/shard_map/ppermute | solution.py:177
  828.2 98.8 %collective-permute-start.85 = (bf16[104,128,128]{2,1,0:T(8,128)(2,1)}, bf16[104,128,128]{2,1,0:T(8,128)(2,1)}, u32[]{:S(2)}, u32[]{:S(2)}) collective-permute-start(bf16[104,128,128]{2,1,0:T(8,128)(2,1)} %pad_maximum_fusion.4), channel_id=1, source_target_pairs={{0,4},{4,0},{8,12},{12,8},{16,20},{20,16},{24,28},{28,24},{1,5},{5... | collective-permute-start | bytes 10223624 | tf_op jit(solution)/shard_map/ppermute | solution.py:185
  829.4 97.7 %collective-permute-start.86 = (bf16[104,128,128]{2,1,0:T(8,128)(2,1)}, bf16[104,128,128]{2,1,0:T(8,128)(2,1)}, u32[]{:S(2)}, u32[]{:S(2)}) collective-permute-start(bf16[104,128,128]{2,1,0:T(8,128)(2,1)} %pad_maximum_fusion.5), channel_id=1, source_target_pairs={{0,2},{2,0},{1,3},{3,1},{4,6},{6,4},{5,7},{7,5},{8,10},{10,8},{9,1... | collective-permute-start | bytes 10223624 | tf_op jit(solution)/shard_map/ppermute | solution.py:181
  855.4 117.6 %collective-permute-start.63 = (f32[4,2048]{1,0:T(4,128)}, f32[4,2048]{1,0:T(4,128)}, u32[]{:S(2)}, u32[]{:S(2)}) collective-permute-start(f32[4,2048]{1,0:T(4,128)} %dynamic_update_slice.20), channel_id=1, source_target_pairs={{0,1},{1,0},{2,3},{3,2},{4,5},{5,4},{6,7},{7,6},{8,9},{9,8},{10,11... | collective-permute-start | bytes 98312 | tf_op jit(solution)/shard_map/ppermute | solution.py:177
  873.7 63.5 %collective-permute-start.79 = (f32[512,1024]{1,0:T(8,128)}, f32[512,1024]{1,0:T(8,128)S(1)}, u32[]{:S(2)}, u32[]{:S(2)}) collective-permute-start(f32[512,1024]{1,0:T(8,128)} %get-tuple-element.492), channel_id=1, source_target_pairs={{0,1},{1,0},{2,3},{3,2},{4,5},{5,4},{6,7},{7,6},{8,9},{9,8},{10,11... | collective-permute-start | bytes 6291464 | tf_op jit(solution)/shard_map/ppermute | solution.py:177
  1034.5 37.2 %collective-permute-start.95 = (bf16[47,128,128]{2,1,0:T(8,128)(2,1)}, bf16[47,128,128]{2,1,0:T(8,128)(2,1)S(1)}, u32[]{:S(2)}, u32[]{:S(2)}) collective-permute-start(bf16[47,128,128]{2,1,0:T(8,128)(2,1)} %pad_maximum_fusion.7), channel_id=1, source_target_pairs={{0,4},{4,0},{8,12},{12,8},{16,20},{20,16},{24,28},{28,24},{1,5},{5... | collective-permute-start | bytes 4620296 | tf_op jit(solution)/shard_map/ppermute | solution.py:185
  1035.4 36.3 %collective-permute-start.96 = (bf16[47,128,128]{2,1,0:T(8,128)(2,1)}, bf16[47,128,128]{2,1,0:T(8,128)(2,1)}, u32[]{:S(2)}, u32[]{:S(2)}) collective-permute-start(bf16[47,128,128]{2,1,0:T(8,128)(2,1)} %pad_maximum_fusion.8), channel_id=1, source_target_pairs={{0,2},{2,0},{1,3},{3,1},{4,6},{6,4},{5,7},{7,5},{8,10},{10,8},{9,1... | collective-permute-start | bytes 4620296 | tf_op jit(solution)/shard_map/ppermute | solution.py:181
  1111.6 38.1 %collective-permute-start.105 = (bf16[47,128,128]{2,1,0:T(8,128)(2,1)}, bf16[47,128,128]{2,1,0:T(8,128)(2,1)}, u32[]{:S(2)}, u32[]{:S(2)}) collective-permute-start(bf16[47,128,128]{2,1,0:T(8,128)(2,1)} %pad_maximum_fusion.9), channel_id=1, source_target_pairs={{0,4},{4,0},{8,12},{12,8},{16,20},{20,16},{24,28},{28,24},{1,5},{5... | collective-permute-start | bytes 4620296 | tf_op jit(solution)/shard_map/ppermute | solution.py:185
  1113.3 36.4 %collective-permute-start.106 = (bf16[47,128,128]{2,1,0:T(8,128)(2,1)}, bf16[47,128,128]{2,1,0:T(8,128)(2,1)}, u32[]{:S(2)}, u32[]{:S(2)}) collective-permute-start(bf16[47,128,128]{2,1,0:T(8,128)(2,1)} %pad_maximum_fusion.10), channel_id=1, source_target_pairs={{0,2},{2,0},{1,3},{3,1},{4,6},{6,4},{5,7},{7,5},{8,10},{10,8},{9,1... | collective-permute-start | bytes 4620296 | tf_op jit(solution)/shard_map/ppermute | solution.py:181
  1213.2 35.9 %collective-permute-start.116 = (bf16[47,128,128]{2,1,0:T(8,128)(2,1)}, bf16[47,128,128]{2,1,0:T(8,128)(2,1)}, u32[]{:S(2)}, u32[]{:S(2)}) collective-permute-start(bf16[47,128,128]{2,1,0:T(8,128)(2,1)} %pad_maximum_fusion.11), channel_id=1, source_target_pairs={{0,4},{4,0},{8,12},{12,8},{16,20},{20,16},{24,28},{28,24},{1,5},{5... | collective-permute-start | bytes 4620296 | tf_op jit(solution)/shard_map/ppermute | solution.py:185
  (214 other events, 2839.8 us)

commit v3 on v2

--- a/solution.py
+++ b/solution.py
@@ -295,28 +295,25 @@
         sends = [(swap_x, block), (swap_y, block)]
         waits = token
         if rel == 2:
-            waits += (flat,)
+            waits += (whole,)
         elif rel == 3:
             waits += rest
-        if rel < 3:
-            by_x, by_y, *arrived = lanes.step(sends + line.sends(), *waits)
-            line.take(arrived)
-        else:
-            by_x, by_y, *arrived = lanes.step(sends + late_line.sends(), *waits)
-            late_line.take(arrived)
+        going = line if rel < 3 else late_line
+        by_x, by_y, *arrived = lanes.step(sends + going.sends(), *waits)
+        going.take(arrived)
         sends = [(swap_y, by_x[:half]), (swap_x, by_y[half:])]
         if rel == 0:
             first, second, *arrived = lanes.step(
                 sends + [(to_z(other), else_low.reshape(1, -1, 128)) for other in (1, 2, 3)],
                 targets,
             )
-            flat = gather_else(else_low, lanes, arrived)
-            rest = cut_else(flat)
-        elif rel == 1:
-            first, second = lanes.step(sends)
-        else:
+            whole = gather_else(else_low, lanes, arrived)
+            rest = cut_else(whole)
+        elif rel < 3:
             first, second, *arrived = lanes.step(sends + late_line.sends())
             late_line.take(arrived)
+        else:
+            first, second = lanes.step(sends)
         at = 4 * rel * early
         group = [
             (block, at),
@@ -352,19 +349,34 @@
     return ((rel_x * 2 + rel_y) * 4 + rel_z) * slots + slot
 
 
-def scatter_late(parts, slots, lanes):
+def scatter_late_first(parts, slots, lanes, head_sum, images_part):
+    both = parts[12 * slots :]
+    arrived = lanes.step(
+        [(swap_y, both[: 2 * slots]), (swap_x, both[2 * slots :]), (swap_y, head_sum)]
+        + [(to_z(rel), images_part) for rel in (1, 2, 3)]
+    )
+    return arrived[:2], head_sum + arrived[2], jnp.concatenate([images_part] + arrived[3:], 0)
+
+
+def scatter_late(parts, slots, lanes, wait, later):
     count = 4 * slots
     half = count // 2
-    keep, to_y, to_x, both = (parts[part * count : (part + 1) * count] for part in range(4))
-    by_y, by_x = lanes.step([(swap_y, both[:half]), (swap_x, both[half:])])
+    keep, to_y, to_x, _ = (parts[part * count : (part + 1) * count] for part in range(4))
+    (by_y, by_x), head_sum, images = wait
     to_x = jnp.concatenate([low(wide(to_x[:half]) + by_y), to_x[half:]], 0)
     to_y = jnp.concatenate([to_y[:half], low(wide(to_y[half:]) + by_x)], 0)
-    from_x, from_y = lanes.step([(swap_x, to_x), (swap_y, to_y)])
+    from_x, from_y, head_x, images_y = lanes.step(
+        [(swap_x, to_x), (swap_y, to_y), (swap_x, head_sum), (swap_y, images)], later
+    )
     keep = wide(keep) + from_x + from_y
-    return [keep[rel * slots : (rel + 1) * slots] for rel in range(4)]
-
-
-def scatter_early(parts, slots, lanes, late, images_part):
+    return (
+        [keep[rel * slots : (rel + 1) * slots] for rel in range(4)],
+        head_sum + head_x,
+        jnp.concatenate([images, images_y], 0),
+    )
+
+
+def scatter_early(parts, slots, lanes, late, head_sum, early_images, images_part):
     half = slots // 2
 
     def block(part, begin, end):
@@ -405,9 +417,13 @@
         return wide(block(4 * rel, 0, slots)) + arrived[0] + arrived[1]
 
     line, late_line = ZSum(), ZSum()
-    arrived = lanes.step(diagonal(3) + late_line.sends(3, late[3]))
+    arrived = lanes.step(
+        diagonal(3) + late_line.sends(3, late[3]) + [(to_z(1), head_sum), (swap_x, early_images)]
+    )
     diagonal_3 = arrived[:2]
-    late_line.take(arrived[2:])
+    late_line.take(arrived[2:4])
+    head_sum = head_sum + arrived[4]
+    early_images = jnp.concatenate([early_images, arrived[5]], 0)
     arrived = lanes.step(diagonal(2) + late_line.sends(2, late[2]))
     diagonal_2 = arrived[:2]
     late_line.take(arrived[2:])
@@ -415,9 +431,12 @@
     late_line.take(arrived[2:])
     owned_late = late_line.total(late[0])
     kept_3 = kept(3, arrived)
-    arrived = lanes.step(diagonal(1) + [(to_z(rel), images_part) for rel in (1, 2, 3)])
+    arrived = lanes.step(
+        diagonal(1) + [(to_z(rel), images_part) for rel in (1, 2, 3)] + [(to_z(2), head_sum)]
+    )
     diagonal_1 = arrived[:2]
-    images = jnp.concatenate([images_part] + arrived[2:], 0)
+    images = jnp.concatenate([images_part] + arrived[2:5], 0)
+    head_sum = head_sum + arrived[5]
     arrived = lanes.step(sides(2, diagonal_2) + line.sends(3, kept_3) + [(swap_y, images)])
     line.take(arrived[2:4])
     kept_2 = kept(2, arrived)
@@ -429,7 +448,7 @@
     line.take(arrived[2:4])
     arrived_0 = lanes.step(sides(0, diagonal_0) + line.sends(1, kept(1, arrived)))
     line.take(arrived_0[2:4])
-    return line.total(kept(0, arrived_0)), owned_late, images
+    return line.total(kept(0, arrived_0)), owned_late, images, head_sum, early_images
 
 
 def gather_images(value):
@@ -471,7 +490,7 @@
     other = swap_tp(chip)
     return jnp.stack(
         [jnp.where(core == 0, chip, other), jnp.where(core == 0, other, chip)], 3
-    ).reshape(-1)
+    )
 
 
 def cut_else(flat):
@@ -588,10 +607,10 @@
         query = values[:, at : at + HD]
         key_rows = values[:, width + at : width + at + HD]
         value_rows = values[:, 2 * width + at : 2 * width + at + HD]
-        scores = against_value(query, key_rows) * HD ** (-0.5)
-        exponent = jnp.exp(scores - jnp.max(scores, -1, keepdims=True))
-        probabilities = low(exponent / jnp.sum(exponent, -1, keepdims=True))
-        results.append(low(product(probabilities, value_rows)))
+        scores = against_value(key_rows, query) * HD ** (-0.5)
+        exponent = jnp.exp(scores - jnp.max(scores, 0, keepdims=True))
+        probabilities = low(exponent / jnp.sum(exponent, 0, keepdims=True))
+        results.append(low(over_rows(probabilities, value_rows)))
     result = jnp.concatenate(results, 1)
     attended[...] = result
     partial[...] = product(result, w_proj[...])
@@ -647,17 +666,17 @@
         key_rows = values[:, width + at : width + at + HD]
         value_rows = values[:, 2 * width + at : 2 * width + at + HD]
         grad_here = grad_attended[:, at : at + HD]
-        scores = against_value(query, key_rows) * HD ** (-0.5)
-        exponent = jnp.exp(scores - jnp.max(scores, -1, keepdims=True))
-        probabilities = exponent / jnp.sum(exponent, -1, keepdims=True)
-        grad_prob = against_value(grad_here, value_rows)
+        scores = against_value(key_rows, query) * HD ** (-0.5)
+        exponent = jnp.exp(scores - jnp.max(scores, 0, keepdims=True))
+        probabilities = exponent / jnp.sum(exponent, 0, keepdims=True)
+        grad_prob = against_value(value_rows, grad_here)
         grad_scores = low(
             probabilities
-            * (grad_prob - jnp.sum(probabilities * grad_prob, -1, keepdims=True))
-        )
-        grads[0].append(low(product(grad_scores, key_rows) * HD ** (-0.5)))
-        grads[1].append(low(over_rows(grad_scores, query) * HD ** (-0.5)))
-        grads[2].append(low(over_rows(low(probabilities), grad_here)))
+            * (grad_prob - jnp.sum(probabilities * grad_prob, 0, keepdims=True))
+        )
+        grads[0].append(low(over_rows(grad_scores, key_rows) * HD ** (-0.5)))
+        grads[1].append(low(product(grad_scores, query) * HD ** (-0.5)))
+        grads[2].append(low(product(low(probabilities), grad_here)))
     result = jnp.concatenate(grads[0] + grads[1] + grads[2], 1)
     grad_qkv[...] = result
     partial[...] = against_value(result, w_qkv[...])
@@ -688,34 +707,66 @@
     )(grad_branch, projected, store, store)
 
 
-def mlp_kernel(normed_mid, up_tiles, down_tiles, hidden, partial, w_up, w_down):
+def mlp_chunk(tp_parts):
+    return min(4 * B, F // tp_parts)
+
+
+def chunk_specs(tp_parts):
+    amount = D * mlp_chunk(tp_parts) // (B * B)
+    up, down = (segments(tp_parts)[kind][1] // amount for kind in (2, 3))
+    return [
+        pl.BlockSpec((amount, B, B), lambda step: (up + step, 0, 0)),
+        pl.BlockSpec((amount, B, B), lambda step: (down + step, 0, 0)),
+    ]
+
+
+def store_of_tile(tile, tp_parts):
+    amount, begin = segments(tp_parts)[2]
+    within = tile % sum(count for count, _ in segments(tp_parts)) - begin
+    columns, wide_step = F // tp_parts // B, mlp_chunk(tp_parts) // B
+    row, column = within // columns, within % columns
+    moved = (column // wide_step * (D // B) + row) * wide_step + column % wide_step
+    return jnp.where((within >= 0) & (within < amount), tile + moved - within, tile)
+
+
+def add_to(total_ref, value):
     @pl.when(pl.program_id(0) == 0)
     def _():
-        untile_into(w_up, up_tiles)
-        untile_into(w_down, down_tiles)
-
+        total_ref[...] = value
+
+    @pl.when(pl.program_id(0) > 0)
+    def _():
+        total_ref[...] += value
+
+
+def mlp_kernel(normed_mid, up_tiles, down_tiles, hidden, partial, w_up, w_down):
+    untile_into(w_up, up_tiles)
+    untile_into(w_down, down_tiles)
     values = product(normed_mid[...], w_up[...])
     hidden[...] = values
-    partial[...] = product(low(gelu_tanh(values)), w_down[...])
+    add_to(partial, product(low(gelu_tanh(values)), w_down[...]))
+
+
+def chunk_scratch(tp_parts):
+    width = mlp_chunk(tp_parts)
+    return [pltpu.VMEM((D, width), jnp.bfloat16), pltpu.VMEM((width, D), jnp.bfloat16)]
+
+
+def all_rows(rows):
+    return pl.BlockSpec((rows, D), lambda step: (0, 0))
 
 
 def mlp_call(normed_mid, store, tp_parts, local_len):
     rows = normed_mid.shape[0]
-    width = F // tp_parts
+    width, step_width = F // tp_parts, mlp_chunk(tp_parts)
+    step_spec = pl.BlockSpec((rows, step_width), lambda step: (0, step))
     return pl.pallas_call(
         mlp_kernel,
-        grid=(rows // local_len,),
-        in_specs=[
-            rows_spec(local_len, D),
-            weight_spec(2, tp_parts),
-            weight_spec(3, tp_parts),
-        ],
-        out_specs=[rows_spec(local_len, width), rows_spec(local_len, D)],
+        grid=(width // step_width,),
+        in_specs=[all_rows(rows)] + chunk_specs(tp_parts),
+        out_specs=[step_spec, all_rows(rows)],
         out_shape=[shaped(rows, width, jnp.float32), shaped(rows, D, jnp.float32)],
-        scratch_shapes=[
-            pltpu.VMEM((D, width), jnp.bfloat16),
-            pltpu.VMEM((width, D), jnp.bfloat16),
-        ],
+        scratch_shapes=chunk_scratch(tp_parts),
         compiler_params=params(),
         cost_estimate=pl.CostEstimate(
             flops=rows * D * width * 4,
@@ -728,11 +779,8 @@
 def mlp_back_kernel(
     grad_mlp, hidden, up_tiles, down_tiles, activation, grad_hidden, partial, w_up, w_down
 ):
-    @pl.when(pl.program_id(0) == 0)
-    def _():
-        untile_into(w_up, up_tiles)
-        untile_into(w_down, down_tiles)
-
+    untile_into(w_up, up_tiles)
+    untile_into(w_down, down_tiles)
     values = hidden[...]
     factor = math.sqrt(2.0 / math.pi)
     square = values * values
@@ -744,35 +792,24 @@
     )
     grad = low(against_value(grad_mlp[...], w_down[...]) * slope)
     grad_hidden[...] = grad
-    partial[...] = against_value(grad, w_up[...])
+    add_to(partial, against_value(grad, w_up[...]))
 
 
 def mlp_back_call(grad_mlp, hidden, store, tp_parts, local_len):
     rows = grad_mlp.shape[0]
-    width = F // tp_parts
+    width, step_width = F // tp_parts, mlp_chunk(tp_parts)
+    step_spec = pl.BlockSpec((rows, step_width), lambda step: (0, step))
     return pl.pallas_call(
         mlp_back_kernel,
-        grid=(rows // local_len,),
-        in_specs=[
-            rows_spec(local_len, D),
-            rows_spec(local_len, width),
-            weight_spec(2, tp_parts),
-            weight_spec(3, tp_parts),
-        ],
-        out_specs=[
-            rows_spec(local_len, width),
-            rows_spec(local_len, width),
-            rows_spec(local_len, D),
-        ],
+        grid=(width // step_width,),
+        in_specs=[all_rows(rows), step_spec] + chunk_specs(tp_parts),
+        out_specs=[step_spec, step_spec, all_rows(rows)],
         out_shape=[
             shaped(rows, width, jnp.bfloat16),
             shaped(rows, width, jnp.bfloat16),
             shaped(rows, D, jnp.float32),
         ],
-        scratch_shapes=[
-            pltpu.VMEM((D, width), jnp.bfloat16),
-            pltpu.VMEM((width, D), jnp.bfloat16),
-        ],
+        scratch_shapes=chunk_scratch(tp_parts),
         compiler_params=params(),
         cost_estimate=pl.CostEstimate(
             flops=rows * D * width * 4,
@@ -846,24 +883,18 @@
 
 def weight_grad_call(lefts, rights, places, first_tile, held):
     height, breadth = lefts[0].shape[1], rights[0].shape[1]
-    width = 512 if breadth % 512 == 0 else breadth
-    steps = breadth // width
+    steps = min(4, height // B)
     count = len(lefts)
-    row_tiles, column_tiles, all_columns = height // B, width // B, breadth // B
+    row_tiles, column_tiles = height // B // steps, breadth // B
     amount = row_tiles * column_tiles
     given = [array for _, _, array in held if array is not None]
 
     def kernel(place, *refs):
         left_refs, right_refs = refs[:count], refs[count : 2 * count]
         outs = refs[2 * count + len(given) : 2 * count + len(given) + len(held)]
-        turned, ready, sem = refs[-2 - count : -2], refs[-2], refs[-1]
+        ready, sem = refs[-2], refs[-1]
         step = pl.program_id(0)
         slot = lax.rem(step, 2)
-
-        @pl.when(step == 0)
-        def _():
-            for turned_here, left in zip(turned, left_refs):
-                turned_here[...] = left[...].T
 
         def drain(which):
             pltpu.make_async_copy(
@@ -874,9 +905,9 @@
         def _():
             drain(slot)
 
-        block = product(turned[0][...], right_refs[0][...])
-        for turned_here, right in zip(turned[1:], right_refs[1:]):
-            block = block + product(turned_here[...], right[...])
+        block = over_rows(left_refs[0][...], right_refs[0][...])
+        for left, right in zip(left_refs[1:], right_refs[1:]):
+            block = block + over_rows(left[...], right[...])
         block = low(block)
         for row in range(row_tiles):
             for column in range(column_tiles):
@@ -885,8 +916,7 @@
                 ]
 
         def send(index, carry):
-            row, column = index // column_tiles, index % column_tiles
-            where_to = place[first_tile + row * all_columns + step * column_tiles + column]
+            where_to = place[first_tile + step * amount + index]
             for number, (begin, _, _) in enumerate(held):
                 end = held[number + 1][0] if number + 1 < len(held) else 1 << 30
                 copy = pltpu.make_async_copy(
@@ -909,9 +939,11 @@
     rows = [left.shape[0] for left in lefts]
     anywhere = pl.BlockSpec(memory_space=pl.ANY)
     in_specs = [
-        pl.BlockSpec((size, height), lambda step, place: (0, 0), pipeline_mode=pl.Buffered(1))
+        pl.BlockSpec((size, height // steps), lambda step, place: (0, step)) for size in rows
+    ] + [
+        pl.BlockSpec((size, breadth), lambda step, place: (0, 0), pipeline_mode=pl.Buffered(1))
         for size in rows
-    ] + [pl.BlockSpec((size, width), lambda step, place: (0, step)) for size in rows]
+    ]
     in_specs += [anywhere] * len(given)
     operands = [places, *lefts, *rights, *given]
     aliases = {}
@@ -925,8 +957,10 @@
             grid=(steps,),
             in_specs=in_specs,
             out_specs=[anywhere] * len(held),
-            scratch_shapes=[pltpu.VMEM((height, size), jnp.bfloat16) for size in rows]
-            + [pltpu.VMEM((2, amount, B, B), jnp.bfloat16), pltpu.SemaphoreType.DMA((2,))],
+            scratch_shapes=[
+                pltpu.VMEM((2, amount, B, B), jnp.bfloat16),
+                pltpu.SemaphoreType.DMA((2,)),
+            ],
         ),
         out_shape=[
             jax.ShapeDtypeStruct((places_here, B, B), jnp.bfloat16) for _, places_here, _ in held
@@ -1027,7 +1061,7 @@
     return (count + LOT - 1) // LOT
 
 
-def bring_strays(store, strays, count, owned_tiles, ordering, slots, me):
+def bring_strays(store, strays, count, owned_tiles, ordering, slots, me, tp_parts):
     def body(state):
         lot, held = state
         tiles = lax.dynamic_slice_in_dim(strays, lot * LOT, LOT, 0)
@@ -1036,7 +1070,7 @@
         mine = valid & (here // slots == me)
         sent = jnp.where(mine[:, None, None], owned_tiles[here % slots], 0)
         sent = chips_sum(sent)
-        at = jnp.where(valid, tiles, held.shape[0])
+        at = jnp.where(valid, store_of_tile(tiles, tp_parts), held.shape[0])
         return lot + 1, held.at[at].set(sent, mode="drop")
 
     return lax.while_loop(lambda state: state[0] < lots(count), body, (0, store))[1]
@@ -1157,33 +1191,29 @@
 
 def update_kernel(clip, grad, master, first, second, bases, master_out, first_out, second_out, low_out):
     eye = lax.broadcasted_iota(jnp.int32, (B, B), 0) == lax.broadcasted_iota(jnp.int32, (B, B), 1)
-    for tile in range(grad.shape[0]):
-        left_row = bases[tile, 0:1, :]
-        right_row = bases[tile, 1:2, :]
-        left_col = jnp.sum(jnp.where(eye, left_row, 0.0), 1, keepdims=True)
-        left_rate = 2.0 / jnp.sum(left_row * left_row, 1, keepdims=True)
-        right_rate = 2.0 / jnp.sum(right_row * right_row, 1, keepdims=True)
-        left_scaled = left_col * left_rate
-        right_scaled = right_row * right_rate
-
-        def turn(middle):
-            middle = middle - left_scaled * jnp.sum(left_col * middle, 0, keepdims=True)
-            return middle - jnp.sum(middle * right_row, 1, keepdims=True) * right_scaled
-
-        turned = turn(clip[0, 0] * grad[tile])
-        first_new = 0.5 * first[tile] + 0.5 * turned
-        second_new = 0.5 * second[tile] + 0.5 * turned * turned
-        direction = first_new / (jnp.sqrt(second_new) + 1e-08)
-        master_new = master[tile] - RATE * turn(direction)
-        master_out[tile] = master_new
-        first_out[tile] = first_new
-        second_out[tile] = second_new
-        low_out[tile] = master_new.astype(jnp.bfloat16)
+    left_row = bases[:, 0:1, :]
+    right_row = bases[:, 1:2, :]
+    left_col = jnp.sum(jnp.where(eye[None], left_row, 0.0), 2, keepdims=True)
+    left_scaled = left_col * (2.0 / jnp.sum(left_row * left_row, 2, keepdims=True))
+    right_scaled = right_row * (2.0 / jnp.sum(right_row * right_row, 2, keepdims=True))
+
+    def turn(middle):
+        middle = middle - left_scaled * jnp.sum(left_col * middle, 1, keepdims=True)
+        return middle - jnp.sum(middle * right_row, 2, keepdims=True) * right_scaled
+
+    turned = turn(clip[0, 0] * grad[...])
+    first_new = 0.5 * first[...] + 0.5 * turned
+    second_new = 0.5 * second[...] + 0.5 * turned * turned
+    first_out[...] = first_new
+    second_out[...] = second_new
+    master_new = master[...] - RATE * turn(first_new / (jnp.sqrt(second_new) + 1e-08))
+    master_out[...] = master_new
+    low_out[...] = master_new.astype(jnp.bfloat16)
 
 
 def update_tiles(clip_factor, grad, master, first, second, bases):
     slots = grad.shape[0]
-    amount = 3
+    amount = max(count for count in (1, 2, 3, 4, 6, 8) if slots % count == 0)
     tile_spec = pl.BlockSpec((amount, B, B), lambda step: (step, 0, 0))
     whole = jax.ShapeDtypeStruct(grad.shape, jnp.float32)
     return pl.pallas_call(
@@ -1244,7 +1274,7 @@
         place_early = early_place(owner, slot, early)
         place_late = late_place(owner, slot - early, slots - early)
         gather_places = jnp.where(is_early, place_early, 16 * early + place_late)
-        targets = jnp.argsort(gather_places).astype(jnp.int32)
+        targets = store_of_tile(jnp.argsort(gather_places), tp_parts).astype(jnp.int32)
         is_stray = jnp.logical_not(is_early) & (tile < per_layer)
         stray_count = jnp.sum(is_stray.astype(jnp.int32))
         stray_rank = jnp.cumsum(is_stray.astype(jnp.int32)) - 1
@@ -1277,13 +1307,17 @@
             tiles_low[0], early, place_early_tiles, place_late_tiles, else_low, targets
         )
         store = [
-            bring_strays(stores[0][2], strays, stray_count, tiles_low[0], inverse, slots, me),
+            bring_strays(
+                stores[0][2], strays, stray_count, tiles_low[0], inverse, slots, me, tp_parts
+            ),
             late_store[0][2],
         ]
         held = [(0, room, None), (room, 16 * (slots + 1) + LOT, None)]
     else:
         places = jnp.arange(all_tiles, dtype=jnp.int32)
-        gathered = lax.all_gather(tiles_low, ("fsdp", "ctx"), axis=1, tiled=True)[0][inverse]
+        tile_stored = jnp.argsort(store_of_tile(places, tp_parts))
+        gathered = lax.all_gather(tiles_low, ("fsdp", "ctx"), axis=1, tiled=True)[0]
+        gathered = gathered[inverse[tile_stored]]
         store = [gathered[:per_layer], gathered[per_layer:]]
         held = [(0, all_tiles, None)]
         else_parts = cut_else(gather_else(else_low, None, None))
@@ -1381,21 +1415,8 @@
         part = packed.shape[1] // 2
         return lax.dynamic_slice_in_dim(packed, tp_index * part, part, 1)
 
-    def every_image(columns):
-        if not box:
-            return gather_images(jnp.concatenate(columns, 1))
-        return columns_in(gather_images(image_part(columns)))
-
     label_column = jnp.broadcast_to(wide(labels)[:, None], (images, 128))
-    cuts = [128]
-    for length in (TFREQ, D, D):
-        cuts.append(cuts[-1] + length)
-    early_images = every_image(
-        [label_column, wide(features_low), wide(time_act), cond_wide, grad_final]
-    )
-    all_labels, all_features, all_time, all_cond, all_final = jnp.split(early_images, cuts, 1)
-    all_final = all_final[:, : 2 * D]
-    head_rows = total(grad_head).T.reshape(P_SIZE, D)
+    early_columns = [label_column, wide(features_low), wide(time_act), cond_wide, grad_final]
     grad_cond_act = 0.0
     for layer_no in reversed(range(L)):
         stream, row_sets, halves, branch, middle, mid_sets, hidden, mlp_out = kept[layer_no]
@@ -1414,6 +1435,8 @@
         upstream, mlp_sums, grad_low = back_call(
             middle, terms, upstream, modes[layer_no], 4, (branch, modes[layer_no], 2)
         )
+        if box and layer_no == 0:
+            late_sums = scatter_late(late_parts, slots - early, lanes, late_first, upstream)
         grad_sets = rows_in(grad_low.reshape(sp_rows, D))
         results, terms = each_half(
             lambda pair: attend_back_call(pair[0], pair[1], store[layer_no], tp_parts, local_len),
@@ -1445,9 +1468,16 @@
         if below:
             grad_low, gate_sum = found[2], found[1][:, 2:]
         if box and layer_no == L - 1:
-            grad_low = after(grad_low, held[0][2], held[1][2], early_images, head_rows)
+            grad_low = after(grad_low, held[0][2], held[1][2])
             lanes = Lanes()
-            late_sums = scatter_late(held[0][2], slots - early, lanes)
+            late_parts = held[0][2]
+            late_first = scatter_late_first(
+                late_parts,
+                slots - early,
+                lanes,
+                tp_sum(grad_head),
+                image_part(early_columns),
+            )
             held = held[1:]
     grad_patch = over_rows(noisy_rows, low(upstream).reshape(sp_rows, D))
     grad_cond_act = tp_sum(grad_cond_act) + against_low(grad_final, final_weight)
@@ -1456,19 +1486,24 @@
         against_low(grad_condition, time_second)
     )[0]
     if box:
-        patch_sum = tp_sum(grad_patch)
+        patch_sum = tp_sum(grad_patch).reshape(1, B, B)
         patch_first = low(patch_sum)
-        patch_part = jnp.where(tp_index == 0, patch_first, low(patch_sum - wide(patch_first)))
         parts = lax.dynamic_update_slice_in_dim(
             held[0][2],
-            patch_part.reshape(1, B, B),
+            jnp.where(tp_index == 0, patch_first, low(patch_sum - wide(patch_first))),
             early_place(0, early, early + 1),
             0,
         )
-        owned, owned_late, images_rows = scatter_early(
-            parts, early + 1, lanes, late_sums, image_part([grad_time_hidden, grad_condition])
-        )
-        late_images = columns_in(images_rows)
+        owned, owned_late, late_images, head_sum, early_images = scatter_early(
+            parts,
+            early + 1,
+            lanes,
+            *late_sums,
+            image_part([grad_time_hidden, grad_condition]),
+        )
+        late_images = columns_in(late_images)
+        early_images = columns_in(early_images)
+        head_rows = head_sum.T.reshape(P_SIZE, D)
         patch_rows = tp_sum(owned[early]).reshape(P_SIZE, D)
         owned = jnp.concatenate([owned[:early], owned_late], 0)
         owned = sum_strays(
@@ -1479,8 +1514,15 @@
             wide(held[0][2])[ordering], ("fsdp", "ctx"), scatter_dimension=0, tiled=True
         )
         patch_rows = lax.psum(grad_patch, ("fsdp", "ctx", "tp"))
-        late_images = every_image([grad_time_hidden, grad_condition])
+        head_rows = lax.psum(grad_head, ("fsdp", "ctx", "tp")).T.reshape(P_SIZE, D)
+        late_images = gather_images(jnp.concatenate([grad_time_hidden, grad_condition], 1))
+        early_images = gather_images(jnp.concatenate(early_columns, 1))
     all_hidden, all_condition = jnp.split(late_images, 2, 1)
+    cuts = [128]
+    for length in (TFREQ, D, D):
+        cuts.append(cuts[-1] + length)
+    all_labels, all_features, all_time, all_cond, all_final = jnp.split(early_images, cuts, 1)
+    all_final = all_final[:, : 2 * D]
     all_onehot = wide(all_labels[:, :1] == jnp.arange(NCLS, dtype=jnp.float32)[None, :])
     share = else_low.shape[0]
     device = (lax.axis_index("fsdp") * ctx_parts + lax.axis_index("ctx")) * tp_parts + tp_index

time: 1330 us -> 1260 us (0.947)
  Pallas kernels: 443 us -> 402 us
  waiting for transfers between devices: 391 us -> 373 us
    ppermute x26, waiting for transfers between devices: 89.2 us -> 68 us  [swap_y(): return lax.ppermute(value, 'ctx', [(0, 1), (1, 0)])]
    reshape x2 -> x3, local copies, waits for them, and re-layouts: 0.91 us -> 17.5 us  [the longest x1 15.6 us: cut_else(): rows = flat.reshape(-1, D)]
    another operation x4 -> x3, local copies, waits for them, and re-layouts: 15.7 us -> 0.79 us  [the longest x1 15.6 us: cut_else(): rows = flat.reshape(-1, D)]
    ppermute x40 -> x39, starting transfers between devices: 53.4 us -> 44.5 us  [swap_f(): lax.ppermute(value, 'fsdp', [(place, place ^ bit) for place in range(8)])]
    ppermute x40 -> x39, waiting for transfers between devices: 218 us -> 225 us  [swap_f(): lax.ppermute(value, 'fsdp', [(place, place ^ bit) for place in range(8)])]
    unnamed x259 -> x279, local copies, waits for them, and re-layouts: 29.5 us -> 24.7 us
    convert_element_type x17 -> x18, other arithmetic: 39.8 us -> 39.9 us  [low(): return value.astype(jnp.bfloat16)]
  transfers between devices with their start and end apart: 119 -> 118, of which waited for: 53 -> 48; matrix products, arithmetic and copies ran while one was open for 20% -> 21% of each run, Pallas kernels for 24% -> 22%
where the time goes in v3:
time: 1260 us; the launch traced here: 1250 us
  Pallas kernels  402 us (32%)
  waiting for transfers between devices  373 us (30%)
  local copies, waits for them, and re-layouts  173 us (14%)
  other arithmetic  142 us (11%)
  starting transfers between devices  127 us (10%)
  matrix products  22.5 us (2%)
    ppermute x39, waiting for transfers between devices, swap_f(): lax.ppermute(value, 'fsdp', [(place, place ^ bit) for place in range(8)])  225 us
    pallas_call x10, Pallas kernels, weight_grad_call(): pl.pallas_call(kernel, grid_spec=pltpu.PrefetchScalarGridSpec(num_scalar_...  83.3 us
    ppermute x26, waiting for transfers between devices, swap_y(): return lax.ppermute(value, 'ctx', [(0, 1), (1, 0)])  68 us
    ppermute x24, waiting for transfers between devices, move_z(): return lambda value: lax.ppermute(value, 'fsdp', pairs)  62.7 us
    pallas_call x4, Pallas kernels, attend_back_call(): pl.pallas_call(attend_back_kernel, grid=(rows // local_len,), in_specs=[r...  55.9 us
    pallas_call x10, Pallas kernels, rows_kernel_call(): pl.pallas_call(kernel, grid=(own,), in_specs=[rows] * len(wide_ins) + [fe...  52.5 us
    ppermute x24, starting transfers between devices, move_z(): return lambda value: lax.ppermute(value, 'fsdp', pairs)  52.3 us
    pallas_call x4, Pallas kernels, mlp_back_call(): pl.pallas_call(mlp_back_kernel, grid=(width // step_width,), in_specs=[al...  50.1 us
  transfers between devices with their start and end apart: 118, of which 48 were waited for; matrix products, arithmetic and copies ran while one was open for 21% of the time, Pallas kernels for 22%

profile of v3, /device:TPU:0, one launch (start us, length us, event | category | flops | bytes accessed | tf_op | source)
XLA Modules:
  0.0 1247.4 jit_solution(2706324994816158437)
XLA Ops:
  58.8 11.3 collective-permute-done.13
  81.7 15.3 %collective-permute-done.18 = bf16[4,1090,128]{2,0,1:T(4,128)(2,1)S(1)} collective-permute-done((bf16[4,1090,128]{2,0,1:T(4,128)(2,1)S(1)}, bf16[4,1090,128]{2,0,1:T(4,128)(2,1)S(1)}, u32[]{:S(2)}, u32[]{:S(2)}) %collective-permute-start.18) | collective-permute-done | bytes 1116192 | tf_op jit(solution)/shard_map/ppermute | solution.py:185
  121.7 10.2 copy.97
  141.3 29.0 %collective-permute-done.24.refs_2_ = bf16[46,128,128]{2,1,0:T(8,128)(2,1)} collective-permute-done((bf16[46,128,128]{2,1,0:T(8,128)(2,1)}, bf16[46,128,128]{2,1,0:T(8,128)(2,1)}, u32[]{:S(2)}, u32[]{:S(2)}) %collective-permute-start.24) | collective-permute-done | bytes 1507360 | tf_op jit(solution)/shard_map/ppermute | solution.py:185
  216.8 26.7 %collective-permute-done.32.refs_2_ = bf16[46,128,128]{2,1,0:T(8,128)(2,1)S(1)} collective-permute-done((bf16[46,128,128]{2,1,0:T(8,128)(2,1)S(1)}, bf16[46,128,128]{2,1,0:T(8,128)(2,1)S(1)}, u32[]{:S(2)}, u32[]{:S(2)}) %collective-permute-start.32) | collective-permute-done | bytes 1507360 | tf_op jit(solution)/shard_map/ppermute | solution.py:185
  259.9 15.6 %reshape.490 = bf16[4360,1024]{1,0:T(8,128)(2,1)} reshape(bf16[4,2,2,2,1090,128]{5,4,3,2,1,0:T(8,128)(2,1)} %copy.100) | data formatting | bytes 17858560 | tf_op jit(solution)/shard_map/reshape | solution.py:497
  386.4 49.8 %collective-permute-done.49.refs_1_ = bf16[104,128,128]{2,1,0:T(8,128)(2,1)S(1)} collective-permute-done((bf16[104,128,128]{2,1,0:T(8,128)(2,1)S(1)}, bf16[104,128,128]{2,1,0:T(8,128)(2,1)S(1)}, u32[]{:S(2)}, u32[]{:S(2)}) %collective-permute-start.49) | collective-permute-done | bytes 3407904 | tf_op jit(solution)/shard_map/ppermute | solution.py:185
  443.2 10.6 shard_map.223
  465.2 14.2 %collective-permute-done.51.refs_0_ = bf16[52,128,128]{2,1,0:T(8,128)(2,1)S(1)} collective-permute-done((bf16[52,128,128]{2,1,0:T(8,128)(2,1)}, bf16[52,128,128]{2,1,0:T(8,128)(2,1)S(1)}, u32[]{:S(2)}, u32[]{:S(2)}) %collective-permute-start.51) | collective-permute-done | bytes 1703968 | tf_op jit(solution)/shard_map/ppermute | solution.py:181
  491.0 10.6 shard_map.222
  512.3 9.0 shard_map.230
  540.9 10.6 shard_map.233
  553.0 10.5 shard_map.232
  582.4 12.4 shard_map.237
  595.3 12.5 %shard_map.236 = (bf16[512,2048]{1,0:T(8,128)(2,1)}, bf16[512,2048]{1,0:T(8,128)(2,1)}, f32[512,1024]{1,0:T(8,128)}) custom-call(bf16[512,1024]{1,0:T(8,128)(2,1)} %bitcast.195, f32[512,2048]{1,0:T(8,128)} %get-tuple-element.506.hidden, bf16[577,128,128]{2,1,0:T(8,128)(2,1)} %get-tuple-element.493.tile_set.qkv_tiles.proj_tiles.up_tiles.down_tiles, ...), custom_call_target="tpu_custom_call" | custom-call | flops 4294967296 | bytes 16777216 | tf_op jit(solution)/shard_map/pallas_call | solution.py:802
  619.8 13.8 %shard_map.240 = (bf16[512,1536]{1,0:T(8,128)(2,1)}, f32[512,1024]{1,0:T(8,128)}) custom-call(bf16[512,1024]{1,0:T(8,128)(2,1)} %copy-done.22, bf16[512,1536]{1,0:T(8,128)(2,1)} %get-tuple-element.515.projected, bf16[577,128,128]{2,1,0:T(8,128)(2,1)} %get-tuple-element.493.tile_set.qkv_tiles.proj_tiles.up_tiles.down_tiles, ...), custom_call_target="tpu_custom_call" | custom-call | flops 2684354560 | bytes 4194304 | tf_op jit(solution)/shard_map/pallas_call | solution.py:688
  634.4 10.4 shard_map.242
  644.8 10.6 shard_map.243
  655.5 13.8 %shard_map.239 = (bf16[512,1536]{1,0:T(8,128)(2,1)}, f32[512,1024]{1,0:T(8,128)}) custom-call(bf16[512,1024]{1,0:T(8,128)(2,1)} %bitcast.172, bf16[512,1536]{1,0:T(8,128)(2,1)} %get-tuple-element.513.projected, bf16[577,128,128]{2,1,0:T(8,128)(2,1)} %get-tuple-element.493.tile_set.qkv_tiles.proj_tiles.up_tiles.down_tiles, ...), custom_call_target="tpu_custom_call" | custom-call | flops 2684354560 | bytes 4194304 | tf_op jit(solution)/shard_map/pallas_call | solution.py:688
  705.4 12.7 %shard_map.248 = (bf16[512,2048]{1,0:T(8,128)(2,1)}, bf16[512,2048]{1,0:T(8,128)(2,1)}, f32[512,1024]{1,0:T(8,128)}) custom-call(bf16[512,1024]{1,0:T(8,128)(2,1)} %copy-done.21, f32[512,2048]{1,0:T(8,128)} %get-tuple-element.544.hidden, bf16[577,128,128]{2,1,0:T(8,128)(2,1)} %get-tuple-element.479.tile_set.qkv_tiles.proj_tiles.up_tiles.down_tiles, ...), custom_call_target="tpu_custom_call" | custom-call | flops 4294967296 | bytes 16777216 | tf_op jit(solution)/shard_map/pallas_call | solution.py:802
  724.1 12.4 shard_map.247
  760.2 14.0 %shard_map.251 = (bf16[512,1536]{1,0:T(8,128)(2,1)}, f32[512,1024]{1,0:T(8,128)}) custom-call(bf16[512,1024]{1,0:T(8,128)(2,1)} %collective-permute-done.65.grad_branch.refs_3_, bf16[512,1536]{1,0:T(8,128)(2,1)} %get-tuple-element.551.projected, bf16[577,128,128]{2,1,0:T(8,128)(2,1)} %get-tuple-element.479.tile_set.qkv_tiles.proj_tiles.up_tiles.down_tiles, ...), custom_call_target="tpu_custom_call" | custom-call | flops 2684354560 | bytes 4194304 | tf_op jit(solution)/shard_map/pallas_call | solution.py:688
  775.3 16.9 %collective-permute-done.72 = f32[16,1024]{1,0:T(8,128)S(1)} collective-permute-done((f32[16,1024]{1,0:T(8,128)S(1)}, f32[16,1024]{1,0:T(8,128)S(1)}, u32[]{:S(2)}, u32[]{:S(2)}) %collective-permute-start.72) | collective-permute-done | bytes 65568 | tf_op jit(solution)/shard_map/ppermute | solution.py:181
  792.3 9.6 shard_map.253.refs_4_
  801.9 10.1 shard_map.254.refs_4_
  822.4 14.2 %shard_map.250 = (bf16[512,1536]{1,0:T(8,128)(2,1)}, f32[512,1024]{1,0:T(8,128)}) custom-call(bf16[512,1024]{1,0:T(8,128)(2,1)} %bitcast.179, bf16[512,1536]{1,0:T(8,128)(2,1)} %get-tuple-element.549.projected, bf16[577,128,128]{2,1,0:T(8,128)(2,1)} %get-tuple-element.479.tile_set.qkv_tiles.proj_tiles.up_tiles.down_tiles, ...), custom_call_target="tpu_custom_call" | custom-call | flops 2684354560 | bytes 4194304 | tf_op jit(solution)/shard_map/pallas_call | solution.py:688
  892.2 20.4 %collective-permute-done.79 = bf16[104,128,128]{2,1,0:T(8,128)(2,1)S(1)} collective-permute-done((bf16[104,128,128]{2,1,0:T(8,128)(2,1)}, bf16[104,128,128]{2,1,0:T(8,128)(2,1)S(1)}, u32[]{:S(2)}, u32[]{:S(2)}) %collective-permute-start.79) | collective-permute-done | bytes 3407904 | tf_op jit(solution)/shard_map/ppermute | solution.py:185
  925.8 14.4 %collective-permute-done.85 = bf16[26,128,128]{2,1,0:T(8,128)(2,1)S(1)} collective-permute-done((bf16[26,128,128]{2,1,0:T(8,128)(2,1)S(1)}, bf16[26,128,128]{2,1,0:T(8,128)(2,1)S(1)}, u32[]{:S(2)}, u32[]{:S(2)}) %collective-permute-start.85) | collective-permute-done | bytes 852000 | tf_op jit(solution)/shard_map/ppermute | solution.py:220
  996.9 16.2 %collective-permute-done.94 = bf16[26,128,128]{2,1,0:T(8,128)(2,1)S(1)} collective-permute-done((bf16[26,128,128]{2,1,0:T(8,128)(2,1)S(1)}, bf16[26,128,128]{2,1,0:T(8,128)(2,1)S(1)}, u32[]{:S(2)}, u32[]{:S(2)}) %collective-permute-start.94) | collective-permute-done | bytes 852000 | tf_op jit(solution)/shard_map/ppermute | solution.py:220
  1065.8 13.1 %slice.455 = bf16[432,128,128]{2,1,0:T(8,128)(2,1)} slice(bf16[1184,128,128]{2,1,0:T(8,128)(2,1)} %fusion.51), slice={[752:1184], [0:128], [0:128]} | slice | bytes 28311552 | tf_op jit(solution)/shard_map/slice | solution.py:1510
  1126.5 18.6 %collective-permute-done.110 = bf16[47,128,128]{2,1,0:T(8,128)(2,1)S(1)} collective-permute-done((bf16[47,128,128]{2,1,0:T(8,128)(2,1)S(1)}, bf16[47,128,128]{2,1,0:T(8,128)(2,1)S(1)}, u32[]{:S(2)}, u32[]{:S(2)}) %collective-permute-start.110) | collective-permute-done | bytes 1540128 | tf_op jit(solution)/shard_map/ppermute | solution.py:185
  1228.4 17.5 %shard_map.260 = (f32[72,128,128]{2,1,0:T(8,128)}, f32[72,128,128]{2,1,0:T(8,128)}, f32[72,128,128]{2,1,0:T(8,128)}, bf16[72,128,128]{2,1,0:T(8,128)(2,1)}) custom-call(f32[1,1]{1,0:T(1,128)} %bitcast.58.clip, f32[72,128,128]{2,1,0:T(8,128)} %get-tuple-element.611.grad, f32[72,128,128]{2,1,0:T(8,128)} %bitcast.156, f32[72,128,128]{2,1,0:T(8,128)} %bitcast.157, ...), custom_call_target="tpu_custom_call" | custom-call | flops 35389440 | bytes 35389440 | tf_op jit(solution)/shard_map/pallas_call | solution.py:1219
  (752 shorter events, 753.0 us)
Async XLA Ops:
  2.2 36.0 %collective-permute-start.8 = (bf16[46,128,128]{2,1,0:T(8,128)(2,1)S(1)}, bf16[46,128,128]{2,1,0:T(8,128)(2,1)S(1)}, u32[]{:S(2)}, u32[]{:S(2)}) collective-permute-start(bf16[46,128,128]{2,1,0:T(8,128)(2,1)S(1)} %slice_bitcast_fusion.refs_0_), channel_id=1, source_target_pairs={{0,4},{4,0},{8,12},{12,8},{16,20},{20,16},{24,28},{28,24},{1,5},{5... | collective-permute-start | bytes 4521992 | tf_op jit(solution)/shard_map/ppermute | solution.py:185
  5.2 34.6 %collective-permute-start.9 = (bf16[46,128,128]{2,1,0:T(8,128)(2,1)S(1)}, bf16[46,128,128]{2,1,0:T(8,128)(2,1)}, u32[]{:S(2)}, u32[]{:S(2)}) collective-permute-start(bf16[46,128,128]{2,1,0:T(8,128)(2,1)S(1)} %slice_bitcast_fusion.refs_0_), channel_id=1, source_target_pairs={{0,2},{2,0},{1,3},{3,1},{4,6},{6,4},{5,7},{7,5},{8,10},{10,8},{9,1... | collective-permute-start | bytes 4521992 | tf_op jit(solution)/shard_map/ppermute | solution.py:181
  6.7 35.1 %collective-permute-start.10 = (bf16[46,128,128]{2,1,0:T(8,128)(2,1)S(1)}, bf16[46,128,128]{2,1,0:T(8,128)(2,1)}, u32[]{:S(2)}, u32[]{:S(2)}) collective-permute-start(bf16[46,128,128]{2,1,0:T(8,128)(2,1)S(1)} %slice_bitcast_fusion.refs_0_), channel_id=1, source_target_pairs={{0,8},{4,12},{8,16},{12,20},{16,24},{20,28},{1,9},{5,13},{9,17},{1... | collective-permute-start | bytes 4521992 | tf_op jit(solution)/shard_map/ppermute | solution.py:220
  11.3 35.9 %collective-permute-start.11 = (bf16[46,128,128]{2,1,0:T(8,128)(2,1)S(1)}, bf16[46,128,128]{2,1,0:T(8,128)(2,1)}, u32[]{:S(2)}, u32[]{:S(2)}) collective-permute-start(bf16[46,128,128]{2,1,0:T(8,128)(2,1)S(1)} %slice_bitcast_fusion.refs_0_), channel_id=1, source_target_pairs={{8,0},{12,4},{16,8},{20,12},{24,16},{28,20},{9,1},{13,5},{17,9},{2... | collective-permute-start | bytes 4521992 | tf_op jit(solution)/shard_map/ppermute | solution.py:220
  131.9 60.2 %collective-permute-start.21 = (bf16[4,2,2,1090,128]{4,0,3,2,1:T(4,128)(2,1)}, bf16[4,2,2,1090,128]{4,0,3,2,1:T(4,128)(2,1)}, u32[]{:S(2)}, u32[]{:S(2)}) collective-permute-start(bf16[4,2,2,1090,128]{4,0,3,2,1:T(4,128)(2,1)} %copy.97), channel_id=1, source_target_pairs={{0,1},{1,0},{2,3},{3,2},{4,5},{5,4},{6,7},{7,6},{8,9},{9,8},{10,11... | collective-permute-start | bytes 13393928 | tf_op jit(solution)/shard_map/ppermute | solution.py:177
  134.6 35.7 %collective-permute-start.24 = (bf16[46,128,128]{2,1,0:T(8,128)(2,1)}, bf16[46,128,128]{2,1,0:T(8,128)(2,1)}, u32[]{:S(2)}, u32[]{:S(2)}) collective-permute-start(bf16[46,128,128]{2,1,0:T(8,128)(2,1)} %broadcast_select_fusion.1.refs_0_), channel_id=1, source_target_pairs={{0,4},{4,0},{8,12},{12,8},{16,20},{20,16},{24,28},{28,24},{1,5},{5... | collective-permute-start | bytes 4521992 | tf_op jit(solution)/shard_map/ppermute | solution.py:185
  136.1 36.4 %collective-permute-start.25 = (bf16[46,128,128]{2,1,0:T(8,128)(2,1)}, bf16[46,128,128]{2,1,0:T(8,128)(2,1)}, u32[]{:S(2)}, u32[]{:S(2)}) collective-permute-start(bf16[46,128,128]{2,1,0:T(8,128)(2,1)} %broadcast_select_fusion.1.refs_0_), channel_id=1, source_target_pairs={{0,2},{2,0},{1,3},{3,1},{4,6},{6,4},{5,7},{7,5},{8,10},{10,8},{9,1... | collective-permute-start | bytes 4521992 | tf_op jit(solution)/shard_map/ppermute | solution.py:181
  137.0 37.6 %collective-permute-start.22 = (bf16[46,128,128]{2,1,0:T(8,128)(2,1)}, bf16[46,128,128]{2,1,0:T(8,128)(2,1)}, u32[]{:S(2)}, u32[]{:S(2)}) collective-permute-start(bf16[46,128,128]{2,1,0:T(8,128)(2,1)} %collective-permute-done.10), channel_id=1, source_target_pairs={{8,16},{12,20},{16,24},{20,28},{9,17},{13,21},{17,25},{21,29},{10,... | collective-permute-start | bytes 4521992 | tf_op jit(solution)/shard_map/ppermute | solution.py:220
  138.8 42.9 %collective-permute-start.23 = (bf16[46,128,128]{2,1,0:T(8,128)(2,1)}, bf16[46,128,128]{2,1,0:T(8,128)(2,1)}, u32[]{:S(2)}, u32[]{:S(2)}) collective-permute-start(bf16[46,128,128]{2,1,0:T(8,128)(2,1)} %collective-permute-done.11), channel_id=1, source_target_pairs={{8,0},{12,4},{16,8},{20,12},{9,1},{13,5},{17,9},{21,13},{10,2},{14... | collective-permute-start | bytes 4521992 | tf_op jit(solution)/shard_map/ppermute | solution.py:220
  211.6 31.9 %collective-permute-start.32 = (bf16[46,128,128]{2,1,0:T(8,128)(2,1)S(1)}, bf16[46,128,128]{2,1,0:T(8,128)(2,1)S(1)}, u32[]{:S(2)}, u32[]{:S(2)}) collective-permute-start(bf16[46,128,128]{2,1,0:T(8,128)(2,1)S(1)} %copy-done.13), channel_id=1, source_target_pairs={{0,4},{4,0},{8,12},{12,8},{16,20},{20,16},{24,28},{28,24},{1,5},{5... | collective-permute-start | bytes 4521992 | tf_op jit(solution)/shard_map/ppermute | solution.py:185
  213.7 33.5 %collective-permute-start.30 = (bf16[46,128,128]{2,1,0:T(8,128)(2,1)}, bf16[46,128,128]{2,1,0:T(8,128)(2,1)}, u32[]{:S(2)}, u32[]{:S(2)}) collective-permute-start(bf16[46,128,128]{2,1,0:T(8,128)(2,1)} %collective-permute-done.23), channel_id=1, source_target_pairs={{8,0},{12,4},{9,1},{13,5},{10,2},{14,6},{11,3},{15,7}} | collective-permute-start | bytes 4521992 | tf_op jit(solution)/shard_map/ppermute | solution.py:220
  215.0 32.3 %collective-permute-start.31 = (bf16[46,128,128]{2,1,0:T(8,128)(2,1)}, bf16[46,128,128]{2,1,0:T(8,128)(2,1)}, u32[]{:S(2)}, u32[]{:S(2)}) collective-permute-start(bf16[46,128,128]{2,1,0:T(8,128)(2,1)} %collective-permute-done.22), channel_id=1, source_target_pairs={{16,24},{20,28},{17,25},{21,29},{18,26},{22,30},{19,27},{23,31}} | collective-permute-start | bytes 4521992 | tf_op jit(solution)/shard_map/ppermute | solution.py:220
  247.2 43.2 %collective-permute-start.34 = (bf16[26,128,128]{2,1,0:T(8,128)(2,1)}, bf16[26,128,128]{2,1,0:T(8,128)(2,1)}, u32[]{:S(2)}, u32[]{:S(2)}) collective-permute-start(bf16[26,128,128]{2,1,0:T(8,128)(2,1)} %collective-permute-done.28), channel_id=1, source_target_pairs={{8,16},{12,20},{16,24},{20,28},{9,17},{13,21},{17,25},{21,29},{10,... | collective-permute-start | bytes 2555912 | tf_op jit(solution)/shard_map/ppermute | solution.py:220
  248.8 41.7 %collective-permute-start.35 = (bf16[26,128,128]{2,1,0:T(8,128)(2,1)}, bf16[26,128,128]{2,1,0:T(8,128)(2,1)}, u32[]{:S(2)}, u32[]{:S(2)}) collective-permute-start(bf16[26,128,128]{2,1,0:T(8,128)(2,1)} %collective-permute-done.29), channel_id=1, source_target_pairs={{8,0},{12,4},{16,8},{20,12},{9,1},{13,5},{17,9},{21,13},{10,2},{14... | collective-permute-start | bytes 2555912 | tf_op jit(solution)/shard_map/ppermute | solution.py:220
  250.1 40.4 %collective-permute-start.36 = (bf16[23,128,128]{2,1,0:T(8,128)(2,1)}, bf16[23,128,128]{2,1,0:T(8,128)(2,1)}, u32[]{:S(2)}, u32[]{:S(2)}) collective-permute-start(bf16[23,128,128]{2,1,0:T(8,128)(2,1)} %slice.400), channel_id=1, source_target_pairs={{0,2},{2,0},{1,3},{3,1},{4,6},{6,4},{5,7},{7,5},{8,10},{10,8},{9,1... | collective-permute-start | bytes 2261000 | tf_op jit(solution)/shard_map/ppermute | solution.py:181
  251.6 38.9 %collective-permute-start.37 = (bf16[23,128,128]{2,1,0:T(8,128)(2,1)}, bf16[23,128,128]{2,1,0:T(8,128)(2,1)}, u32[]{:S(2)}, u32[]{:S(2)}) collective-permute-start(bf16[23,128,128]{2,1,0:T(8,128)(2,1)} %slice.401), channel_id=1, source_target_pairs={{0,4},{4,0},{8,12},{12,8},{16,20},{20,16},{24,28},{28,24},{1,5},{5... | collective-permute-start | bytes 2261000 | tf_op jit(solution)/shard_map/ppermute | solution.py:185
  360.5 75.7 %collective-permute-start.49 = (bf16[104,128,128]{2,1,0:T(8,128)(2,1)S(1)}, bf16[104,128,128]{2,1,0:T(8,128)(2,1)S(1)}, u32[]{:S(2)}, u32[]{:S(2)}) collective-permute-start(bf16[104,128,128]{2,1,0:T(8,128)(2,1)S(1)} %pad_maximum_fusion.3.refs_0_), channel_id=1, source_target_pairs={{0,4},{4,0},{8,12},{12,8},{16,20},{20,16},{24,28},{28,24},{1,5},{5... | collective-permute-start | bytes 10223624 | tf_op jit(solution)/shard_map/ppermute | solution.py:185
  360.7 77.1 %collective-permute-start.50 = (bf16[104,128,128]{2,1,0:T(8,128)(2,1)S(1)}, bf16[104,128,128]{2,1,0:T(8,128)(2,1)}, u32[]{:S(2)}, u32[]{:S(2)}) collective-permute-start(bf16[104,128,128]{2,1,0:T(8,128)(2,1)S(1)} %pad_maximum_fusion.3.refs_0_), channel_id=1, source_target_pairs={{0,2},{2,0},{1,3},{3,1},{4,6},{6,4},{5,7},{7,5},{8,10},{10,8},{9,1... | collective-permute-start | bytes 10223624 | tf_op jit(solution)/shard_map/ppermute | solution.py:181
  385.9 56.3 %collective-permute-start.47 = (bf16[512,1024]{1,0:T(8,128)(2,1)}, bf16[512,1024]{1,0:T(8,128)(2,1)S(1)}, u32[]{:S(2)}, u32[]{:S(2)}) collective-permute-start(bf16[512,1024]{1,0:T(8,128)(2,1)} %bitcast.159), channel_id=1, source_target_pairs={{0,1},{1,0},{2,3},{3,2},{4,5},{5,4},{6,7},{7,6},{8,9},{9,8},{10,11... | collective-permute-start | bytes 3145736 | tf_op jit(solution)/shard_map/ppermute | solution.py:177
  440.8 38.6 %collective-permute-start.51 = (bf16[52,128,128]{2,1,0:T(8,128)(2,1)}, bf16[52,128,128]{2,1,0:T(8,128)(2,1)S(1)}, u32[]{:S(2)}, u32[]{:S(2)}) collective-permute-start(bf16[52,128,128]{2,1,0:T(8,128)(2,1)} %slice.406), channel_id=1, source_target_pairs={{0,2},{2,0},{1,3},{3,1},{4,6},{6,4},{5,7},{7,5},{8,10},{10,8},{9,1... | collective-permute-start | bytes 5111816 | tf_op jit(solution)/shard_map/ppermute | solution.py:181
  441.6 38.3 %collective-permute-start.52 = (bf16[52,128,128]{2,1,0:T(8,128)(2,1)}, bf16[52,128,128]{2,1,0:T(8,128)(2,1)S(1)}, u32[]{:S(2)}, u32[]{:S(2)}) collective-permute-start(bf16[52,128,128]{2,1,0:T(8,128)(2,1)} %slice.407), channel_id=1, source_target_pairs={{0,4},{4,0},{8,12},{12,8},{16,20},{20,16},{24,28},{28,24},{1,5},{5... | collective-permute-start | bytes 5111816 | tf_op jit(solution)/shard_map/ppermute | solution.py:185
  453.7 48.5 %collective-permute-start.48 = (f32[512,1024]{1,0:T(8,128)}, f32[512,1024]{1,0:T(8,128)S(1)}, u32[]{:S(2)}, u32[]{:S(2)}) collective-permute-start(f32[512,1024]{1,0:T(8,128)} %get-tuple-element.485), channel_id=1, source_target_pairs={{0,1},{1,0},{2,3},{3,2},{4,5},{5,4},{6,7},{7,6},{8,9},{9,8},{10,11... | collective-permute-start | bytes 6291464 | tf_op jit(solution)/shard_map/ppermute | solution.py:177
  633.6 41.4 %collective-permute-start.61 = (f32[512,1024]{1,0:T(8,128)}, f32[512,1024]{1,0:T(8,128)S(1)}, u32[]{:S(2)}, u32[]{:S(2)}) collective-permute-start(f32[512,1024]{1,0:T(8,128)} %get-tuple-element.516), channel_id=1, source_target_pairs={{0,1},{1,0},{2,3},{3,2},{4,5},{5,4},{6,7},{7,6},{8,9},{9,8},{10,11... | collective-permute-start | bytes 6291464 | tf_op jit(solution)/shard_map/ppermute | solution.py:177
  751.2 60.9 %collective-permute-start.73 = (bf16[52,128,128]{2,1,0:T(8,128)(2,1)}, bf16[52,128,128]{2,1,0:T(8,128)(2,1)}, u32[]{:S(2)}, u32[]{:S(2)}) collective-permute-start(bf16[52,128,128]{2,1,0:T(8,128)(2,1)} %get-tuple-element.566), channel_id=1, source_target_pairs={{0,2},{2,0},{1,3},{3,1},{4,6},{6,4},{5,7},{7,5},{8,10},{10,8},{9,1... | collective-permute-start | bytes 5111816 | tf_op jit(solution)/shard_map/ppermute | solution.py:181
  752.3 59.7 %collective-permute-start.74 = (bf16[52,128,128]{2,1,0:T(8,128)(2,1)}, bf16[52,128,128]{2,1,0:T(8,128)(2,1)}, u32[]{:S(2)}, u32[]{:S(2)}) collective-permute-start(bf16[52,128,128]{2,1,0:T(8,128)(2,1)} %get-tuple-element.567), channel_id=1, source_target_pairs={{0,4},{4,0},{8,12},{12,8},{16,20},{20,16},{24,28},{28,24},{1,5},{5... | collective-permute-start | bytes 5111816 | tf_op jit(solution)/shard_map/ppermute | solution.py:185
  775.2 74.9 %collective-permute-start.66 = (f32[512,1024]{1,0:T(8,128)}, f32[512,1024]{1,0:T(8,128)}, u32[]{:S(2)}, u32[]{:S(2)}) collective-permute-start(f32[512,1024]{1,0:T(8,128)} %get-tuple-element.552), channel_id=1, source_target_pairs={{0,1},{1,0},{2,3},{3,2},{4,5},{5,4},{6,7},{7,6},{8,9},{9,8},{10,11... | collective-permute-start | bytes 6291464 | tf_op jit(solution)/shard_map/ppermute | solution.py:177
  837.8 74.8 %collective-permute-start.79 = (bf16[104,128,128]{2,1,0:T(8,128)(2,1)}, bf16[104,128,128]{2,1,0:T(8,128)(2,1)S(1)}, u32[]{:S(2)}, u32[]{:S(2)}) collective-permute-start(bf16[104,128,128]{2,1,0:T(8,128)(2,1)} %pad_maximum_fusion.4), channel_id=1, source_target_pairs={{0,4},{4,0},{8,12},{12,8},{16,20},{20,16},{24,28},{28,24},{1,5},{5... | collective-permute-start | bytes 10223624 | tf_op jit(solution)/shard_map/ppermute | solution.py:185
  839.2 74.6 %collective-permute-start.80 = (bf16[104,128,128]{2,1,0:T(8,128)(2,1)}, bf16[104,128,128]{2,1,0:T(8,128)(2,1)}, u32[]{:S(2)}, u32[]{:S(2)}) collective-permute-start(bf16[104,128,128]{2,1,0:T(8,128)(2,1)} %pad_maximum_fusion.5), channel_id=1, source_target_pairs={{0,2},{2,0},{1,3},{3,1},{4,6},{6,4},{5,7},{7,5},{8,10},{10,8},{9,1... | collective-permute-start | bytes 10223624 | tf_op jit(solution)/shard_map/ppermute | solution.py:181
  1042.7 36.2 %collective-permute-start.119 = (f32[64,2304]{1,0:T(8,128)S(1)}, f32[64,2304]{1,0:T(8,128)S(1)}, u32[]{:S(2)}, u32[]{:S(2)}) collective-permute-start(f32[64,2304]{1,0:T(8,128)S(1)} %copy-done.65), channel_id=1, source_target_pairs={{0,1},{1,0},{2,3},{3,2},{4,5},{5,4},{6,7},{7,6},{8,9},{9,8},{10,11... | collective-permute-start | bytes 1769480 | tf_op jit(solution)/shard_map/ppermute | solution.py:177
  1056.1 36.6 %collective-permute-start.103 = (bf16[47,128,128]{2,1,0:T(8,128)(2,1)}, bf16[47,128,128]{2,1,0:T(8,128)(2,1)}, u32[]{:S(2)}, u32[]{:S(2)}) collective-permute-start(bf16[47,128,128]{2,1,0:T(8,128)(2,1)} %pad_maximum_fusion.8), channel_id=1, source_target_pairs={{0,4},{4,0},{8,12},{12,8},{16,20},{20,16},{24,28},{28,24},{1,5},{5... | collective-permute-start | bytes 4620296 | tf_op jit(solution)/shard_map/ppermute | solution.py:185
  1056.4 36.4 %collective-permute-start.104 = (bf16[47,128,128]{2,1,0:T(8,128)(2,1)}, bf16[47,128,128]{2,1,0:T(8,128)(2,1)}, u32[]{:S(2)}, u32[]{:S(2)}) collective-permute-start(bf16[47,128,128]{2,1,0:T(8,128)(2,1)} %pad_maximum_fusion.9), channel_id=1, source_target_pairs={{0,2},{2,0},{1,3},{3,1},{4,6},{6,4},{5,7},{7,5},{8,10},{10,8},{9,1... | collective-permute-start | bytes 4620296 | tf_op jit(solution)/shard_map/ppermute | solution.py:181
  1057.4 35.4 %collective-permute-start.105 = (bf16[47,128,128]{2,1,0:T(8,128)(2,1)}, bf16[47,128,128]{2,1,0:T(8,128)(2,1)}, u32[]{:S(2)}, u32[]{:S(2)}) collective-permute-start(bf16[47,128,128]{2,1,0:T(8,128)(2,1)} %fusion.15), channel_id=1, source_target_pairs={{0,8},{4,12},{1,9},{5,13},{2,10},{6,14},{3,11},{7,15}} | collective-permute-start | bytes 4620296 | tf_op jit(solution)/shard_map/ppermute | solution.py:220
  (223 other events, 2983.1 us)

commit v4 on v3

--- a/solution.py
+++ b/solution.py
@@ -239,8 +239,10 @@
         self.above.append(arrived[0])
         self.below.append(arrived[1])
 
-    def block(self, rel):
+    def block(self, rel, token=None):
         z = place_z()
+        if token is not None:
+            z = z + token[0, 0]
         above, below = self.above, self.below
         if rel == 0:
             return above[0]
@@ -281,34 +283,37 @@
 
 
 def early_slots(slots):
-    return slots - slots * 13 // 36
+    return slots - slots * 25 // 72
 
 
 def gather_tiles(own, early, place_early, place_late, else_low, targets):
     half = early // 2
     lanes = Lanes()
     line, late_line = ZLine(own[:early]), ZLine(own[early:])
-    rest = None
-    token = ()
+    rest = whole = None
+    tokens = []
     for rel in range(4):
-        block = line.block(rel)
+        block = line.block(rel, tokens[rel - 2] if rel >= 2 else None)
         sends = [(swap_x, block), (swap_y, block)]
-        waits = token
-        if rel == 2:
-            waits += (whole,)
-        elif rel == 3:
-            waits += rest
+        waits = ()
+        if rel == 3:
+            waits = rest[0]
         going = line if rel < 3 else late_line
-        by_x, by_y, *arrived = lanes.step(sends + going.sends(), *waits)
-        going.take(arrived)
+        sends += going.sends()
+        if rel == 1:
+            by_x, by_y, above, below, *both = lanes.step(sends + else_diagonal)
+            whole = finish_else(else_line, both)
+            rest = cut_else(whole)
+        else:
+            by_x, by_y, above, below = lanes.step(sends, *waits)
+        going.take((above, below))
         sends = [(swap_y, by_x[:half]), (swap_x, by_y[half:])]
         if rel == 0:
             first, second, *arrived = lanes.step(
                 sends + [(to_z(other), else_low.reshape(1, -1, 128)) for other in (1, 2, 3)],
                 targets,
             )
-            whole = gather_else(else_low, lanes, arrived)
-            rest = cut_else(whole)
+            else_line, else_diagonal = start_else(else_low, lanes, arrived)
         elif rel < 3:
             first, second, *arrived = lanes.step(sends + late_line.sends())
             late_line.take(arrived)
@@ -322,16 +327,19 @@
             (first, at + 3 * early),
             (second, at + 3 * early + half),
         ]
-        token = (place_early(group),)
+        tokens.append(place_early(group))
     line = jnp.concatenate([late_line.block(rel) for rel in range(4)], 0)
     count = line.shape[0]
     half = count // 2
     by_x, by_y = lanes.step([(swap_x, line), (swap_y, line)])
-    token = place_late([(line, 0)])
-    first, second = lanes.step([(swap_y, by_x[:half]), (swap_x, by_y[half:])], token)
-    place_late([(by_y, count), (by_x, 2 * count)])
-    place_late([(first, 3 * count), (second, 3 * count + half)])
-    return rest
+    place_late([(line, 0)])
+
+    def finish():
+        first, second = lanes.step([(swap_y, by_x[:half]), (swap_x, by_y[half:])])
+        place_late([(by_y, count), (by_x, 2 * count)])
+        place_late([(first, 3 * count), (second, 3 * count + half)])
+
+    return rest, finish, (by_x, by_y)
 
 
 def relative(owner):
@@ -349,30 +357,28 @@
     return ((rel_x * 2 + rel_y) * 4 + rel_z) * slots + slot
 
 
-def scatter_late_first(parts, slots, lanes, head_sum, images_part):
+def scatter_late_first(parts, slots, lanes):
     both = parts[12 * slots :]
-    arrived = lanes.step(
-        [(swap_y, both[: 2 * slots]), (swap_x, both[2 * slots :]), (swap_y, head_sum)]
-        + [(to_z(rel), images_part) for rel in (1, 2, 3)]
-    )
-    return arrived[:2], head_sum + arrived[2], jnp.concatenate([images_part] + arrived[3:], 0)
-
-
-def scatter_late(parts, slots, lanes, wait, later):
+    return lanes.step([(swap_y, both[: 2 * slots]), (swap_x, both[2 * slots :])])
+
+
+def scatter_late(parts, slots, lanes, wait, head_sum, images_part, *earlier):
     count = 4 * slots
     half = count // 2
     keep, to_y, to_x, _ = (parts[part * count : (part + 1) * count] for part in range(4))
-    (by_y, by_x), head_sum, images = wait
+    by_y, by_x = wait
     to_x = jnp.concatenate([low(wide(to_x[:half]) + by_y), to_x[half:]], 0)
     to_y = jnp.concatenate([to_y[:half], low(wide(to_y[half:]) + by_x)], 0)
-    from_x, from_y, head_x, images_y = lanes.step(
-        [(swap_x, to_x), (swap_y, to_y), (swap_x, head_sum), (swap_y, images)], later
+    from_x, from_y, head_y, *images = lanes.step(
+        [(swap_x, to_x), (swap_y, to_y), (swap_y, head_sum)]
+        + [(to_z(rel), images_part) for rel in (1, 2, 3)],
+        *earlier,
     )
     keep = wide(keep) + from_x + from_y
     return (
         [keep[rel * slots : (rel + 1) * slots] for rel in range(4)],
-        head_sum + head_x,
-        jnp.concatenate([images, images_y], 0),
+        head_sum + head_y,
+        jnp.concatenate([images_part] + images, 0),
     )
 
 
@@ -418,15 +424,19 @@
 
     line, late_line = ZSum(), ZSum()
     arrived = lanes.step(
-        diagonal(3) + late_line.sends(3, late[3]) + [(to_z(1), head_sum), (swap_x, early_images)]
+        diagonal(3) + late_line.sends(3, late[3]) + [(swap_x, head_sum), (swap_y, early_images)]
     )
     diagonal_3 = arrived[:2]
     late_line.take(arrived[2:4])
     head_sum = head_sum + arrived[4]
     early_images = jnp.concatenate([early_images, arrived[5]], 0)
-    arrived = lanes.step(diagonal(2) + late_line.sends(2, late[2]))
+    arrived = lanes.step(
+        diagonal(2) + late_line.sends(2, late[2]) + [(to_z(1), head_sum), (swap_x, early_images)]
+    )
     diagonal_2 = arrived[:2]
-    late_line.take(arrived[2:])
+    late_line.take(arrived[2:4])
+    head_sum = head_sum + arrived[4]
+    early_images = jnp.concatenate([early_images, arrived[5]], 0)
     arrived = lanes.step(sides(3, diagonal_3) + late_line.sends(1, late[1]))
     late_line.take(arrived[2:])
     owned_late = late_line.total(late[0])
@@ -459,13 +469,9 @@
     return jnp.concatenate([value, by_y, by_x, swap_x(by_y)], 0)
 
 
-def gather_else(flat, lanes, line):
-    if not is_box():
-        return lax.all_gather(flat, ("fsdp", "ctx", "tp"), axis=0, tiled=True)
-    z, x = place_z(), lax.axis_index("fsdp") % 2
-    y, core = lax.axis_index("ctx"), lax.axis_index("tp")
-    own = flat.reshape(1, -1, 128)
-    line = [own] + line
+def start_else(flat, lanes, arrived):
+    z = place_z()
+    line = [flat.reshape(1, -1, 128)] + arrived
     line = [
         jnp.where(
             z == place,
@@ -477,7 +483,13 @@
     line = jnp.concatenate(line, 0)
     by_x, by_y = lanes.step([(swap_x, line), (swap_y, line)])
     half = line.shape[1] // 2
-    both = jnp.concatenate(lanes.step([(swap_y, by_x[:, :half]), (swap_x, by_y[:, half:])]), 1)
+    return (line, by_x, by_y), [(swap_y, by_x[:, :half]), (swap_x, by_y[:, half:])]
+
+
+def finish_else(lines, both):
+    x, y, core = lax.axis_index("fsdp") % 2, lax.axis_index("ctx"), lax.axis_index("tp")
+    line, by_x, by_y = lines
+    both = jnp.concatenate(both, 1)
     y_low = [jnp.where(y == 0, line, by_y), jnp.where(y == 0, by_x, both)]
     y_high = [jnp.where(y == 0, by_y, line), jnp.where(y == 0, both, by_x)]
     chip = jnp.stack(
@@ -493,14 +505,32 @@
     )
 
 
-def cut_else(flat):
-    rows = flat.reshape(-1, D)
+def cut_else(whole):
+    rows = whole.reshape(-1, D)
     counts = [P_SIZE, NCLS, TFREQ, D, 2 * D, P_SIZE]
     ends = [sum(counts[: place + 1]) for place in range(6)]
     parts = [rows[end - count : end] for end, count in zip(ends, counts)]
-    parts[4] = parts[4].reshape(D, 2 * D)
-    parts[5] = parts[5].reshape(D, P_SIZE)
-    return tuple(parts)
+    return tuple(parts[:4]), parts[4], parts[5].reshape(D, P_SIZE)
+
+
+def final_product(left_op, final_rows):
+    rows = left_op.shape[0]
+    nothing = jnp.zeros_like(left_op)
+    spread = jnp.concatenate(
+        [
+            jnp.stack([left_op, nothing], -1).reshape(rows, 2 * D),
+            jnp.stack([nothing, left_op], -1).reshape(rows, 2 * D),
+        ],
+        0,
+    )
+    found = product(spread, final_rows)
+    return jnp.stack([found[:rows], found[rows:]], 1)
+
+
+def final_product_back(grads, final_rows):
+    rows = grads.shape[0]
+    found = against_low(jnp.concatenate([grads[:, :D], grads[:, D:]], 0), final_rows)
+    return found[:rows].reshape(rows, D, 2)[:, :, 0] + found[rows:].reshape(rows, D, 2)[:, :, 1]
 
 
 def total(value):
@@ -1036,7 +1066,7 @@
             + [pltpu.SemaphoreType.DMA((count,))] * 2,
         ),
         out_shape=[jax.ShapeDtypeStruct((amount, B, B), jnp.bfloat16) for _, amount, _ in held]
-        + [jax.ShapeDtypeStruct((8, B), jnp.float32)],
+        + [jax.ShapeDtypeStruct((8, B), jnp.int32)],
         input_output_aliases=aliases,
         compiler_params=params(),
         cost_estimate=pl.CostEstimate(
@@ -1054,7 +1084,7 @@
     return value
 
 
-LOT = 16
+LOT = 8
 
 
 def lots(count):
@@ -1095,14 +1125,21 @@
     return centred * rate, rate
 
 
-def rows_kernel_call(kernel, wide_ins, mode_ins, outs):
+def rows_kernel_call(kernel, wide_ins, mode_ins, outs, earlier=()):
+    count = len(wide_ins) + len(mode_ins)
+
+    def body(*refs):
+        kernel(*refs[:count], *refs[count + len(earlier) :])
+
     own, group = wide_ins[0].shape[:2]
     rows = pl.BlockSpec((1, group, D), lambda step: (step, 0, 0))
     few = lambda count: pl.BlockSpec((1, count, D), lambda step: (step, 0, 0))
     return pl.pallas_call(
-        kernel,
+        body,
         grid=(own,),
-        in_specs=[rows] * len(wide_ins) + [few(modes.shape[1]) for modes in mode_ins],
+        in_specs=[rows] * len(wide_ins)
+        + [few(modes.shape[1]) for modes in mode_ins]
+        + [pl.BlockSpec(memory_space=pl.ANY)] * len(earlier),
         out_specs=[rows if count is None else few(count) for count, _ in outs],
         out_shape=[
             jax.ShapeDtypeStruct((own, group if count is None else count, D), kind)
@@ -1114,7 +1151,7 @@
             bytes_accessed=own * group * D * 4 * (len(wide_ins) + len(outs)),
             transcendentals=own * group,
         ),
-    )(*wide_ins, *mode_ins)
+    )(*wide_ins, *mode_ins, *earlier)
 
 
 def modulate_call(stream, modes, shift, scale):
@@ -1127,7 +1164,7 @@
     return rows_kernel_call(kernel, [stream], [modes], [(None, jnp.bfloat16)])[0]
 
 
-def residual_call(stream, terms, modes, gate, next_modes, shift, scale):
+def residual_call(stream, terms, modes, gate, next_modes, shift, scale, earlier=()):
     def kernel(*refs):
         values, term_refs = refs[0], refs[1 : 1 + len(terms)]
         mode, mode_next, branch, stream_new, out = refs[1 + len(terms) :]
@@ -1148,10 +1185,11 @@
         [stream] + [term.reshape(shape) for term in terms],
         [modes, next_modes],
         [(None, jnp.float32), (None, jnp.float32), (None, jnp.bfloat16)],
-    )
-
-
-def back_call(stream, terms, upstream, modes, scale, below):
+        earlier,
+    )
+
+
+def back_call(stream, terms, upstream, modes, scale, below, earlier=()):
     shape = stream.shape
     wide_ins = [stream] + [term.reshape(shape) for term in terms]
     if upstream is not None:
@@ -1186,7 +1224,7 @@
             results[1][0, 2:3, :] = jnp.sum(grad * ins[-1][0], 0, keepdims=True)
             results[2][0] = low(modes_in[1][0, gate : gate + 1, :] * grad)
 
-    return rows_kernel_call(kernel, wide_ins, mode_ins, outs)
+    return rows_kernel_call(kernel, wide_ins, mode_ins, outs, earlier)
 
 
 def update_kernel(clip, grad, master, first, second, bases, master_out, first_out, second_out, low_out):
@@ -1303,14 +1341,14 @@
             return token
 
         late_store = None
-        else_parts = gather_tiles(
+        else_parts, finish_gather, arriving = gather_tiles(
             tiles_low[0], early, place_early_tiles, place_late_tiles, else_low, targets
         )
         store = [
             bring_strays(
                 stores[0][2], strays, stray_count, tiles_low[0], inverse, slots, me, tp_parts
             ),
-            late_store[0][2],
+            None,
         ]
         held = [(0, room, None), (room, 16 * (slots + 1) + LOT, None)]
     else:
@@ -1320,23 +1358,23 @@
         gathered = gathered[inverse[tile_stored]]
         store = [gathered[:per_layer], gathered[per_layer:]]
         held = [(0, all_tiles, None)]
-        else_parts = cut_else(gather_else(else_low, None, None))
-    patch_weight, class_table, time_first, time_second, final_weight, head_weight = else_parts
+        else_parts = cut_else(lax.all_gather(else_low, ("fsdp", "ctx", "tp"), axis=0, tiled=True))
+    (patch_weight, class_table, time_first, time_second), final_rows, head_weight = else_parts
     features_low = low(time_features(timesteps))
     onehot = low(labels[:, None] == jnp.arange(NCLS)[None, :])
     time_hidden = product(features_low, time_first)
     time_act = low(jax.nn.silu(time_hidden))
     condition = product(time_act, time_second) + product(onehot, class_table)
     cond_act = low(jax.nn.silu(condition))
-    modes = [
-        lax.dynamic_slice_in_dim(
+    def modes_of(layer_no):
+        return lax.dynamic_slice_in_dim(
             columns_in(modes_call(cond_act, store[layer_no], tp_parts)), first_image, own, 0
         ).reshape(own, 6, D)
-        for layer_no in range(L)
-    ]
+
+    modes = [modes_of(0)]
     final_modes = lax.dynamic_slice_in_dim(
-        product(cond_act, final_weight), first_image, own, 0
-    ).reshape(own, 2, D)
+        final_product(cond_act, final_rows), first_image, own, 0
+    )
     row_index = first_row + jnp.arange(sp_rows)
     signal = signal_level(timesteps)
     noisy_input = (
@@ -1361,13 +1399,25 @@
             lambda rows: attend_call(rows, store[layer_no], tp_parts, local_len), row_sets
         )
         branch, middle, normed_mid = residual_call(
-            stream, terms, modes[layer_no], 2, modes[layer_no], 3, 4
+            stream,
+            terms,
+            modes[layer_no],
+            2,
+            modes[layer_no],
+            3,
+            4,
+            arriving if box and layer_no == 0 else (),
         )
         mid_sets = rows_in(normed_mid.reshape(sp_rows, D))
         hidden, terms = each_half(
             lambda rows: mlp_call(rows, store[layer_no], tp_parts, local_len), mid_sets
         )
         last = layer_no == L - 1
+        if not last:
+            if box:
+                finish_gather()
+                store[1] = late_store[0][2]
+            modes.append(modes_of(layer_no + 1))
         mlp_out, stream_new, normed_in = residual_call(
             middle,
             terms,
@@ -1436,7 +1486,16 @@
             middle, terms, upstream, modes[layer_no], 4, (branch, modes[layer_no], 2)
         )
         if box and layer_no == 0:
-            late_sums = scatter_late(late_parts, slots - early, lanes, late_first, upstream)
+            late_sums = scatter_late(
+                late_parts,
+                slots - early,
+                lanes,
+                late_first,
+                tp_sum(grad_head),
+                image_part(early_columns),
+                upstream,
+                grad_cond_early,
+            )
         grad_sets = rows_in(grad_low.reshape(sp_rows, D))
         results, terms = each_half(
             lambda pair: attend_back_call(pair[0], pair[1], store[layer_no], tp_parts, local_len),
@@ -1449,7 +1508,15 @@
             row_sets, [result[0] for result in results], places, base + starts[0], held
         )
         below = None if layer_no == 0 else (kept[layer_no - 1][7], modes[layer_no - 1], 5)
-        found = back_call(stream, terms, upstream, modes[layer_no], 1, below)
+        found = back_call(
+            stream,
+            terms,
+            upstream,
+            modes[layer_no],
+            1,
+            below,
+            (late_sums[0][0],) if box and layer_no == 0 else (),
+        )
         grad_modes = jnp.concatenate(
             [found[1][:, :2], mlp_sums[:, 2:], mlp_sums[:, :2], gate_sum], 1
         ).reshape(own, 6 * D)
@@ -1471,16 +1538,11 @@
             grad_low = after(grad_low, held[0][2], held[1][2])
             lanes = Lanes()
             late_parts = held[0][2]
-            late_first = scatter_late_first(
-                late_parts,
-                slots - early,
-                lanes,
-                tp_sum(grad_head),
-                image_part(early_columns),
-            )
+            late_first = scatter_late_first(late_parts, slots - early, lanes)
+            grad_cond_early = grad_cond_act
             held = held[1:]
     grad_patch = over_rows(noisy_rows, low(upstream).reshape(sp_rows, D))
-    grad_cond_act = tp_sum(grad_cond_act) + against_low(grad_final, final_weight)
+    grad_cond_act = tp_sum(grad_cond_act) + final_product_back(grad_final, final_rows)
     grad_condition = jax.vjp(jax.nn.silu, condition)[1](grad_cond_act)[0]
     grad_time_hidden = jax.vjp(jax.nn.silu, time_hidden)[1](
         against_low(grad_condition, time_second)

time: 1260 us -> 1230 us (0.976)
  waiting for transfers between devices: 373 us -> 305 us
  starting transfers between devices: 127 us -> 142 us
  local copies, waits for them, and re-layouts: 173 us -> 186 us
    ppermute x39, waiting for transfers between devices: 225 us -> 141 us  [swap_f(): lax.ppermute(value, 'fsdp', [(place, place ^ bit) for place in range(8)])]
    ppermute x26, waiting for transfers between devices: 68 us -> 121 us  [swap_y(): return lax.ppermute(value, 'ctx', [(0, 1), (1, 0)])]
    ppermute x24, waiting for transfers between devices: 62.7 us -> 29.6 us  [move_z(): return lambda value: lax.ppermute(value, 'fsdp', pairs)]
    unnamed x279 -> x262, local copies, waits for them, and re-layouts: 24.7 us -> 38 us
    slice x5 -> x14, local copies, waits for them, and re-layouts: 6.66 us -> 19.3 us  [the longest x3 5.29 us: final_product_back(): found[rows:].reshape(rows, D, 2)[:, :, 1]]
    convert_element_type x18 -> x16, other arithmetic: 39.9 us -> 40 us  [low(): return value.astype(jnp.bfloat16)]
  transfers between devices with their start and end apart: 118 -> 118, of which waited for: 48 -> 47; matrix products, arithmetic and copies ran while one was open for 21% -> 23% of each run, Pallas kernels for 22% -> 21%
where the time goes in v4:
time: 1230 us; the launch traced here: 1220 us
  Pallas kernels  401 us (33%)
  waiting for transfers between devices  305 us (25%)
  local copies, waits for them, and re-layouts  186 us (15%)
  other arithmetic  148 us (12%)
  starting transfers between devices  142 us (12%)
  matrix products  28.1 us (2%)
    ppermute x39, waiting for transfers between devices, swap_f(): lax.ppermute(value, 'fsdp', [(place, place ^ bit) for place in range(8)])  141 us
    ppermute x26, waiting for transfers between devices, swap_y(): return lax.ppermute(value, 'ctx', [(0, 1), (1, 0)])  121 us
    pallas_call x10, Pallas kernels, weight_grad_call(): pl.pallas_call(kernel, grid_spec=pltpu.PrefetchScalarGridSpec(num_scalar_...  82.9 us
    ppermute x24, starting transfers between devices, move_z(): return lambda value: lax.ppermute(value, 'fsdp', pairs)  60.7 us
    pallas_call x4, Pallas kernels, attend_back_call(): pl.pallas_call(attend_back_kernel, grid=(rows // local_len,), in_specs=[r...  55.5 us
    ppermute x39, starting transfers between devices, swap_f(): lax.ppermute(value, 'fsdp', [(place, place ^ bit) for place in range(8)])  52.1 us
    pallas_call x10, Pallas kernels, rows_kernel_call(): pl.pallas_call(body, grid=(own,), in_specs=[rows] * len(wide_ins) + [few(...  51.9 us
    pallas_call x4, Pallas kernels, mlp_back_call(): pl.pallas_call(mlp_back_kernel, grid=(width // step_width,), in_specs=[al...  50.4 us
  transfers between devices with their start and end apart: 118, of which 47 were waited for; matrix products, arithmetic and copies ran while one was open for 23% of the time, Pallas kernels for 21%

profile of v4, /device:TPU:0, one launch (start us, length us, event | category | flops | bytes accessed | tf_op | source)
XLA Modules:
  0.0 1219.3 jit_solution(13667167755134438115)
XLA Ops:
  30.3 10.0 collective-permute-done.9.refs_1_
  59.1 13.0 %collective-permute-done.13 = bf16[1,1090,128]{2,1,0:T(8,128)(2,1)} collective-permute-done((bf16[1,1090,128]{2,1,0:T(8,128)(2,1)S(1)}, bf16[1,1090,128]{2,1,0:T(8,128)(2,1)}, u32[]{:S(2)}, u32[]{:S(2)}) %collective-permute-start.13) | collective-permute-done | bytes 279072 | tf_op jit(solution)/shard_map/ppermute | solution.py:185
  87.4 12.1 collective-permute-done.18
  114.8 10.1 collective-permute-done.19
  133.5 10.2 copy.111
  185.8 26.3 %collective-permute-done.33.refs_1_ = bf16[47,128,128]{2,1,0:T(8,128)(2,1)} collective-permute-done((bf16[47,128,128]{2,1,0:T(8,128)(2,1)}, bf16[47,128,128]{2,1,0:T(8,128)(2,1)}, u32[]{:S(2)}, u32[]{:S(2)}) %collective-permute-start.33) | collective-permute-done | bytes 1540128 | tf_op jit(solution)/shard_map/ppermute | solution.py:181
  278.0 15.6 %reshape.497 = bf16[4360,1024]{1,0:T(8,128)(2,1)} reshape(bf16[4,2,2,2,1090,128]{5,4,3,2,1,0:T(8,128)(2,1)} %copy.114) | data formatting | bytes 17858560 | tf_op jit(solution)/shard_map/reshape | solution.py:509
  353.0 52.4 %collective-permute-done.47.refs_5_.refs_1_ = bf16[100,128,128]{2,1,0:T(8,128)(2,1)S(1)} collective-permute-done((bf16[100,128,128]{2,1,0:T(8,128)(2,1)}, bf16[100,128,128]{2,1,0:T(8,128)(2,1)S(1)}, u32[]{:S(2)}, u32[]{:S(2)}) %collective-permute-start.47) | collective-permute-done | bytes 3276832 | tf_op jit(solution)/shard_map/ppermute | solution.py:185
  420.4 10.6 shard_map.223
  442.0 13.9 %collective-permute-done.51.refs_0_ = bf16[50,128,128]{2,1,0:T(8,128)(2,1)S(1)} collective-permute-done((bf16[50,128,128]{2,1,0:T(8,128)(2,1)}, bf16[50,128,128]{2,1,0:T(8,128)(2,1)S(1)}, u32[]{:S(2)}, u32[]{:S(2)}) %collective-permute-start.51) | collective-permute-done | bytes 1638432 | tf_op jit(solution)/shard_map/ppermute | solution.py:181
  467.2 10.6 shard_map.222
  517.2 10.7 shard_map.233
  536.1 11.0 shard_map.232
  565.8 12.5 %shard_map.237 = (bf16[512,2048]{1,0:T(8,128)(2,1)}, bf16[512,2048]{1,0:T(8,128)(2,1)}, f32[512,1024]{1,0:T(8,128)}) custom-call(bf16[512,1024]{1,0:T(8,128)(2,1)} %copy-done.54, f32[512,2048]{1,0:T(8,128)} %get-tuple-element.512.hidden, bf16[577,128,128]{2,1,0:T(8,128)(2,1)} %get-tuple-element.497.tile_set.qkv_tiles.proj_tiles.up_tiles.down_tiles, ...), custom_call_target="tpu_custom_call" | custom-call | flops 4294967296 | bytes 16777216 | tf_op jit(solution)/shard_map/pallas_call | solution.py:832
  578.7 12.6 %shard_map.236 = (bf16[512,2048]{1,0:T(8,128)(2,1)}, bf16[512,2048]{1,0:T(8,128)(2,1)}, f32[512,1024]{1,0:T(8,128)}) custom-call(bf16[512,1024]{1,0:T(8,128)(2,1)} %bitcast.204, f32[512,2048]{1,0:T(8,128)} %get-tuple-element.510.hidden, bf16[577,128,128]{2,1,0:T(8,128)(2,1)} %get-tuple-element.497.tile_set.qkv_tiles.proj_tiles.up_tiles.down_tiles, ...), custom_call_target="tpu_custom_call" | custom-call | flops 4294967296 | bytes 16777216 | tf_op jit(solution)/shard_map/pallas_call | solution.py:832
  603.3 14.0 %shard_map.240 = (bf16[512,1536]{1,0:T(8,128)(2,1)}, f32[512,1024]{1,0:T(8,128)}) custom-call(bf16[512,1024]{1,0:T(8,128)(2,1)} %copy-done.26, bf16[512,1536]{1,0:T(8,128)(2,1)} %get-tuple-element.519.projected, bf16[577,128,128]{2,1,0:T(8,128)(2,1)} %get-tuple-element.497.tile_set.qkv_tiles.proj_tiles.up_tiles.down_tiles, ...), custom_call_target="tpu_custom_call" | custom-call | flops 2684354560 | bytes 4194304 | tf_op jit(solution)/shard_map/pallas_call | solution.py:718
  618.0 9.9 shard_map.242
  628.0 10.6 shard_map.243
  638.7 13.8 %shard_map.239 = (bf16[512,1536]{1,0:T(8,128)(2,1)}, f32[512,1024]{1,0:T(8,128)}) custom-call(bf16[512,1024]{1,0:T(8,128)(2,1)} %bitcast.173, bf16[512,1536]{1,0:T(8,128)(2,1)} %get-tuple-element.517.projected, bf16[577,128,128]{2,1,0:T(8,128)(2,1)} %get-tuple-element.497.tile_set.qkv_tiles.proj_tiles.up_tiles.down_tiles, ...), custom_call_target="tpu_custom_call" | custom-call | flops 2684354560 | bytes 4194304 | tf_op jit(solution)/shard_map/pallas_call | solution.py:718
  697.2 12.5 %shard_map.248 = (bf16[512,2048]{1,0:T(8,128)(2,1)}, bf16[512,2048]{1,0:T(8,128)(2,1)}, f32[512,1024]{1,0:T(8,128)}) custom-call(bf16[512,1024]{1,0:T(8,128)(2,1)} %copy-done.25, f32[512,2048]{1,0:T(8,128)} %get-tuple-element.548.hidden, bf16[577,128,128]{2,1,0:T(8,128)(2,1)} %get-tuple-element.483.tile_set.qkv_tiles.proj_tiles.up_tiles.down_tiles, ...), custom_call_target="tpu_custom_call" | custom-call | flops 4294967296 | bytes 16777216 | tf_op jit(solution)/shard_map/pallas_call | solution.py:832
  719.1 12.8 %shard_map.247 = (bf16[512,2048]{1,0:T(8,128)(2,1)}, bf16[512,2048]{1,0:T(8,128)(2,1)}, f32[512,1024]{1,0:T(8,128)}) custom-call(bf16[512,1024]{1,0:T(8,128)(2,1)} %bitcast.169, f32[512,2048]{1,0:T(8,128)} %get-tuple-element.546.hidden, bf16[577,128,128]{2,1,0:T(8,128)(2,1)} %get-tuple-element.483.tile_set.qkv_tiles.proj_tiles.up_tiles.down_tiles, ...), custom_call_target="tpu_custom_call" | custom-call | flops 4294967296 | bytes 16777216 | tf_op jit(solution)/shard_map/pallas_call | solution.py:832
  754.1 13.8 %shard_map.251 = (bf16[512,1536]{1,0:T(8,128)(2,1)}, f32[512,1024]{1,0:T(8,128)}) custom-call(bf16[512,1024]{1,0:T(8,128)(2,1)} %copy-done.29, bf16[512,1536]{1,0:T(8,128)(2,1)} %get-tuple-element.555.projected, bf16[577,128,128]{2,1,0:T(8,128)(2,1)} %get-tuple-element.483.tile_set.qkv_tiles.proj_tiles.up_tiles.down_tiles, ...), custom_call_target="tpu_custom_call" | custom-call | flops 2684354560 | bytes 4194304 | tf_op jit(solution)/shard_map/pallas_call | solution.py:718
  768.0 9.6 shard_map.254.refs_4_
  784.4 10.1 shard_map.255.refs_4_
  799.2 14.0 %shard_map.250 = (bf16[512,1536]{1,0:T(8,128)(2,1)}, f32[512,1024]{1,0:T(8,128)}) custom-call(bf16[512,1024]{1,0:T(8,128)(2,1)} %bitcast.183, bf16[512,1536]{1,0:T(8,128)(2,1)} %get-tuple-element.553.projected, bf16[577,128,128]{2,1,0:T(8,128)(2,1)} %get-tuple-element.483.tile_set.qkv_tiles.proj_tiles.up_tiles.down_tiles, ...), custom_call_target="tpu_custom_call" | custom-call | flops 2684354560 | bytes 4194304 | tf_op jit(solution)/shard_map/pallas_call | solution.py:718
  896.9 15.6 %collective-permute-done.83 = f32[16,2304]{1,0:T(8,128)} collective-permute-done((f32[16,2304]{1,0:T(8,128)}, f32[16,2304]{1,0:T(8,128)}, u32[]{:S(2)}, u32[]{:S(2)}) %collective-permute-start.83) | collective-permute-done | bytes 147488 | tf_op jit(solution)/shard_map/ppermute | solution.py:181
  976.8 13.1 %collective-permute-done.94 = bf16[25,128,128]{2,1,0:T(8,128)(2,1)S(1)} collective-permute-done((bf16[25,128,128]{2,1,0:T(8,128)(2,1)}, bf16[25,128,128]{2,1,0:T(8,128)(2,1)S(1)}, u32[]{:S(2)}, u32[]{:S(2)}) %collective-permute-start.94) | collective-permute-done | bytes 819232 | tf_op jit(solution)/shard_map/ppermute | solution.py:220
  1042.0 11.2 slice.503
  1063.2 11.1 collective-permute-done.107
  1088.9 25.6 %collective-permute-done.110 = bf16[48,128,128]{2,1,0:T(8,128)(2,1)S(1)} collective-permute-done((bf16[48,128,128]{2,1,0:T(8,128)(2,1)S(1)}, bf16[48,128,128]{2,1,0:T(8,128)(2,1)S(1)}, u32[]{:S(2)}, u32[]{:S(2)}) %collective-permute-start.110) | collective-permute-done | bytes 1572896 | tf_op jit(solution)/shard_map/ppermute | solution.py:185
  1139.3 13.7 %collective-permute-done.114 = bf16[48,128,128]{2,1,0:T(8,128)(2,1)} collective-permute-done((bf16[48,128,128]{2,1,0:T(8,128)(2,1)}, bf16[48,128,128]{2,1,0:T(8,128)(2,1)}, u32[]{:S(2)}, u32[]{:S(2)}) %collective-permute-start.114) | collective-permute-done | bytes 1572896 | tf_op jit(solution)/shard_map/ppermute | solution.py:185
  1200.5 17.5 %shard_map.260 = (f32[72,128,128]{2,1,0:T(8,128)}, f32[72,128,128]{2,1,0:T(8,128)}, f32[72,128,128]{2,1,0:T(8,128)}, bf16[72,128,128]{2,1,0:T(8,128)(2,1)}) custom-call(f32[1,1]{1,0:T(1,128)} %bitcast.66.clip, f32[72,128,128]{2,1,0:T(8,128)} %get-tuple-element.615.grad, f32[72,128,128]{2,1,0:T(8,128)} %bitcast.160, f32[72,128,128]{2,1,0:T(8,128)} %bitcast.161, ...), custom_call_target="tpu_custom_call" | custom-call | flops 35389440 | bytes 35389440 | tf_op jit(solution)/shard_map/pallas_call | solution.py:1257
  (744 shorter events, 750.8 us)
Async XLA Ops:
  3.4 37.0 %collective-permute-start.9 = (bf16[47,128,128]{2,1,0:T(8,128)(2,1)}, bf16[47,128,128]{2,1,0:T(8,128)(2,1)}, u32[]{:S(2)}, u32[]{:S(2)}) collective-permute-start(bf16[47,128,128]{2,1,0:T(8,128)(2,1)} %slice_bitcast_fusion.refs_0_), channel_id=1, source_target_pairs={{0,2},{2,0},{1,3},{3,1},{4,6},{6,4},{5,7},{7,5},{8,10},{10,8},{9,1... | collective-permute-start | bytes 4620296 | tf_op jit(solution)/shard_map/ppermute | solution.py:181
  6.3 36.1 %collective-permute-start.8 = (bf16[47,128,128]{2,1,0:T(8,128)(2,1)}, bf16[47,128,128]{2,1,0:T(8,128)(2,1)}, u32[]{:S(2)}, u32[]{:S(2)}) collective-permute-start(bf16[47,128,128]{2,1,0:T(8,128)(2,1)} %slice_bitcast_fusion.refs_0_), channel_id=1, source_target_pairs={{0,4},{4,0},{8,12},{12,8},{16,20},{20,16},{24,28},{28,24},{1,5},{5... | collective-permute-start | bytes 4620296 | tf_op jit(solution)/shard_map/ppermute | solution.py:185
  7.8 36.7 %collective-permute-start.10 = (bf16[47,128,128]{2,1,0:T(8,128)(2,1)}, bf16[47,128,128]{2,1,0:T(8,128)(2,1)S(1)}, u32[]{:S(2)}, u32[]{:S(2)}) collective-permute-start(bf16[47,128,128]{2,1,0:T(8,128)(2,1)} %slice_bitcast_fusion.refs_0_), channel_id=1, source_target_pairs={{0,8},{4,12},{8,16},{12,20},{16,24},{20,28},{1,9},{5,13},{9,17},{1... | collective-permute-start | bytes 4620296 | tf_op jit(solution)/shard_map/ppermute | solution.py:220
  11.4 36.7 %collective-permute-start.11 = (bf16[47,128,128]{2,1,0:T(8,128)(2,1)}, bf16[47,128,128]{2,1,0:T(8,128)(2,1)S(1)}, u32[]{:S(2)}, u32[]{:S(2)}) collective-permute-start(bf16[47,128,128]{2,1,0:T(8,128)(2,1)} %slice_bitcast_fusion.refs_0_), channel_id=1, source_target_pairs={{8,0},{12,4},{16,8},{20,12},{24,16},{28,20},{9,1},{13,5},{17,9},{2... | collective-permute-start | bytes 4620296 | tf_op jit(solution)/shard_map/ppermute | solution.py:220
  111.0 38.6 %collective-permute-start.22 = (bf16[47,128,128]{2,1,0:T(8,128)(2,1)}, bf16[47,128,128]{2,1,0:T(8,128)(2,1)S(1)}, u32[]{:S(2)}, u32[]{:S(2)}) collective-permute-start(bf16[47,128,128]{2,1,0:T(8,128)(2,1)} %broadcast_select_fusion.2.refs_0_), channel_id=1, source_target_pairs={{0,2},{2,0},{1,3},{3,1},{4,6},{6,4},{5,7},{7,5},{8,10},{10,8},{9,1... | collective-permute-start | bytes 4620296 | tf_op jit(solution)/shard_map/ppermute | solution.py:181
  112.5 39.2 %collective-permute-start.23 = (bf16[47,128,128]{2,1,0:T(8,128)(2,1)}, bf16[47,128,128]{2,1,0:T(8,128)(2,1)S(1)}, u32[]{:S(2)}, u32[]{:S(2)}) collective-permute-start(bf16[47,128,128]{2,1,0:T(8,128)(2,1)} %broadcast_select_fusion.2.refs_0_), channel_id=1, source_target_pairs={{0,4},{4,0},{8,12},{12,8},{16,20},{20,16},{24,28},{28,24},{1,5},{5... | collective-permute-start | bytes 4620296 | tf_op jit(solution)/shard_map/ppermute | solution.py:185
  113.0 40.8 %collective-permute-start.24 = (bf16[47,128,128]{2,1,0:T(8,128)(2,1)}, bf16[47,128,128]{2,1,0:T(8,128)(2,1)}, u32[]{:S(2)}, u32[]{:S(2)}) collective-permute-start(bf16[47,128,128]{2,1,0:T(8,128)(2,1)} %copy-done.13), channel_id=1, source_target_pairs={{8,16},{12,20},{16,24},{20,28},{9,17},{13,21},{17,25},{21,29},{10,... | collective-permute-start | bytes 4620296 | tf_op jit(solution)/shard_map/ppermute | solution.py:220
  143.7 112.2 %collective-permute-start.21 = (bf16[4,2,2,1090,128]{4,0,3,2,1:T(4,128)(2,1)}, bf16[4,2,2,1090,128]{4,0,3,2,1:T(4,128)(2,1)}, u32[]{:S(2)}, u32[]{:S(2)}) collective-permute-start(bf16[4,2,2,1090,128]{4,0,3,2,1:T(4,128)(2,1)} %copy.111), channel_id=1, source_target_pairs={{0,1},{1,0},{2,3},{3,2},{4,5},{5,4},{6,7},{7,6},{8,9},{9,8},{10,11... | collective-permute-start | bytes 13393928 | tf_op jit(solution)/shard_map/ppermute | solution.py:177
  182.4 34.0 %collective-permute-start.30 = (bf16[47,128,128]{2,1,0:T(8,128)(2,1)}, bf16[47,128,128]{2,1,0:T(8,128)(2,1)}, u32[]{:S(2)}, u32[]{:S(2)}) collective-permute-start(bf16[47,128,128]{2,1,0:T(8,128)(2,1)} %collective-permute-done.25), channel_id=1, source_target_pairs={{8,0},{12,4},{9,1},{13,5},{10,2},{14,6},{11,3},{15,7}} | collective-permute-start | bytes 4620296 | tf_op jit(solution)/shard_map/ppermute | solution.py:220
  247.7 49.6 %collective-permute-start.40 = (bf16[25,128,128]{2,1,0:T(8,128)(2,1)}, bf16[25,128,128]{2,1,0:T(8,128)(2,1)}, u32[]{:S(2)}, u32[]{:S(2)}) collective-permute-start(bf16[25,128,128]{2,1,0:T(8,128)(2,1)} %collective-permute-done.34), channel_id=1, source_target_pairs={{16,24},{20,28},{17,25},{21,29},{18,26},{22,30},{19,27},{23,31}} | collective-permute-start | bytes 2457608 | tf_op jit(solution)/shard_map/ppermute | solution.py:220
  249.4 47.9 %collective-permute-start.41 = (bf16[25,128,128]{2,1,0:T(8,128)(2,1)}, bf16[25,128,128]{2,1,0:T(8,128)(2,1)}, u32[]{:S(2)}, u32[]{:S(2)}) collective-permute-start(bf16[25,128,128]{2,1,0:T(8,128)(2,1)} %collective-permute-done.35), channel_id=1, source_target_pairs={{8,0},{12,4},{9,1},{13,5},{10,2},{14,6},{11,3},{15,7}} | collective-permute-start | bytes 2457608 | tf_op jit(solution)/shard_map/ppermute | solution.py:220
  250.7 44.2 %collective-permute-start.38 = (bf16[47,128,128]{2,1,0:T(8,128)(2,1)}, bf16[47,128,128]{2,1,0:T(8,128)(2,1)}, u32[]{:S(2)}, u32[]{:S(2)}) collective-permute-start(bf16[47,128,128]{2,1,0:T(8,128)(2,1)} %select_select_fusion.refs_0_), channel_id=1, source_target_pairs={{0,2},{2,0},{1,3},{3,1},{4,6},{6,4},{5,7},{7,5},{8,10},{10,8},{9,1... | collective-permute-start | bytes 4620296 | tf_op jit(solution)/shard_map/ppermute | solution.py:181
  254.6 41.5 %collective-permute-start.39 = (bf16[47,128,128]{2,1,0:T(8,128)(2,1)}, bf16[47,128,128]{2,1,0:T(8,128)(2,1)}, u32[]{:S(2)}, u32[]{:S(2)}) collective-permute-start(bf16[47,128,128]{2,1,0:T(8,128)(2,1)} %select_select_fusion.refs_0_), channel_id=1, source_target_pairs={{0,4},{4,0},{8,12},{12,8},{16,20},{20,16},{24,28},{28,24},{1,5},{5... | collective-permute-start | bytes 4620296 | tf_op jit(solution)/shard_map/ppermute | solution.py:185
  332.4 73.0 %collective-permute-start.47 = (bf16[100,128,128]{2,1,0:T(8,128)(2,1)}, bf16[100,128,128]{2,1,0:T(8,128)(2,1)S(1)}, u32[]{:S(2)}, u32[]{:S(2)}) collective-permute-start(bf16[100,128,128]{2,1,0:T(8,128)(2,1)} %pad_maximum_fusion.3.refs_0_), channel_id=1, source_target_pairs={{0,4},{4,0},{8,12},{12,8},{16,20},{20,16},{24,28},{28,24},{1,5},{5... | collective-permute-start | bytes 9830408 | tf_op jit(solution)/shard_map/ppermute | solution.py:185
  333.6 72.8 %collective-permute-start.48 = (bf16[100,128,128]{2,1,0:T(8,128)(2,1)}, bf16[100,128,128]{2,1,0:T(8,128)(2,1)S(1)}, u32[]{:S(2)}, u32[]{:S(2)}) collective-permute-start(bf16[100,128,128]{2,1,0:T(8,128)(2,1)} %pad_maximum_fusion.3.refs_0_), channel_id=1, source_target_pairs={{0,2},{2,0},{1,3},{3,1},{4,6},{6,4},{5,7},{7,5},{8,10},{10,8},{9,1... | collective-permute-start | bytes 9830408 | tf_op jit(solution)/shard_map/ppermute | solution.py:181
  417.6 38.3 %collective-permute-start.51 = (bf16[50,128,128]{2,1,0:T(8,128)(2,1)}, bf16[50,128,128]{2,1,0:T(8,128)(2,1)S(1)}, u32[]{:S(2)}, u32[]{:S(2)}) collective-permute-start(bf16[50,128,128]{2,1,0:T(8,128)(2,1)} %slice.444), channel_id=1, source_target_pairs={{0,2},{2,0},{1,3},{3,1},{4,6},{6,4},{5,7},{7,5},{8,10},{10,8},{9,1... | collective-permute-start | bytes 4915208 | tf_op jit(solution)/shard_map/ppermute | solution.py:181
  418.0 38.0 %collective-permute-start.52 = (bf16[50,128,128]{2,1,0:T(8,128)(2,1)}, bf16[50,128,128]{2,1,0:T(8,128)(2,1)S(1)}, u32[]{:S(2)}, u32[]{:S(2)}) collective-permute-start(bf16[50,128,128]{2,1,0:T(8,128)(2,1)} %slice.445), channel_id=1, source_target_pairs={{0,4},{4,0},{8,12},{12,8},{16,20},{20,16},{24,28},{28,24},{1,5},{5... | collective-permute-start | bytes 4915208 | tf_op jit(solution)/shard_map/ppermute | solution.py:185
  431.0 47.6 %collective-permute-start.50 = (f32[512,1024]{1,0:T(8,128)}, f32[512,1024]{1,0:T(8,128)S(1)}, u32[]{:S(2)}, u32[]{:S(2)}) collective-permute-start(f32[512,1024]{1,0:T(8,128)} %get-tuple-element.491), channel_id=1, source_target_pairs={{0,1},{1,0},{2,3},{3,2},{4,5},{5,4},{6,7},{7,6},{8,9},{9,8},{10,11... | collective-permute-start | bytes 6291464 | tf_op jit(solution)/shard_map/ppermute | solution.py:177
  617.3 41.3 %collective-permute-start.61 = (f32[512,1024]{1,0:T(8,128)}, f32[512,1024]{1,0:T(8,128)S(1)}, u32[]{:S(2)}, u32[]{:S(2)}) collective-permute-start(f32[512,1024]{1,0:T(8,128)} %get-tuple-element.520), channel_id=1, source_target_pairs={{0,1},{1,0},{2,3},{3,2},{4,5},{5,4},{6,7},{7,6},{8,9},{9,8},{10,11... | collective-permute-start | bytes 6291464 | tf_op jit(solution)/shard_map/ppermute | solution.py:177
  693.7 38.4 %collective-permute-start.67 = (bf16[50,128,128]{2,1,0:T(8,128)(2,1)}, bf16[50,128,128]{2,1,0:T(8,128)(2,1)}, u32[]{:S(2)}, u32[]{:S(2)}) collective-permute-start(bf16[50,128,128]{2,1,0:T(8,128)(2,1)} %get-tuple-element.558), channel_id=1, source_target_pairs={{0,2},{2,0},{1,3},{3,1},{4,6},{6,4},{5,7},{7,5},{8,10},{10,8},{9,1... | collective-permute-start | bytes 4915208 | tf_op jit(solution)/shard_map/ppermute | solution.py:181
  695.1 38.1 %collective-permute-start.68 = (bf16[50,128,128]{2,1,0:T(8,128)(2,1)}, bf16[50,128,128]{2,1,0:T(8,128)(2,1)}, u32[]{:S(2)}, u32[]{:S(2)}) collective-permute-start(bf16[50,128,128]{2,1,0:T(8,128)(2,1)} %get-tuple-element.559), channel_id=1, source_target_pairs={{0,4},{4,0},{8,12},{12,8},{16,20},{20,16},{24,28},{28,24},{1,5},{5... | collective-permute-start | bytes 4915208 | tf_op jit(solution)/shard_map/ppermute | solution.py:185
  748.3 81.0 %collective-permute-start.71 = (bf16[100,128,128]{2,1,0:T(8,128)(2,1)}, bf16[100,128,128]{2,1,0:T(8,128)(2,1)}, u32[]{:S(2)}, u32[]{:S(2)}) collective-permute-start(bf16[100,128,128]{2,1,0:T(8,128)(2,1)} %pad_maximum_fusion.4), channel_id=1, source_target_pairs={{0,4},{4,0},{8,12},{12,8},{16,20},{20,16},{24,28},{28,24},{1,5},{5... | collective-permute-start | bytes 9830408 | tf_op jit(solution)/shard_map/ppermute | solution.py:185
  749.3 80.0 %collective-permute-start.72 = (bf16[100,128,128]{2,1,0:T(8,128)(2,1)}, bf16[100,128,128]{2,1,0:T(8,128)(2,1)}, u32[]{:S(2)}, u32[]{:S(2)}) collective-permute-start(bf16[100,128,128]{2,1,0:T(8,128)(2,1)} %pad_maximum_fusion.5), channel_id=1, source_target_pairs={{0,2},{2,0},{1,3},{3,1},{4,6},{6,4},{5,7},{7,5},{8,10},{10,8},{9,1... | collective-permute-start | bytes 9830408 | tf_op jit(solution)/shard_map/ppermute | solution.py:181
  767.9 71.5 %collective-permute-start.66 = (f32[512,1024]{1,0:T(8,128)}, f32[512,1024]{1,0:T(8,128)S(1)}, u32[]{:S(2)}, u32[]{:S(2)}) collective-permute-start(f32[512,1024]{1,0:T(8,128)} %get-tuple-element.556), channel_id=1, source_target_pairs={{0,1},{1,0},{2,3},{3,2},{4,5},{5,4},{6,7},{7,6},{8,9},{9,8},{10,11... | collective-permute-start | bytes 6291464 | tf_op jit(solution)/shard_map/ppermute | solution.py:177
  878.0 39.0 %collective-permute-start.81 = (bf16[25,128,128]{2,1,0:T(8,128)(2,1)}, bf16[25,128,128]{2,1,0:T(8,128)(2,1)}, u32[]{:S(2)}, u32[]{:S(2)}) collective-permute-start(bf16[25,128,128]{2,1,0:T(8,128)(2,1)} %slice.593), channel_id=1, source_target_pairs={{0,8},{4,12},{1,9},{5,13},{2,10},{6,14},{3,11},{7,15}} | collective-permute-start | bytes 2457608 | tf_op jit(solution)/shard_map/ppermute | solution.py:220
  951.9 42.1 %collective-permute-start.92 = (bf16[48,128,128]{2,1,0:T(8,128)(2,1)}, bf16[48,128,128]{2,1,0:T(8,128)(2,1)S(1)}, u32[]{:S(2)}, u32[]{:S(2)}) collective-permute-start(bf16[48,128,128]{2,1,0:T(8,128)(2,1)} %pad_maximum_fusion.6), channel_id=1, source_target_pairs={{0,4},{4,0},{8,12},{12,8},{16,20},{20,16},{24,28},{28,24},{1,5},{5... | collective-permute-start | bytes 4718600 | tf_op jit(solution)/shard_map/ppermute | solution.py:185
  952.8 41.2 %collective-permute-start.93 = (bf16[48,128,128]{2,1,0:T(8,128)(2,1)}, bf16[48,128,128]{2,1,0:T(8,128)(2,1)}, u32[]{:S(2)}, u32[]{:S(2)}) collective-permute-start(bf16[48,128,128]{2,1,0:T(8,128)(2,1)} %pad_maximum_fusion.7), channel_id=1, source_target_pairs={{0,2},{2,0},{1,3},{3,1},{4,6},{6,4},{5,7},{7,5},{8,10},{10,8},{9,1... | collective-permute-start | bytes 4718600 | tf_op jit(solution)/shard_map/ppermute | solution.py:181
  1014.7 39.9 %collective-permute-start.103 = (bf16[48,128,128]{2,1,0:T(8,128)(2,1)}, bf16[48,128,128]{2,1,0:T(8,128)(2,1)}, u32[]{:S(2)}, u32[]{:S(2)}) collective-permute-start(bf16[48,128,128]{2,1,0:T(8,128)(2,1)} %pad_maximum_fusion.8), channel_id=1, source_target_pairs={{0,4},{4,0},{8,12},{12,8},{16,20},{20,16},{24,28},{28,24},{1,5},{5... | collective-permute-start | bytes 4718600 | tf_op jit(solution)/shard_map/ppermute | solution.py:185
  1015.8 38.9 %collective-permute-start.104 = (bf16[48,128,128]{2,1,0:T(8,128)(2,1)}, bf16[48,128,128]{2,1,0:T(8,128)(2,1)}, u32[]{:S(2)}, u32[]{:S(2)}) collective-permute-start(bf16[48,128,128]{2,1,0:T(8,128)(2,1)} %pad_maximum_fusion.9), channel_id=1, source_target_pairs={{0,2},{2,0},{1,3},{3,1},{4,6},{6,4},{5,7},{7,5},{8,10},{10,8},{9,1... | collective-permute-start | bytes 4718600 | tf_op jit(solution)/shard_map/ppermute | solution.py:181
  1016.6 38.0 %collective-permute-start.105 = (bf16[48,128,128]{2,1,0:T(8,128)(2,1)}, bf16[48,128,128]{2,1,0:T(8,128)(2,1)}, u32[]{:S(2)}, u32[]{:S(2)}) collective-permute-start(bf16[48,128,128]{2,1,0:T(8,128)(2,1)} %fusion.18), channel_id=1, source_target_pairs={{0,8},{4,12},{1,9},{5,13},{2,10},{6,14},{3,11},{7,15}} | collective-permute-start | bytes 4718600 | tf_op jit(solution)/shard_map/ppermute | solution.py:220
  1122.2 34.0 %collective-permute-start.116 = (bf16[48,128,128]{2,1,0:T(8,128)(2,1)}, bf16[48,128,128]{2,1,0:T(8,128)(2,1)}, u32[]{:S(2)}, u32[]{:S(2)}) collective-permute-start(bf16[48,128,128]{2,1,0:T(8,128)(2,1)} %get-tuple-element.613), channel_id=1, source_target_pairs={{0,8},{4,12},{8,16},{12,20},{16,24},{20,28},{1,9},{5,13},{9,17},{1... | collective-permute-start | bytes 4718600 | tf_op jit(solution)/shard_map/ppermute | solution.py:220
  1127.7 33.7 %collective-permute-start.117 = (bf16[48,128,128]{2,1,0:T(8,128)(2,1)}, bf16[48,128,128]{2,1,0:T(8,128)(2,1)}, u32[]{:S(2)}, u32[]{:S(2)}) collective-permute-start(bf16[48,128,128]{2,1,0:T(8,128)(2,1)} %get-tuple-element.614), channel_id=1, source_target_pairs={{8,0},{12,4},{16,8},{20,12},{24,16},{28,20},{9,1},{13,5},{17,9},{2... | collective-permute-start | bytes 4718600 | tf_op jit(solution)/shard_map/ppermute | solution.py:220
  (213 other events, 2776.9 us)

commit v5 on v4

--- a/solution.py
+++ b/solution.py
@@ -327,17 +327,21 @@
             (first, at + 3 * early),
             (second, at + 3 * early + half),
         ]
-        tokens.append(place_early(group))
-    line = jnp.concatenate([late_line.block(rel) for rel in range(4)], 0)
+        earlier = ()
+        if rel == 3:
+            late = jnp.concatenate([late_line.block(other) for other in range(4)], 0)
+            earlier = (late,)
+        tokens.append(place_early(group, *earlier))
+    line = late
     count = line.shape[0]
     half = count // 2
     by_x, by_y = lanes.step([(swap_x, line), (swap_y, line)])
     place_late([(line, 0)])
 
-    def finish():
+    def finish(*earlier):
         first, second = lanes.step([(swap_y, by_x[:half]), (swap_x, by_y[half:])])
         place_late([(by_y, count), (by_x, 2 * count)])
-        place_late([(first, 3 * count), (second, 3 * count + half)])
+        place_late([(first, 3 * count), (second, 3 * count + half)], *earlier)
 
     return rest, finish, (by_x, by_y)
 
@@ -622,7 +626,9 @@
     return pltpu.CompilerParams(vmem_limit_bytes=BIG)
 
 
-def attend_kernel(normed_in, qkv_tiles, proj_tiles, projected, attended, partial, w_qkv, w_proj):
+def attend_kernel(normed_in, qkv_tiles, proj_tiles, *refs):
+    projected, attended, partial, w_qkv, w_proj = refs[-5:]
+
     @pl.when(pl.program_id(0) == 0)
     def _():
         untile_into(w_qkv, qkv_tiles)
@@ -646,7 +652,7 @@
     partial[...] = product(result, w_proj[...])
 
 
-def attend_call(normed_in, store, tp_parts, local_len):
+def attend_call(normed_in, store, tp_parts, local_len, earlier=()):
     rows = normed_in.shape[0]
     width = D // tp_parts
     return pl.pallas_call(
@@ -656,7 +662,8 @@
             rows_spec(local_len, D),
             weight_spec(0, tp_parts),
             weight_spec(1, tp_parts),
-        ],
+        ]
+        + [pl.BlockSpec(memory_space=pl.ANY)] * len(earlier),
         out_specs=[
             rows_spec(local_len, 3 * width),
             rows_spec(local_len, width),
@@ -675,7 +682,7 @@
         cost_estimate=pl.CostEstimate(
             flops=rows * D * width * 8, bytes_accessed=rows * D * 8, transcendentals=rows * 2048
         ),
-    )(normed_in, store, store)
+    )(normed_in, store, store, *earlier)
 
 
 def attend_back_kernel(
@@ -1008,13 +1015,14 @@
     ]
 
 
-def place_call(pieces, targets, held):
+def place_call(pieces, targets, held, earlier=()):
     count = len(pieces)
     given = [array for _, _, array in held if array is not None]
 
     def kernel(target, *refs):
-        outs = refs[count + len(given) : count + len(given) + len(held)]
-        token = refs[count + len(given) + len(held)]
+        begin_outs = count + len(given) + len(earlier)
+        outs = refs[begin_outs : begin_outs + len(held)]
+        token = refs[begin_outs + len(held)]
         buffers, loaded, stored = refs[-2 - count : -2], refs[-2], refs[-1]
         token[...] = jnp.zeros_like(token)
         for number in range(count):
@@ -1050,7 +1058,7 @@
             ).wait()
 
     anywhere = pl.BlockSpec(memory_space=pl.ANY)
-    operands = [targets] + [piece for piece, _ in pieces] + given
+    operands = [targets] + [piece for piece, _ in pieces] + given + list(earlier)
     aliases = {}
     for number, (_, _, array) in enumerate(held):
         if array is not None:
@@ -1327,17 +1335,17 @@
         stores = [(0, per_layer + 1, None), (per_layer, per_layer + 1, None)]
         late_store = None
 
-        def place_early_tiles(tile_group):
+        def place_early_tiles(tile_group, *earlier):
             nonlocal stores
-            stores, token = place_call(tile_group, targets, stores)
+            stores, token = place_call(tile_group, targets, stores, earlier)
             return token
 
-        def place_late_tiles(tile_group):
+        def place_late_tiles(tile_group, *earlier):
             nonlocal late_store
             tile_group = [(piece, 16 * early + at) for piece, at in tile_group]
             if late_store is None:
                 late_store = [stores[1]]
-            late_store, token = place_call(tile_group, targets, late_store)
+            late_store, token = place_call(tile_group, targets, late_store, earlier)
             return token
 
         late_store = None
@@ -1396,7 +1404,14 @@
     for layer_no in range(L):
         row_sets = rows_in(normed_in.reshape(sp_rows, D))
         halves, terms = each_half(
-            lambda rows: attend_call(rows, store[layer_no], tp_parts, local_len), row_sets
+            lambda rows: attend_call(
+                rows,
+                store[layer_no],
+                tp_parts,
+                local_len,
+                arriving if box and layer_no == 0 and rows is row_sets[0] else (),
+            ),
+            row_sets,
         )
         branch, middle, normed_mid = residual_call(
             stream,
@@ -1406,7 +1421,6 @@
             modes[layer_no],
             3,
             4,
-            arriving if box and layer_no == 0 else (),
         )
         mid_sets = rows_in(normed_mid.reshape(sp_rows, D))
         hidden, terms = each_half(
@@ -1415,7 +1429,7 @@
         last = layer_no == L - 1
         if not last:
             if box:
-                finish_gather()
+                finish_gather(terms[0])
                 store[1] = late_store[0][2]
             modes.append(modes_of(layer_no + 1))
         mlp_out, stream_new, normed_in = residual_call(

time: 1230 us -> 1230 us (level)
    unnamed x262 -> x250, local copies, waits for them, and re-layouts: 38 us -> 35.7 us
  transfers between devices with their start and end apart: 118 -> 118, of which waited for: 47 -> 48; matrix products, arithmetic and copies ran while one was open for 23% -> 23% of each run, Pallas kernels for 21% -> 22%
where the time goes in v5:
time: 1230 us; the launch traced here: 1210 us
  Pallas kernels  401 us (33%)
  waiting for transfers between devices  304 us (25%)
  local copies, waits for them, and re-layouts  182 us (15%)
  other arithmetic  148 us (12%)
  starting transfers between devices  141 us (11%)
  matrix products  28.2 us (2%)
    ppermute x39, waiting for transfers between devices, swap_f(): lax.ppermute(value, 'fsdp', [(place, place ^ bit) for place in range(8)])  144 us
    ppermute x26, waiting for transfers between devices, swap_y(): return lax.ppermute(value, 'ctx', [(0, 1), (1, 0)])  112 us
    pallas_call x10, Pallas kernels, weight_grad_call(): pl.pallas_call(kernel, grid_spec=pltpu.PrefetchScalarGridSpec(num_scalar_...  82.9 us
    ppermute x24, starting transfers between devices, move_z(): return lambda value: lax.ppermute(value, 'fsdp', pairs)  60.8 us
    pallas_call x4, Pallas kernels, attend_back_call(): pl.pallas_call(attend_back_kernel, grid=(rows // local_len,), in_specs=[r...  55.6 us
    pallas_call x10, Pallas kernels, rows_kernel_call(): pl.pallas_call(body, grid=(own,), in_specs=[rows] * len(wide_ins) + [few(...  51.9 us
    ppermute x39, starting transfers between devices, swap_f(): lax.ppermute(value, 'fsdp', [(place, place ^ bit) for place in range(8)])  51.2 us
    pallas_call x4, Pallas kernels, mlp_back_call(): pl.pallas_call(mlp_back_kernel, grid=(width // step_width,), in_specs=[al...  50.4 us
  transfers between devices with their start and end apart: 118, of which 48 were waited for; matrix products, arithmetic and copies ran while one was open for 23% of the time, Pallas kernels for 22%

profile of v5, /device:TPU:0, one launch (start us, length us, event | category | flops | bytes accessed | tf_op | source)
XLA Modules:
  0.0 1213.6 jit_solution(3172043341211637261)
XLA Ops:
  30.3 10.0 collective-permute-done.9.refs_1_
  59.1 13.0 %collective-permute-done.13 = bf16[1,1090,128]{2,1,0:T(8,128)(2,1)} collective-permute-done((bf16[1,1090,128]{2,1,0:T(8,128)(2,1)S(1)}, bf16[1,1090,128]{2,1,0:T(8,128)(2,1)}, u32[]{:S(2)}, u32[]{:S(2)}) %collective-permute-start.13) | collective-permute-done | bytes 279072 | tf_op jit(solution)/shard_map/ppermute | solution.py:185
  87.5 12.1 collective-permute-done.18
  114.9 10.0 collective-permute-done.19
  133.5 10.2 copy.111
  185.8 26.3 %collective-permute-done.33.refs_1_ = bf16[47,128,128]{2,1,0:T(8,128)(2,1)} collective-permute-done((bf16[47,128,128]{2,1,0:T(8,128)(2,1)}, bf16[47,128,128]{2,1,0:T(8,128)(2,1)}, u32[]{:S(2)}, u32[]{:S(2)}) %collective-permute-start.33) | collective-permute-done | bytes 1540128 | tf_op jit(solution)/shard_map/ppermute | solution.py:181
  278.5 15.6 %reshape.497 = bf16[4360,1024]{1,0:T(8,128)(2,1)} reshape(bf16[4,2,2,2,1090,128]{5,4,3,2,1,0:T(8,128)(2,1)} %copy.114) | data formatting | bytes 17858560 | tf_op jit(solution)/shard_map/reshape | solution.py:513
  346.8 55.3 %collective-permute-done.45.refs_0_.refs_1_ = bf16[100,128,128]{2,1,0:T(8,128)(2,1)} collective-permute-done((bf16[100,128,128]{2,1,0:T(8,128)(2,1)S(1)}, bf16[100,128,128]{2,1,0:T(8,128)(2,1)}, u32[]{:S(2)}, u32[]{:S(2)}) %collective-permute-start.45) | collective-permute-done | bytes 3276832 | tf_op jit(solution)/shard_map/ppermute | solution.py:185
  423.9 10.5 shard_map.223
  445.4 10.6 shard_map.222
  511.1 10.6 shard_map.233
  530.2 11.0 shard_map.232
  559.8 12.5 %shard_map.237 = (bf16[512,2048]{1,0:T(8,128)(2,1)}, bf16[512,2048]{1,0:T(8,128)(2,1)}, f32[512,1024]{1,0:T(8,128)}) custom-call(bf16[512,1024]{1,0:T(8,128)(2,1)} %copy-done.49, f32[512,2048]{1,0:T(8,128)} %get-tuple-element.512.hidden, bf16[577,128,128]{2,1,0:T(8,128)(2,1)} %get-tuple-element.497.tile_set.qkv_tiles.proj_tiles.up_tiles.down_tiles, ...), custom_call_target="tpu_custom_call" | custom-call | flops 4294967296 | bytes 16777216 | tf_op jit(solution)/shard_map/pallas_call | solution.py:839
  572.5 12.6 %shard_map.236 = (bf16[512,2048]{1,0:T(8,128)(2,1)}, bf16[512,2048]{1,0:T(8,128)(2,1)}, f32[512,1024]{1,0:T(8,128)}) custom-call(bf16[512,1024]{1,0:T(8,128)(2,1)} %bitcast.205, f32[512,2048]{1,0:T(8,128)} %get-tuple-element.510.hidden, bf16[577,128,128]{2,1,0:T(8,128)(2,1)} %get-tuple-element.497.tile_set.qkv_tiles.proj_tiles.up_tiles.down_tiles, ...), custom_call_target="tpu_custom_call" | custom-call | flops 4294967296 | bytes 16777216 | tf_op jit(solution)/shard_map/pallas_call | solution.py:839
  597.1 14.0 %shard_map.240 = (bf16[512,1536]{1,0:T(8,128)(2,1)}, f32[512,1024]{1,0:T(8,128)}) custom-call(bf16[512,1024]{1,0:T(8,128)(2,1)} %copy-done.24, bf16[512,1536]{1,0:T(8,128)(2,1)} %get-tuple-element.519.projected, bf16[577,128,128]{2,1,0:T(8,128)(2,1)} %get-tuple-element.497.tile_set.qkv_tiles.proj_tiles.up_tiles.down_tiles, ...), custom_call_target="tpu_custom_call" | custom-call | flops 2684354560 | bytes 4194304 | tf_op jit(solution)/shard_map/pallas_call | solution.py:725
  612.1 10.0 shard_map.242
  622.0 10.6 shard_map.243
  632.7 13.8 %shard_map.239 = (bf16[512,1536]{1,0:T(8,128)(2,1)}, f32[512,1024]{1,0:T(8,128)}) custom-call(bf16[512,1024]{1,0:T(8,128)(2,1)} %bitcast.174, bf16[512,1536]{1,0:T(8,128)(2,1)} %get-tuple-element.517.projected, bf16[577,128,128]{2,1,0:T(8,128)(2,1)} %get-tuple-element.497.tile_set.qkv_tiles.proj_tiles.up_tiles.down_tiles, ...), custom_call_target="tpu_custom_call" | custom-call | flops 2684354560 | bytes 4194304 | tf_op jit(solution)/shard_map/pallas_call | solution.py:725
  691.0 12.5 %shard_map.248 = (bf16[512,2048]{1,0:T(8,128)(2,1)}, bf16[512,2048]{1,0:T(8,128)(2,1)}, f32[512,1024]{1,0:T(8,128)}) custom-call(bf16[512,1024]{1,0:T(8,128)(2,1)} %copy-done.23, f32[512,2048]{1,0:T(8,128)} %get-tuple-element.548.hidden, bf16[577,128,128]{2,1,0:T(8,128)(2,1)} %get-tuple-element.483.tile_set.qkv_tiles.proj_tiles.up_tiles.down_tiles, ...), custom_call_target="tpu_custom_call" | custom-call | flops 4294967296 | bytes 16777216 | tf_op jit(solution)/shard_map/pallas_call | solution.py:839
  713.0 12.8 %shard_map.247 = (bf16[512,2048]{1,0:T(8,128)(2,1)}, bf16[512,2048]{1,0:T(8,128)(2,1)}, f32[512,1024]{1,0:T(8,128)}) custom-call(bf16[512,1024]{1,0:T(8,128)(2,1)} %bitcast.170, f32[512,2048]{1,0:T(8,128)} %get-tuple-element.546.hidden, bf16[577,128,128]{2,1,0:T(8,128)(2,1)} %get-tuple-element.483.tile_set.qkv_tiles.proj_tiles.up_tiles.down_tiles, ...), custom_call_target="tpu_custom_call" | custom-call | flops 4294967296 | bytes 16777216 | tf_op jit(solution)/shard_map/pallas_call | solution.py:839
  747.5 13.8 %shard_map.251 = (bf16[512,1536]{1,0:T(8,128)(2,1)}, f32[512,1024]{1,0:T(8,128)}) custom-call(bf16[512,1024]{1,0:T(8,128)(2,1)} %copy-done.27, bf16[512,1536]{1,0:T(8,128)(2,1)} %get-tuple-element.555.projected, bf16[577,128,128]{2,1,0:T(8,128)(2,1)} %get-tuple-element.483.tile_set.qkv_tiles.proj_tiles.up_tiles.down_tiles, ...), custom_call_target="tpu_custom_call" | custom-call | flops 2684354560 | bytes 4194304 | tf_op jit(solution)/shard_map/pallas_call | solution.py:725
  761.4 9.6 shard_map.254.refs_4_
  778.0 10.1 shard_map.255.refs_4_
  792.6 14.0 %shard_map.250 = (bf16[512,1536]{1,0:T(8,128)(2,1)}, f32[512,1024]{1,0:T(8,128)}) custom-call(bf16[512,1024]{1,0:T(8,128)(2,1)} %bitcast.184, bf16[512,1536]{1,0:T(8,128)(2,1)} %get-tuple-element.553.projected, bf16[577,128,128]{2,1,0:T(8,128)(2,1)} %get-tuple-element.483.tile_set.qkv_tiles.proj_tiles.up_tiles.down_tiles, ...), custom_call_target="tpu_custom_call" | custom-call | flops 2684354560 | bytes 4194304 | tf_op jit(solution)/shard_map/pallas_call | solution.py:725
  872.2 9.6 collective-permute-start.81
  891.1 15.5 %collective-permute-done.83 = f32[16,2304]{1,0:T(8,128)} collective-permute-done((f32[16,2304]{1,0:T(8,128)}, f32[16,2304]{1,0:T(8,128)}, u32[]{:S(2)}, u32[]{:S(2)}) %collective-permute-start.83) | collective-permute-done | bytes 147488 | tf_op jit(solution)/shard_map/ppermute | solution.py:181
  970.8 13.1 %collective-permute-done.94 = bf16[25,128,128]{2,1,0:T(8,128)(2,1)S(1)} collective-permute-done((bf16[25,128,128]{2,1,0:T(8,128)(2,1)}, bf16[25,128,128]{2,1,0:T(8,128)(2,1)S(1)}, u32[]{:S(2)}, u32[]{:S(2)}) %collective-permute-start.94) | collective-permute-done | bytes 819232 | tf_op jit(solution)/shard_map/ppermute | solution.py:220
  1036.4 11.2 slice.503
  1057.5 11.3 collective-permute-done.107
  1083.5 25.2 %collective-permute-done.110 = bf16[48,128,128]{2,1,0:T(8,128)(2,1)S(1)} collective-permute-done((bf16[48,128,128]{2,1,0:T(8,128)(2,1)S(1)}, bf16[48,128,128]{2,1,0:T(8,128)(2,1)S(1)}, u32[]{:S(2)}, u32[]{:S(2)}) %collective-permute-start.110) | collective-permute-done | bytes 1572896 | tf_op jit(solution)/shard_map/ppermute | solution.py:185
  1134.2 13.2 %collective-permute-done.114 = bf16[48,128,128]{2,1,0:T(8,128)(2,1)} collective-permute-done((bf16[48,128,128]{2,1,0:T(8,128)(2,1)}, bf16[48,128,128]{2,1,0:T(8,128)(2,1)}, u32[]{:S(2)}, u32[]{:S(2)}) %collective-permute-start.114) | collective-permute-done | bytes 1572896 | tf_op jit(solution)/shard_map/ppermute | solution.py:185
  1194.9 17.5 %shard_map.260 = (f32[72,128,128]{2,1,0:T(8,128)}, f32[72,128,128]{2,1,0:T(8,128)}, f32[72,128,128]{2,1,0:T(8,128)}, bf16[72,128,128]{2,1,0:T(8,128)(2,1)}) custom-call(f32[1,1]{1,0:T(1,128)} %bitcast.66.clip, f32[72,128,128]{2,1,0:T(8,128)} %get-tuple-element.615.grad, f32[72,128,128]{2,1,0:T(8,128)} %bitcast.161, f32[72,128,128]{2,1,0:T(8,128)} %bitcast.162, ...), custom_call_target="tpu_custom_call" | custom-call | flops 35389440 | bytes 35389440 | tf_op jit(solution)/shard_map/pallas_call | solution.py:1265
  (732 shorter events, 747.6 us)
Async XLA Ops:
  3.4 37.0 %collective-permute-start.9 = (bf16[47,128,128]{2,1,0:T(8,128)(2,1)}, bf16[47,128,128]{2,1,0:T(8,128)(2,1)}, u32[]{:S(2)}, u32[]{:S(2)}) collective-permute-start(bf16[47,128,128]{2,1,0:T(8,128)(2,1)} %slice_bitcast_fusion.refs_0_), channel_id=1, source_target_pairs={{0,2},{2,0},{1,3},{3,1},{4,6},{6,4},{5,7},{7,5},{8,10},{10,8},{9,1... | collective-permute-start | bytes 4620296 | tf_op jit(solution)/shard_map/ppermute | solution.py:181
  6.3 36.1 %collective-permute-start.8 = (bf16[47,128,128]{2,1,0:T(8,128)(2,1)}, bf16[47,128,128]{2,1,0:T(8,128)(2,1)}, u32[]{:S(2)}, u32[]{:S(2)}) collective-permute-start(bf16[47,128,128]{2,1,0:T(8,128)(2,1)} %slice_bitcast_fusion.refs_0_), channel_id=1, source_target_pairs={{0,4},{4,0},{8,12},{12,8},{16,20},{20,16},{24,28},{28,24},{1,5},{5... | collective-permute-start | bytes 4620296 | tf_op jit(solution)/shard_map/ppermute | solution.py:185
  7.8 36.7 %collective-permute-start.10 = (bf16[47,128,128]{2,1,0:T(8,128)(2,1)}, bf16[47,128,128]{2,1,0:T(8,128)(2,1)S(1)}, u32[]{:S(2)}, u32[]{:S(2)}) collective-permute-start(bf16[47,128,128]{2,1,0:T(8,128)(2,1)} %slice_bitcast_fusion.refs_0_), channel_id=1, source_target_pairs={{0,8},{4,12},{8,16},{12,20},{16,24},{20,28},{1,9},{5,13},{9,17},{1... | collective-permute-start | bytes 4620296 | tf_op jit(solution)/shard_map/ppermute | solution.py:220
  11.4 36.7 %collective-permute-start.11 = (bf16[47,128,128]{2,1,0:T(8,128)(2,1)}, bf16[47,128,128]{2,1,0:T(8,128)(2,1)S(1)}, u32[]{:S(2)}, u32[]{:S(2)}) collective-permute-start(bf16[47,128,128]{2,1,0:T(8,128)(2,1)} %slice_bitcast_fusion.refs_0_), channel_id=1, source_target_pairs={{8,0},{12,4},{16,8},{20,12},{24,16},{28,20},{9,1},{13,5},{17,9},{2... | collective-permute-start | bytes 4620296 | tf_op jit(solution)/shard_map/ppermute | solution.py:220
  111.0 38.6 %collective-permute-start.22 = (bf16[47,128,128]{2,1,0:T(8,128)(2,1)}, bf16[47,128,128]{2,1,0:T(8,128)(2,1)S(1)}, u32[]{:S(2)}, u32[]{:S(2)}) collective-permute-start(bf16[47,128,128]{2,1,0:T(8,128)(2,1)} %broadcast_select_fusion.2.refs_0_), channel_id=1, source_target_pairs={{0,2},{2,0},{1,3},{3,1},{4,6},{6,4},{5,7},{7,5},{8,10},{10,8},{9,1... | collective-permute-start | bytes 4620296 | tf_op jit(solution)/shard_map/ppermute | solution.py:181
  112.5 39.2 %collective-permute-start.23 = (bf16[47,128,128]{2,1,0:T(8,128)(2,1)}, bf16[47,128,128]{2,1,0:T(8,128)(2,1)S(1)}, u32[]{:S(2)}, u32[]{:S(2)}) collective-permute-start(bf16[47,128,128]{2,1,0:T(8,128)(2,1)} %broadcast_select_fusion.2.refs_0_), channel_id=1, source_target_pairs={{0,4},{4,0},{8,12},{12,8},{16,20},{20,16},{24,28},{28,24},{1,5},{5... | collective-permute-start | bytes 4620296 | tf_op jit(solution)/shard_map/ppermute | solution.py:185
  113.0 40.7 %collective-permute-start.24 = (bf16[47,128,128]{2,1,0:T(8,128)(2,1)}, bf16[47,128,128]{2,1,0:T(8,128)(2,1)}, u32[]{:S(2)}, u32[]{:S(2)}) collective-permute-start(bf16[47,128,128]{2,1,0:T(8,128)(2,1)} %copy-done.11), channel_id=1, source_target_pairs={{8,16},{12,20},{16,24},{20,28},{9,17},{13,21},{17,25},{21,29},{10,... | collective-permute-start | bytes 4620296 | tf_op jit(solution)/shard_map/ppermute | solution.py:220
  143.7 112.7 %collective-permute-start.21 = (bf16[4,2,2,1090,128]{4,0,3,2,1:T(4,128)(2,1)}, bf16[4,2,2,1090,128]{4,0,3,2,1:T(4,128)(2,1)}, u32[]{:S(2)}, u32[]{:S(2)}) collective-permute-start(bf16[4,2,2,1090,128]{4,0,3,2,1:T(4,128)(2,1)} %copy.111), channel_id=1, source_target_pairs={{0,1},{1,0},{2,3},{3,2},{4,5},{5,4},{6,7},{7,6},{8,9},{9,8},{10,11... | collective-permute-start | bytes 13393928 | tf_op jit(solution)/shard_map/ppermute | solution.py:177
  182.3 34.0 %collective-permute-start.30 = (bf16[47,128,128]{2,1,0:T(8,128)(2,1)}, bf16[47,128,128]{2,1,0:T(8,128)(2,1)}, u32[]{:S(2)}, u32[]{:S(2)}) collective-permute-start(bf16[47,128,128]{2,1,0:T(8,128)(2,1)} %collective-permute-done.25), channel_id=1, source_target_pairs={{8,0},{12,4},{9,1},{13,5},{10,2},{14,6},{11,3},{15,7}} | collective-permute-start | bytes 4620296 | tf_op jit(solution)/shard_map/ppermute | solution.py:220
  248.1 51.6 %collective-permute-start.40 = (bf16[25,128,128]{2,1,0:T(8,128)(2,1)}, bf16[25,128,128]{2,1,0:T(8,128)(2,1)}, u32[]{:S(2)}, u32[]{:S(2)}) collective-permute-start(bf16[25,128,128]{2,1,0:T(8,128)(2,1)} %collective-permute-done.34), channel_id=1, source_target_pairs={{16,24},{20,28},{17,25},{21,29},{18,26},{22,30},{19,27},{23,31}} | collective-permute-start | bytes 2457608 | tf_op jit(solution)/shard_map/ppermute | solution.py:220
  249.8 49.9 %collective-permute-start.41 = (bf16[25,128,128]{2,1,0:T(8,128)(2,1)}, bf16[25,128,128]{2,1,0:T(8,128)(2,1)}, u32[]{:S(2)}, u32[]{:S(2)}) collective-permute-start(bf16[25,128,128]{2,1,0:T(8,128)(2,1)} %collective-permute-done.35), channel_id=1, source_target_pairs={{8,0},{12,4},{9,1},{13,5},{10,2},{14,6},{11,3},{15,7}} | collective-permute-start | bytes 2457608 | tf_op jit(solution)/shard_map/ppermute | solution.py:220
  251.1 46.1 %collective-permute-start.38 = (bf16[47,128,128]{2,1,0:T(8,128)(2,1)}, bf16[47,128,128]{2,1,0:T(8,128)(2,1)}, u32[]{:S(2)}, u32[]{:S(2)}) collective-permute-start(bf16[47,128,128]{2,1,0:T(8,128)(2,1)} %select_select_fusion.refs_0_), channel_id=1, source_target_pairs={{0,2},{2,0},{1,3},{3,1},{4,6},{6,4},{5,7},{7,5},{8,10},{10,8},{9,1... | collective-permute-start | bytes 4620296 | tf_op jit(solution)/shard_map/ppermute | solution.py:181
  254.9 43.6 %collective-permute-start.39 = (bf16[47,128,128]{2,1,0:T(8,128)(2,1)}, bf16[47,128,128]{2,1,0:T(8,128)(2,1)}, u32[]{:S(2)}, u32[]{:S(2)}) collective-permute-start(bf16[47,128,128]{2,1,0:T(8,128)(2,1)} %select_select_fusion.refs_0_), channel_id=1, source_target_pairs={{0,4},{4,0},{8,12},{12,8},{16,20},{20,16},{24,28},{28,24},{1,5},{5... | collective-permute-start | bytes 4620296 | tf_op jit(solution)/shard_map/ppermute | solution.py:185
  328.6 73.4 %collective-permute-start.45 = (bf16[100,128,128]{2,1,0:T(8,128)(2,1)S(1)}, bf16[100,128,128]{2,1,0:T(8,128)(2,1)}, u32[]{:S(2)}, u32[]{:S(2)}) collective-permute-start(bf16[100,128,128]{2,1,0:T(8,128)(2,1)S(1)} %copy-done.3), channel_id=1, source_target_pairs={{0,4},{4,0},{8,12},{12,8},{16,20},{20,16},{24,28},{28,24},{1,5},{5... | collective-permute-start | bytes 9830408 | tf_op jit(solution)/shard_map/ppermute | solution.py:185
  329.9 73.1 %collective-permute-start.46 = (bf16[100,128,128]{2,1,0:T(8,128)(2,1)S(1)}, bf16[100,128,128]{2,1,0:T(8,128)(2,1)}, u32[]{:S(2)}, u32[]{:S(2)}) collective-permute-start(bf16[100,128,128]{2,1,0:T(8,128)(2,1)S(1)} %copy-done.3), channel_id=1, source_target_pairs={{0,2},{2,0},{1,3},{3,1},{4,6},{6,4},{5,7},{7,5},{8,10},{10,8},{9,1... | collective-permute-start | bytes 9830408 | tf_op jit(solution)/shard_map/ppermute | solution.py:181
  346.7 65.3 %collective-permute-start.48 = (f32[512,1024]{1,0:T(8,128)}, f32[512,1024]{1,0:T(8,128)S(1)}, u32[]{:S(2)}, u32[]{:S(2)}) collective-permute-start(f32[512,1024]{1,0:T(8,128)} %get-tuple-element.487), channel_id=1, source_target_pairs={{0,1},{1,0},{2,3},{3,2},{4,5},{5,4},{6,7},{7,6},{8,9},{9,8},{10,11... | collective-permute-start | bytes 6291464 | tf_op jit(solution)/shard_map/ppermute | solution.py:177
  421.5 38.4 %collective-permute-start.51 = (bf16[50,128,128]{2,1,0:T(8,128)(2,1)S(1)}, bf16[50,128,128]{2,1,0:T(8,128)(2,1)}, u32[]{:S(2)}, u32[]{:S(2)}) collective-permute-start(bf16[50,128,128]{2,1,0:T(8,128)(2,1)S(1)} %slice.444), channel_id=1, source_target_pairs={{0,2},{2,0},{1,3},{3,1},{4,6},{6,4},{5,7},{7,5},{8,10},{10,8},{9,1... | collective-permute-start | bytes 4915208 | tf_op jit(solution)/shard_map/ppermute | solution.py:181
  422.1 38.0 %collective-permute-start.52 = (bf16[50,128,128]{2,1,0:T(8,128)(2,1)S(1)}, bf16[50,128,128]{2,1,0:T(8,128)(2,1)}, u32[]{:S(2)}, u32[]{:S(2)}) collective-permute-start(bf16[50,128,128]{2,1,0:T(8,128)(2,1)S(1)} %slice.445), channel_id=1, source_target_pairs={{0,4},{4,0},{8,12},{12,8},{16,20},{20,16},{24,28},{28,24},{1,5},{5... | collective-permute-start | bytes 4915208 | tf_op jit(solution)/shard_map/ppermute | solution.py:185
  434.4 38.4 %collective-permute-start.50 = (f32[512,1024]{1,0:T(8,128)}, f32[512,1024]{1,0:T(8,128)S(1)}, u32[]{:S(2)}, u32[]{:S(2)}) collective-permute-start(f32[512,1024]{1,0:T(8,128)} %get-tuple-element.491), channel_id=1, source_target_pairs={{0,1},{1,0},{2,3},{3,2},{4,5},{5,4},{6,7},{7,6},{8,9},{9,8},{10,11... | collective-permute-start | bytes 6291464 | tf_op jit(solution)/shard_map/ppermute | solution.py:177
  611.1 41.5 %collective-permute-start.61 = (f32[512,1024]{1,0:T(8,128)}, f32[512,1024]{1,0:T(8,128)S(1)}, u32[]{:S(2)}, u32[]{:S(2)}) collective-permute-start(f32[512,1024]{1,0:T(8,128)} %get-tuple-element.520), channel_id=1, source_target_pairs={{0,1},{1,0},{2,3},{3,2},{4,5},{5,4},{6,7},{7,6},{8,9},{9,8},{10,11... | collective-permute-start | bytes 6291464 | tf_op jit(solution)/shard_map/ppermute | solution.py:177
  687.8 38.2 %collective-permute-start.67 = (bf16[50,128,128]{2,1,0:T(8,128)(2,1)}, bf16[50,128,128]{2,1,0:T(8,128)(2,1)}, u32[]{:S(2)}, u32[]{:S(2)}) collective-permute-start(bf16[50,128,128]{2,1,0:T(8,128)(2,1)} %get-tuple-element.558), channel_id=1, source_target_pairs={{0,2},{2,0},{1,3},{3,1},{4,6},{6,4},{5,7},{7,5},{8,10},{10,8},{9,1... | collective-permute-start | bytes 4915208 | tf_op jit(solution)/shard_map/ppermute | solution.py:181
  689.4 37.9 %collective-permute-start.68 = (bf16[50,128,128]{2,1,0:T(8,128)(2,1)}, bf16[50,128,128]{2,1,0:T(8,128)(2,1)}, u32[]{:S(2)}, u32[]{:S(2)}) collective-permute-start(bf16[50,128,128]{2,1,0:T(8,128)(2,1)} %get-tuple-element.559), channel_id=1, source_target_pairs={{0,4},{4,0},{8,12},{12,8},{16,20},{20,16},{24,28},{28,24},{1,5},{5... | collective-permute-start | bytes 4915208 | tf_op jit(solution)/shard_map/ppermute | solution.py:185
  742.3 81.1 %collective-permute-start.71 = (bf16[100,128,128]{2,1,0:T(8,128)(2,1)}, bf16[100,128,128]{2,1,0:T(8,128)(2,1)}, u32[]{:S(2)}, u32[]{:S(2)}) collective-permute-start(bf16[100,128,128]{2,1,0:T(8,128)(2,1)} %pad_maximum_fusion.4), channel_id=1, source_target_pairs={{0,4},{4,0},{8,12},{12,8},{16,20},{20,16},{24,28},{28,24},{1,5},{5... | collective-permute-start | bytes 9830408 | tf_op jit(solution)/shard_map/ppermute | solution.py:185
  743.0 80.5 %collective-permute-start.72 = (bf16[100,128,128]{2,1,0:T(8,128)(2,1)}, bf16[100,128,128]{2,1,0:T(8,128)(2,1)}, u32[]{:S(2)}, u32[]{:S(2)}) collective-permute-start(bf16[100,128,128]{2,1,0:T(8,128)(2,1)} %pad_maximum_fusion.5), channel_id=1, source_target_pairs={{0,2},{2,0},{1,3},{3,1},{4,6},{6,4},{5,7},{7,5},{8,10},{10,8},{9,1... | collective-permute-start | bytes 9830408 | tf_op jit(solution)/shard_map/ppermute | solution.py:181
  761.3 72.3 %collective-permute-start.66 = (f32[512,1024]{1,0:T(8,128)}, f32[512,1024]{1,0:T(8,128)S(1)}, u32[]{:S(2)}, u32[]{:S(2)}) collective-permute-start(f32[512,1024]{1,0:T(8,128)} %get-tuple-element.556), channel_id=1, source_target_pairs={{0,1},{1,0},{2,3},{3,2},{4,5},{5,4},{6,7},{7,6},{8,9},{9,8},{10,11... | collective-permute-start | bytes 6291464 | tf_op jit(solution)/shard_map/ppermute | solution.py:177
  872.2 38.9 %collective-permute-start.81 = (bf16[25,128,128]{2,1,0:T(8,128)(2,1)}, bf16[25,128,128]{2,1,0:T(8,128)(2,1)}, u32[]{:S(2)}, u32[]{:S(2)}) collective-permute-start(bf16[25,128,128]{2,1,0:T(8,128)(2,1)} %slice.593), channel_id=1, source_target_pairs={{0,8},{4,12},{1,9},{5,13},{2,10},{6,14},{3,11},{7,15}} | collective-permute-start | bytes 2457608 | tf_op jit(solution)/shard_map/ppermute | solution.py:220
  946.0 41.9 %collective-permute-start.92 = (bf16[48,128,128]{2,1,0:T(8,128)(2,1)}, bf16[48,128,128]{2,1,0:T(8,128)(2,1)S(1)}, u32[]{:S(2)}, u32[]{:S(2)}) collective-permute-start(bf16[48,128,128]{2,1,0:T(8,128)(2,1)} %pad_maximum_fusion.6), channel_id=1, source_target_pairs={{0,4},{4,0},{8,12},{12,8},{16,20},{20,16},{24,28},{28,24},{1,5},{5... | collective-permute-start | bytes 4718600 | tf_op jit(solution)/shard_map/ppermute | solution.py:185
  946.6 41.3 %collective-permute-start.93 = (bf16[48,128,128]{2,1,0:T(8,128)(2,1)}, bf16[48,128,128]{2,1,0:T(8,128)(2,1)}, u32[]{:S(2)}, u32[]{:S(2)}) collective-permute-start(bf16[48,128,128]{2,1,0:T(8,128)(2,1)} %pad_maximum_fusion.7), channel_id=1, source_target_pairs={{0,2},{2,0},{1,3},{3,1},{4,6},{6,4},{5,7},{7,5},{8,10},{10,8},{9,1... | collective-permute-start | bytes 4718600 | tf_op jit(solution)/shard_map/ppermute | solution.py:181
  1008.8 40.3 %collective-permute-start.103 = (bf16[48,128,128]{2,1,0:T(8,128)(2,1)}, bf16[48,128,128]{2,1,0:T(8,128)(2,1)}, u32[]{:S(2)}, u32[]{:S(2)}) collective-permute-start(bf16[48,128,128]{2,1,0:T(8,128)(2,1)} %pad_maximum_fusion.8), channel_id=1, source_target_pairs={{0,4},{4,0},{8,12},{12,8},{16,20},{20,16},{24,28},{28,24},{1,5},{5... | collective-permute-start | bytes 4718600 | tf_op jit(solution)/shard_map/ppermute | solution.py:185
  1010.2 39.0 %collective-permute-start.104 = (bf16[48,128,128]{2,1,0:T(8,128)(2,1)}, bf16[48,128,128]{2,1,0:T(8,128)(2,1)}, u32[]{:S(2)}, u32[]{:S(2)}) collective-permute-start(bf16[48,128,128]{2,1,0:T(8,128)(2,1)} %pad_maximum_fusion.9), channel_id=1, source_target_pairs={{0,2},{2,0},{1,3},{3,1},{4,6},{6,4},{5,7},{7,5},{8,10},{10,8},{9,1... | collective-permute-start | bytes 4718600 | tf_op jit(solution)/shard_map/ppermute | solution.py:181
  1011.0 38.2 %collective-permute-start.105 = (bf16[48,128,128]{2,1,0:T(8,128)(2,1)}, bf16[48,128,128]{2,1,0:T(8,128)(2,1)}, u32[]{:S(2)}, u32[]{:S(2)}) collective-permute-start(bf16[48,128,128]{2,1,0:T(8,128)(2,1)} %fusion.18), channel_id=1, source_target_pairs={{0,8},{4,12},{1,9},{5,13},{2,10},{6,14},{3,11},{7,15}} | collective-permute-start | bytes 4718600 | tf_op jit(solution)/shard_map/ppermute | solution.py:220
  1116.7 33.8 %collective-permute-start.116 = (bf16[48,128,128]{2,1,0:T(8,128)(2,1)}, bf16[48,128,128]{2,1,0:T(8,128)(2,1)}, u32[]{:S(2)}, u32[]{:S(2)}) collective-permute-start(bf16[48,128,128]{2,1,0:T(8,128)(2,1)} %get-tuple-element.613), channel_id=1, source_target_pairs={{0,8},{4,12},{8,16},{12,20},{16,24},{20,28},{1,9},{5,13},{9,17},{1... | collective-permute-start | bytes 4718600 | tf_op jit(solution)/shard_map/ppermute | solution.py:220
  (207 other events, 2771.9 us)

commit v6 on v5

--- a/solution.py
+++ b/solution.py
@@ -645,7 +645,7 @@
         value_rows = values[:, 2 * width + at : 2 * width + at + HD]
         scores = against_value(key_rows, query) * HD ** (-0.5)
         exponent = jnp.exp(scores - jnp.max(scores, 0, keepdims=True))
-        probabilities = low(exponent / jnp.sum(exponent, 0, keepdims=True))
+        probabilities = low(exponent * (1.0 / jnp.sum(exponent, 0, keepdims=True)))
         results.append(low(over_rows(probabilities, value_rows)))
     result = jnp.concatenate(results, 1)
     attended[...] = result
@@ -705,7 +705,7 @@
         grad_here = grad_attended[:, at : at + HD]
         scores = against_value(key_rows, query) * HD ** (-0.5)
         exponent = jnp.exp(scores - jnp.max(scores, 0, keepdims=True))
-        probabilities = exponent / jnp.sum(exponent, 0, keepdims=True)
+        probabilities = exponent * (1.0 / jnp.sum(exponent, 0, keepdims=True))
         grad_prob = against_value(value_rows, grad_here)
         grad_scores = low(
             probabilities

time: 1230 us -> 1230 us (level)
  no operation moved by 1% of the time
where the time goes in v6:
time: 1230 us; the launch traced here: 1210 us
  Pallas kernels  401 us (33%)
  waiting for transfers between devices  304 us (25%)
  local copies, waits for them, and re-layouts  182 us (15%)
  other arithmetic  148 us (12%)
  starting transfers between devices  141 us (11%)
  matrix products  28.2 us (2%)
    ppermute x39, waiting for transfers between devices, swap_f(): lax.ppermute(value, 'fsdp', [(place, place ^ bit) for place in range(8)])  144 us
    ppermute x26, waiting for transfers between devices, swap_y(): return lax.ppermute(value, 'ctx', [(0, 1), (1, 0)])  112 us
    pallas_call x10, Pallas kernels, weight_grad_call(): pl.pallas_call(kernel, grid_spec=pltpu.PrefetchScalarGridSpec(num_scalar_...  82.9 us
    ppermute x24, starting transfers between devices, move_z(): return lambda value: lax.ppermute(value, 'fsdp', pairs)  60.9 us
    pallas_call x4, Pallas kernels, attend_back_call(): pl.pallas_call(attend_back_kernel, grid=(rows // local_len,), in_specs=[r...  55.6 us
    pallas_call x10, Pallas kernels, rows_kernel_call(): pl.pallas_call(body, grid=(own,), in_specs=[rows] * len(wide_ins) + [few(...  51.9 us
    ppermute x39, starting transfers between devices, swap_f(): lax.ppermute(value, 'fsdp', [(place, place ^ bit) for place in range(8)])  51.1 us
    pallas_call x4, Pallas kernels, mlp_back_call(): pl.pallas_call(mlp_back_kernel, grid=(width // step_width,), in_specs=[al...  50.4 us
  transfers between devices with their start and end apart: 118, of which 48 were waited for; matrix products, arithmetic and copies ran while one was open for 23% of the time, Pallas kernels for 22%

profile of v6, /device:TPU:0, one launch (start us, length us, event | category | flops | bytes accessed | tf_op | source)
XLA Modules:
  0.0 1213.8 jit_solution(3172043341211637261)
XLA Ops:
  30.3 10.0 collective-permute-done.9.refs_1_
  59.1 13.0 %collective-permute-done.13 = bf16[1,1090,128]{2,1,0:T(8,128)(2,1)} collective-permute-done((bf16[1,1090,128]{2,1,0:T(8,128)(2,1)S(1)}, bf16[1,1090,128]{2,1,0:T(8,128)(2,1)}, u32[]{:S(2)}, u32[]{:S(2)}) %collective-permute-start.13) | collective-permute-done | bytes 279072 | tf_op jit(solution)/shard_map/ppermute | solution.py:185
  87.5 12.1 collective-permute-done.18
  114.9 10.0 collective-permute-done.19
  133.5 10.2 copy.111
  185.8 26.3 %collective-permute-done.33.refs_1_ = bf16[47,128,128]{2,1,0:T(8,128)(2,1)} collective-permute-done((bf16[47,128,128]{2,1,0:T(8,128)(2,1)}, bf16[47,128,128]{2,1,0:T(8,128)(2,1)}, u32[]{:S(2)}, u32[]{:S(2)}) %collective-permute-start.33) | collective-permute-done | bytes 1540128 | tf_op jit(solution)/shard_map/ppermute | solution.py:181
  278.5 15.6 %reshape.497 = bf16[4360,1024]{1,0:T(8,128)(2,1)} reshape(bf16[4,2,2,2,1090,128]{5,4,3,2,1,0:T(8,128)(2,1)} %copy.114) | data formatting | bytes 17858560 | tf_op jit(solution)/shard_map/reshape | solution.py:513
  346.9 55.1 %collective-permute-done.45.refs_0_.refs_1_ = bf16[100,128,128]{2,1,0:T(8,128)(2,1)} collective-permute-done((bf16[100,128,128]{2,1,0:T(8,128)(2,1)S(1)}, bf16[100,128,128]{2,1,0:T(8,128)(2,1)}, u32[]{:S(2)}, u32[]{:S(2)}) %collective-permute-start.45) | collective-permute-done | bytes 3276832 | tf_op jit(solution)/shard_map/ppermute | solution.py:185
  423.9 10.5 shard_map.223
  445.4 10.6 shard_map.222
  511.2 10.6 shard_map.233
  530.3 11.0 shard_map.232
  559.9 12.5 %shard_map.237 = (bf16[512,2048]{1,0:T(8,128)(2,1)}, bf16[512,2048]{1,0:T(8,128)(2,1)}, f32[512,1024]{1,0:T(8,128)}) custom-call(bf16[512,1024]{1,0:T(8,128)(2,1)} %copy-done.49, f32[512,2048]{1,0:T(8,128)} %get-tuple-element.512.hidden, bf16[577,128,128]{2,1,0:T(8,128)(2,1)} %get-tuple-element.497.tile_set.qkv_tiles.proj_tiles.up_tiles.down_tiles, ...), custom_call_target="tpu_custom_call" | custom-call | flops 4294967296 | bytes 16777216 | tf_op jit(solution)/shard_map/pallas_call | solution.py:839
  572.6 12.6 %shard_map.236 = (bf16[512,2048]{1,0:T(8,128)(2,1)}, bf16[512,2048]{1,0:T(8,128)(2,1)}, f32[512,1024]{1,0:T(8,128)}) custom-call(bf16[512,1024]{1,0:T(8,128)(2,1)} %bitcast.205, f32[512,2048]{1,0:T(8,128)} %get-tuple-element.510.hidden, bf16[577,128,128]{2,1,0:T(8,128)(2,1)} %get-tuple-element.497.tile_set.qkv_tiles.proj_tiles.up_tiles.down_tiles, ...), custom_call_target="tpu_custom_call" | custom-call | flops 4294967296 | bytes 16777216 | tf_op jit(solution)/shard_map/pallas_call | solution.py:839
  597.2 14.0 %shard_map.240 = (bf16[512,1536]{1,0:T(8,128)(2,1)}, f32[512,1024]{1,0:T(8,128)}) custom-call(bf16[512,1024]{1,0:T(8,128)(2,1)} %copy-done.24, bf16[512,1536]{1,0:T(8,128)(2,1)} %get-tuple-element.519.projected, bf16[577,128,128]{2,1,0:T(8,128)(2,1)} %get-tuple-element.497.tile_set.qkv_tiles.proj_tiles.up_tiles.down_tiles, ...), custom_call_target="tpu_custom_call" | custom-call | flops 2684354560 | bytes 4194304 | tf_op jit(solution)/shard_map/pallas_call | solution.py:725
  612.2 10.0 shard_map.242
  622.1 10.6 shard_map.243
  632.8 13.8 %shard_map.239 = (bf16[512,1536]{1,0:T(8,128)(2,1)}, f32[512,1024]{1,0:T(8,128)}) custom-call(bf16[512,1024]{1,0:T(8,128)(2,1)} %bitcast.174, bf16[512,1536]{1,0:T(8,128)(2,1)} %get-tuple-element.517.projected, bf16[577,128,128]{2,1,0:T(8,128)(2,1)} %get-tuple-element.497.tile_set.qkv_tiles.proj_tiles.up_tiles.down_tiles, ...), custom_call_target="tpu_custom_call" | custom-call | flops 2684354560 | bytes 4194304 | tf_op jit(solution)/shard_map/pallas_call | solution.py:725
  691.0 12.5 %shard_map.248 = (bf16[512,2048]{1,0:T(8,128)(2,1)}, bf16[512,2048]{1,0:T(8,128)(2,1)}, f32[512,1024]{1,0:T(8,128)}) custom-call(bf16[512,1024]{1,0:T(8,128)(2,1)} %copy-done.23, f32[512,2048]{1,0:T(8,128)} %get-tuple-element.548.hidden, bf16[577,128,128]{2,1,0:T(8,128)(2,1)} %get-tuple-element.483.tile_set.qkv_tiles.proj_tiles.up_tiles.down_tiles, ...), custom_call_target="tpu_custom_call" | custom-call | flops 4294967296 | bytes 16777216 | tf_op jit(solution)/shard_map/pallas_call | solution.py:839
  713.0 12.8 %shard_map.247 = (bf16[512,2048]{1,0:T(8,128)(2,1)}, bf16[512,2048]{1,0:T(8,128)(2,1)}, f32[512,1024]{1,0:T(8,128)}) custom-call(bf16[512,1024]{1,0:T(8,128)(2,1)} %bitcast.170, f32[512,2048]{1,0:T(8,128)} %get-tuple-element.546.hidden, bf16[577,128,128]{2,1,0:T(8,128)(2,1)} %get-tuple-element.483.tile_set.qkv_tiles.proj_tiles.up_tiles.down_tiles, ...), custom_call_target="tpu_custom_call" | custom-call | flops 4294967296 | bytes 16777216 | tf_op jit(solution)/shard_map/pallas_call | solution.py:839
  747.4 13.8 %shard_map.251 = (bf16[512,1536]{1,0:T(8,128)(2,1)}, f32[512,1024]{1,0:T(8,128)}) custom-call(bf16[512,1024]{1,0:T(8,128)(2,1)} %copy-done.27, bf16[512,1536]{1,0:T(8,128)(2,1)} %get-tuple-element.555.projected, bf16[577,128,128]{2,1,0:T(8,128)(2,1)} %get-tuple-element.483.tile_set.qkv_tiles.proj_tiles.up_tiles.down_tiles, ...), custom_call_target="tpu_custom_call" | custom-call | flops 2684354560 | bytes 4194304 | tf_op jit(solution)/shard_map/pallas_call | solution.py:725
  761.4 9.6 shard_map.254.refs_4_
  778.0 10.1 shard_map.255.refs_4_
  792.7 14.0 %shard_map.250 = (bf16[512,1536]{1,0:T(8,128)(2,1)}, f32[512,1024]{1,0:T(8,128)}) custom-call(bf16[512,1024]{1,0:T(8,128)(2,1)} %bitcast.184, bf16[512,1536]{1,0:T(8,128)(2,1)} %get-tuple-element.553.projected, bf16[577,128,128]{2,1,0:T(8,128)(2,1)} %get-tuple-element.483.tile_set.qkv_tiles.proj_tiles.up_tiles.down_tiles, ...), custom_call_target="tpu_custom_call" | custom-call | flops 2684354560 | bytes 4194304 | tf_op jit(solution)/shard_map/pallas_call | solution.py:725
  872.2 9.7 collective-permute-start.81
  891.0 15.7 %collective-permute-done.83 = f32[16,2304]{1,0:T(8,128)} collective-permute-done((f32[16,2304]{1,0:T(8,128)}, f32[16,2304]{1,0:T(8,128)}, u32[]{:S(2)}, u32[]{:S(2)}) %collective-permute-start.83) | collective-permute-done | bytes 147488 | tf_op jit(solution)/shard_map/ppermute | solution.py:181
  971.0 13.1 %collective-permute-done.94 = bf16[25,128,128]{2,1,0:T(8,128)(2,1)S(1)} collective-permute-done((bf16[25,128,128]{2,1,0:T(8,128)(2,1)}, bf16[25,128,128]{2,1,0:T(8,128)(2,1)S(1)}, u32[]{:S(2)}, u32[]{:S(2)}) %collective-permute-start.94) | collective-permute-done | bytes 819232 | tf_op jit(solution)/shard_map/ppermute | solution.py:220
  1036.5 11.2 slice.503
  1057.7 11.2 collective-permute-done.107
  1083.6 25.3 %collective-permute-done.110 = bf16[48,128,128]{2,1,0:T(8,128)(2,1)S(1)} collective-permute-done((bf16[48,128,128]{2,1,0:T(8,128)(2,1)S(1)}, bf16[48,128,128]{2,1,0:T(8,128)(2,1)S(1)}, u32[]{:S(2)}, u32[]{:S(2)}) %collective-permute-start.110) | collective-permute-done | bytes 1572896 | tf_op jit(solution)/shard_map/ppermute | solution.py:185
  1134.3 13.1 %collective-permute-done.114 = bf16[48,128,128]{2,1,0:T(8,128)(2,1)} collective-permute-done((bf16[48,128,128]{2,1,0:T(8,128)(2,1)}, bf16[48,128,128]{2,1,0:T(8,128)(2,1)}, u32[]{:S(2)}, u32[]{:S(2)}) %collective-permute-start.114) | collective-permute-done | bytes 1572896 | tf_op jit(solution)/shard_map/ppermute | solution.py:185
  1195.0 17.5 %shard_map.260 = (f32[72,128,128]{2,1,0:T(8,128)}, f32[72,128,128]{2,1,0:T(8,128)}, f32[72,128,128]{2,1,0:T(8,128)}, bf16[72,128,128]{2,1,0:T(8,128)(2,1)}) custom-call(f32[1,1]{1,0:T(1,128)} %bitcast.66.clip, f32[72,128,128]{2,1,0:T(8,128)} %get-tuple-element.615.grad, f32[72,128,128]{2,1,0:T(8,128)} %bitcast.161, f32[72,128,128]{2,1,0:T(8,128)} %bitcast.162, ...), custom_call_target="tpu_custom_call" | custom-call | flops 35389440 | bytes 35389440 | tf_op jit(solution)/shard_map/pallas_call | solution.py:1265
  (732 shorter events, 747.6 us)
Async XLA Ops:
  3.4 37.0 %collective-permute-start.9 = (bf16[47,128,128]{2,1,0:T(8,128)(2,1)}, bf16[47,128,128]{2,1,0:T(8,128)(2,1)}, u32[]{:S(2)}, u32[]{:S(2)}) collective-permute-start(bf16[47,128,128]{2,1,0:T(8,128)(2,1)} %slice_bitcast_fusion.refs_0_), channel_id=1, source_target_pairs={{0,2},{2,0},{1,3},{3,1},{4,6},{6,4},{5,7},{7,5},{8,10},{10,8},{9,1... | collective-permute-start | bytes 4620296 | tf_op jit(solution)/shard_map/ppermute | solution.py:181
  6.3 36.1 %collective-permute-start.8 = (bf16[47,128,128]{2,1,0:T(8,128)(2,1)}, bf16[47,128,128]{2,1,0:T(8,128)(2,1)}, u32[]{:S(2)}, u32[]{:S(2)}) collective-permute-start(bf16[47,128,128]{2,1,0:T(8,128)(2,1)} %slice_bitcast_fusion.refs_0_), channel_id=1, source_target_pairs={{0,4},{4,0},{8,12},{12,8},{16,20},{20,16},{24,28},{28,24},{1,5},{5... | collective-permute-start | bytes 4620296 | tf_op jit(solution)/shard_map/ppermute | solution.py:185
  7.8 36.7 %collective-permute-start.10 = (bf16[47,128,128]{2,1,0:T(8,128)(2,1)}, bf16[47,128,128]{2,1,0:T(8,128)(2,1)S(1)}, u32[]{:S(2)}, u32[]{:S(2)}) collective-permute-start(bf16[47,128,128]{2,1,0:T(8,128)(2,1)} %slice_bitcast_fusion.refs_0_), channel_id=1, source_target_pairs={{0,8},{4,12},{8,16},{12,20},{16,24},{20,28},{1,9},{5,13},{9,17},{1... | collective-permute-start | bytes 4620296 | tf_op jit(solution)/shard_map/ppermute | solution.py:220
  11.4 36.7 %collective-permute-start.11 = (bf16[47,128,128]{2,1,0:T(8,128)(2,1)}, bf16[47,128,128]{2,1,0:T(8,128)(2,1)S(1)}, u32[]{:S(2)}, u32[]{:S(2)}) collective-permute-start(bf16[47,128,128]{2,1,0:T(8,128)(2,1)} %slice_bitcast_fusion.refs_0_), channel_id=1, source_target_pairs={{8,0},{12,4},{16,8},{20,12},{24,16},{28,20},{9,1},{13,5},{17,9},{2... | collective-permute-start | bytes 4620296 | tf_op jit(solution)/shard_map/ppermute | solution.py:220
  111.0 38.6 %collective-permute-start.22 = (bf16[47,128,128]{2,1,0:T(8,128)(2,1)}, bf16[47,128,128]{2,1,0:T(8,128)(2,1)S(1)}, u32[]{:S(2)}, u32[]{:S(2)}) collective-permute-start(bf16[47,128,128]{2,1,0:T(8,128)(2,1)} %broadcast_select_fusion.2.refs_0_), channel_id=1, source_target_pairs={{0,2},{2,0},{1,3},{3,1},{4,6},{6,4},{5,7},{7,5},{8,10},{10,8},{9,1... | collective-permute-start | bytes 4620296 | tf_op jit(solution)/shard_map/ppermute | solution.py:181
  112.5 39.2 %collective-permute-start.23 = (bf16[47,128,128]{2,1,0:T(8,128)(2,1)}, bf16[47,128,128]{2,1,0:T(8,128)(2,1)S(1)}, u32[]{:S(2)}, u32[]{:S(2)}) collective-permute-start(bf16[47,128,128]{2,1,0:T(8,128)(2,1)} %broadcast_select_fusion.2.refs_0_), channel_id=1, source_target_pairs={{0,4},{4,0},{8,12},{12,8},{16,20},{20,16},{24,28},{28,24},{1,5},{5... | collective-permute-start | bytes 4620296 | tf_op jit(solution)/shard_map/ppermute | solution.py:185
  113.0 40.7 %collective-permute-start.24 = (bf16[47,128,128]{2,1,0:T(8,128)(2,1)}, bf16[47,128,128]{2,1,0:T(8,128)(2,1)}, u32[]{:S(2)}, u32[]{:S(2)}) collective-permute-start(bf16[47,128,128]{2,1,0:T(8,128)(2,1)} %copy-done.11), channel_id=1, source_target_pairs={{8,16},{12,20},{16,24},{20,28},{9,17},{13,21},{17,25},{21,29},{10,... | collective-permute-start | bytes 4620296 | tf_op jit(solution)/shard_map/ppermute | solution.py:220
  143.7 112.7 %collective-permute-start.21 = (bf16[4,2,2,1090,128]{4,0,3,2,1:T(4,128)(2,1)}, bf16[4,2,2,1090,128]{4,0,3,2,1:T(4,128)(2,1)}, u32[]{:S(2)}, u32[]{:S(2)}) collective-permute-start(bf16[4,2,2,1090,128]{4,0,3,2,1:T(4,128)(2,1)} %copy.111), channel_id=1, source_target_pairs={{0,1},{1,0},{2,3},{3,2},{4,5},{5,4},{6,7},{7,6},{8,9},{9,8},{10,11... | collective-permute-start | bytes 13393928 | tf_op jit(solution)/shard_map/ppermute | solution.py:177
  182.3 34.0 %collective-permute-start.30 = (bf16[47,128,128]{2,1,0:T(8,128)(2,1)}, bf16[47,128,128]{2,1,0:T(8,128)(2,1)}, u32[]{:S(2)}, u32[]{:S(2)}) collective-permute-start(bf16[47,128,128]{2,1,0:T(8,128)(2,1)} %collective-permute-done.25), channel_id=1, source_target_pairs={{8,0},{12,4},{9,1},{13,5},{10,2},{14,6},{11,3},{15,7}} | collective-permute-start | bytes 4620296 | tf_op jit(solution)/shard_map/ppermute | solution.py:220
  248.1 51.6 %collective-permute-start.40 = (bf16[25,128,128]{2,1,0:T(8,128)(2,1)}, bf16[25,128,128]{2,1,0:T(8,128)(2,1)}, u32[]{:S(2)}, u32[]{:S(2)}) collective-permute-start(bf16[25,128,128]{2,1,0:T(8,128)(2,1)} %collective-permute-done.34), channel_id=1, source_target_pairs={{16,24},{20,28},{17,25},{21,29},{18,26},{22,30},{19,27},{23,31}} | collective-permute-start | bytes 2457608 | tf_op jit(solution)/shard_map/ppermute | solution.py:220
  249.9 49.9 %collective-permute-start.41 = (bf16[25,128,128]{2,1,0:T(8,128)(2,1)}, bf16[25,128,128]{2,1,0:T(8,128)(2,1)}, u32[]{:S(2)}, u32[]{:S(2)}) collective-permute-start(bf16[25,128,128]{2,1,0:T(8,128)(2,1)} %collective-permute-done.35), channel_id=1, source_target_pairs={{8,0},{12,4},{9,1},{13,5},{10,2},{14,6},{11,3},{15,7}} | collective-permute-start | bytes 2457608 | tf_op jit(solution)/shard_map/ppermute | solution.py:220
  251.2 46.1 %collective-permute-start.38 = (bf16[47,128,128]{2,1,0:T(8,128)(2,1)}, bf16[47,128,128]{2,1,0:T(8,128)(2,1)}, u32[]{:S(2)}, u32[]{:S(2)}) collective-permute-start(bf16[47,128,128]{2,1,0:T(8,128)(2,1)} %select_select_fusion.refs_0_), channel_id=1, source_target_pairs={{0,2},{2,0},{1,3},{3,1},{4,6},{6,4},{5,7},{7,5},{8,10},{10,8},{9,1... | collective-permute-start | bytes 4620296 | tf_op jit(solution)/shard_map/ppermute | solution.py:181
  254.9 43.6 %collective-permute-start.39 = (bf16[47,128,128]{2,1,0:T(8,128)(2,1)}, bf16[47,128,128]{2,1,0:T(8,128)(2,1)}, u32[]{:S(2)}, u32[]{:S(2)}) collective-permute-start(bf16[47,128,128]{2,1,0:T(8,128)(2,1)} %select_select_fusion.refs_0_), channel_id=1, source_target_pairs={{0,4},{4,0},{8,12},{12,8},{16,20},{20,16},{24,28},{28,24},{1,5},{5... | collective-permute-start | bytes 4620296 | tf_op jit(solution)/shard_map/ppermute | solution.py:185
  328.6 73.4 %collective-permute-start.45 = (bf16[100,128,128]{2,1,0:T(8,128)(2,1)S(1)}, bf16[100,128,128]{2,1,0:T(8,128)(2,1)}, u32[]{:S(2)}, u32[]{:S(2)}) collective-permute-start(bf16[100,128,128]{2,1,0:T(8,128)(2,1)S(1)} %copy-done.3), channel_id=1, source_target_pairs={{0,4},{4,0},{8,12},{12,8},{16,20},{20,16},{24,28},{28,24},{1,5},{5... | collective-permute-start | bytes 9830408 | tf_op jit(solution)/shard_map/ppermute | solution.py:185
  329.9 73.1 %collective-permute-start.46 = (bf16[100,128,128]{2,1,0:T(8,128)(2,1)S(1)}, bf16[100,128,128]{2,1,0:T(8,128)(2,1)}, u32[]{:S(2)}, u32[]{:S(2)}) collective-permute-start(bf16[100,128,128]{2,1,0:T(8,128)(2,1)S(1)} %copy-done.3), channel_id=1, source_target_pairs={{0,2},{2,0},{1,3},{3,1},{4,6},{6,4},{5,7},{7,5},{8,10},{10,8},{9,1... | collective-permute-start | bytes 9830408 | tf_op jit(solution)/shard_map/ppermute | solution.py:181
  346.8 65.2 %collective-permute-start.48 = (f32[512,1024]{1,0:T(8,128)}, f32[512,1024]{1,0:T(8,128)S(1)}, u32[]{:S(2)}, u32[]{:S(2)}) collective-permute-start(f32[512,1024]{1,0:T(8,128)} %get-tuple-element.487), channel_id=1, source_target_pairs={{0,1},{1,0},{2,3},{3,2},{4,5},{5,4},{6,7},{7,6},{8,9},{9,8},{10,11... | collective-permute-start | bytes 6291464 | tf_op jit(solution)/shard_map/ppermute | solution.py:177
  421.6 38.4 %collective-permute-start.51 = (bf16[50,128,128]{2,1,0:T(8,128)(2,1)S(1)}, bf16[50,128,128]{2,1,0:T(8,128)(2,1)}, u32[]{:S(2)}, u32[]{:S(2)}) collective-permute-start(bf16[50,128,128]{2,1,0:T(8,128)(2,1)S(1)} %slice.444), channel_id=1, source_target_pairs={{0,2},{2,0},{1,3},{3,1},{4,6},{6,4},{5,7},{7,5},{8,10},{10,8},{9,1... | collective-permute-start | bytes 4915208 | tf_op jit(solution)/shard_map/ppermute | solution.py:181
  422.2 38.0 %collective-permute-start.52 = (bf16[50,128,128]{2,1,0:T(8,128)(2,1)S(1)}, bf16[50,128,128]{2,1,0:T(8,128)(2,1)}, u32[]{:S(2)}, u32[]{:S(2)}) collective-permute-start(bf16[50,128,128]{2,1,0:T(8,128)(2,1)S(1)} %slice.445), channel_id=1, source_target_pairs={{0,4},{4,0},{8,12},{12,8},{16,20},{20,16},{24,28},{28,24},{1,5},{5... | collective-permute-start | bytes 4915208 | tf_op jit(solution)/shard_map/ppermute | solution.py:185
  434.4 38.5 %collective-permute-start.50 = (f32[512,1024]{1,0:T(8,128)}, f32[512,1024]{1,0:T(8,128)S(1)}, u32[]{:S(2)}, u32[]{:S(2)}) collective-permute-start(f32[512,1024]{1,0:T(8,128)} %get-tuple-element.491), channel_id=1, source_target_pairs={{0,1},{1,0},{2,3},{3,2},{4,5},{5,4},{6,7},{7,6},{8,9},{9,8},{10,11... | collective-permute-start | bytes 6291464 | tf_op jit(solution)/shard_map/ppermute | solution.py:177
  611.2 41.5 %collective-permute-start.61 = (f32[512,1024]{1,0:T(8,128)}, f32[512,1024]{1,0:T(8,128)S(1)}, u32[]{:S(2)}, u32[]{:S(2)}) collective-permute-start(f32[512,1024]{1,0:T(8,128)} %get-tuple-element.520), channel_id=1, source_target_pairs={{0,1},{1,0},{2,3},{3,2},{4,5},{5,4},{6,7},{7,6},{8,9},{9,8},{10,11... | collective-permute-start | bytes 6291464 | tf_op jit(solution)/shard_map/ppermute | solution.py:177
  687.9 38.2 %collective-permute-start.67 = (bf16[50,128,128]{2,1,0:T(8,128)(2,1)}, bf16[50,128,128]{2,1,0:T(8,128)(2,1)}, u32[]{:S(2)}, u32[]{:S(2)}) collective-permute-start(bf16[50,128,128]{2,1,0:T(8,128)(2,1)} %get-tuple-element.558), channel_id=1, source_target_pairs={{0,2},{2,0},{1,3},{3,1},{4,6},{6,4},{5,7},{7,5},{8,10},{10,8},{9,1... | collective-permute-start | bytes 4915208 | tf_op jit(solution)/shard_map/ppermute | solution.py:181
  689.4 37.9 %collective-permute-start.68 = (bf16[50,128,128]{2,1,0:T(8,128)(2,1)}, bf16[50,128,128]{2,1,0:T(8,128)(2,1)}, u32[]{:S(2)}, u32[]{:S(2)}) collective-permute-start(bf16[50,128,128]{2,1,0:T(8,128)(2,1)} %get-tuple-element.559), channel_id=1, source_target_pairs={{0,4},{4,0},{8,12},{12,8},{16,20},{20,16},{24,28},{28,24},{1,5},{5... | collective-permute-start | bytes 4915208 | tf_op jit(solution)/shard_map/ppermute | solution.py:185
  742.3 81.2 %collective-permute-start.71 = (bf16[100,128,128]{2,1,0:T(8,128)(2,1)}, bf16[100,128,128]{2,1,0:T(8,128)(2,1)}, u32[]{:S(2)}, u32[]{:S(2)}) collective-permute-start(bf16[100,128,128]{2,1,0:T(8,128)(2,1)} %pad_maximum_fusion.4), channel_id=1, source_target_pairs={{0,4},{4,0},{8,12},{12,8},{16,20},{20,16},{24,28},{28,24},{1,5},{5... | collective-permute-start | bytes 9830408 | tf_op jit(solution)/shard_map/ppermute | solution.py:185
  743.0 80.5 %collective-permute-start.72 = (bf16[100,128,128]{2,1,0:T(8,128)(2,1)}, bf16[100,128,128]{2,1,0:T(8,128)(2,1)}, u32[]{:S(2)}, u32[]{:S(2)}) collective-permute-start(bf16[100,128,128]{2,1,0:T(8,128)(2,1)} %pad_maximum_fusion.5), channel_id=1, source_target_pairs={{0,2},{2,0},{1,3},{3,1},{4,6},{6,4},{5,7},{7,5},{8,10},{10,8},{9,1... | collective-permute-start | bytes 9830408 | tf_op jit(solution)/shard_map/ppermute | solution.py:181
  761.2 72.3 %collective-permute-start.66 = (f32[512,1024]{1,0:T(8,128)}, f32[512,1024]{1,0:T(8,128)S(1)}, u32[]{:S(2)}, u32[]{:S(2)}) collective-permute-start(f32[512,1024]{1,0:T(8,128)} %get-tuple-element.556), channel_id=1, source_target_pairs={{0,1},{1,0},{2,3},{3,2},{4,5},{5,4},{6,7},{7,6},{8,9},{9,8},{10,11... | collective-permute-start | bytes 6291464 | tf_op jit(solution)/shard_map/ppermute | solution.py:177
  872.2 39.0 %collective-permute-start.81 = (bf16[25,128,128]{2,1,0:T(8,128)(2,1)}, bf16[25,128,128]{2,1,0:T(8,128)(2,1)}, u32[]{:S(2)}, u32[]{:S(2)}) collective-permute-start(bf16[25,128,128]{2,1,0:T(8,128)(2,1)} %slice.593), channel_id=1, source_target_pairs={{0,8},{4,12},{1,9},{5,13},{2,10},{6,14},{3,11},{7,15}} | collective-permute-start | bytes 2457608 | tf_op jit(solution)/shard_map/ppermute | solution.py:220
  946.2 41.9 %collective-permute-start.92 = (bf16[48,128,128]{2,1,0:T(8,128)(2,1)}, bf16[48,128,128]{2,1,0:T(8,128)(2,1)S(1)}, u32[]{:S(2)}, u32[]{:S(2)}) collective-permute-start(bf16[48,128,128]{2,1,0:T(8,128)(2,1)} %pad_maximum_fusion.6), channel_id=1, source_target_pairs={{0,4},{4,0},{8,12},{12,8},{16,20},{20,16},{24,28},{28,24},{1,5},{5... | collective-permute-start | bytes 4718600 | tf_op jit(solution)/shard_map/ppermute | solution.py:185
  946.8 41.3 %collective-permute-start.93 = (bf16[48,128,128]{2,1,0:T(8,128)(2,1)}, bf16[48,128,128]{2,1,0:T(8,128)(2,1)}, u32[]{:S(2)}, u32[]{:S(2)}) collective-permute-start(bf16[48,128,128]{2,1,0:T(8,128)(2,1)} %pad_maximum_fusion.7), channel_id=1, source_target_pairs={{0,2},{2,0},{1,3},{3,1},{4,6},{6,4},{5,7},{7,5},{8,10},{10,8},{9,1... | collective-permute-start | bytes 4718600 | tf_op jit(solution)/shard_map/ppermute | solution.py:181
  1009.0 40.2 %collective-permute-start.103 = (bf16[48,128,128]{2,1,0:T(8,128)(2,1)}, bf16[48,128,128]{2,1,0:T(8,128)(2,1)}, u32[]{:S(2)}, u32[]{:S(2)}) collective-permute-start(bf16[48,128,128]{2,1,0:T(8,128)(2,1)} %pad_maximum_fusion.8), channel_id=1, source_target_pairs={{0,4},{4,0},{8,12},{12,8},{16,20},{20,16},{24,28},{28,24},{1,5},{5... | collective-permute-start | bytes 4718600 | tf_op jit(solution)/shard_map/ppermute | solution.py:185
  1010.4 38.9 %collective-permute-start.104 = (bf16[48,128,128]{2,1,0:T(8,128)(2,1)}, bf16[48,128,128]{2,1,0:T(8,128)(2,1)}, u32[]{:S(2)}, u32[]{:S(2)}) collective-permute-start(bf16[48,128,128]{2,1,0:T(8,128)(2,1)} %pad_maximum_fusion.9), channel_id=1, source_target_pairs={{0,2},{2,0},{1,3},{3,1},{4,6},{6,4},{5,7},{7,5},{8,10},{10,8},{9,1... | collective-permute-start | bytes 4718600 | tf_op jit(solution)/shard_map/ppermute | solution.py:181
  1011.1 38.2 %collective-permute-start.105 = (bf16[48,128,128]{2,1,0:T(8,128)(2,1)}, bf16[48,128,128]{2,1,0:T(8,128)(2,1)}, u32[]{:S(2)}, u32[]{:S(2)}) collective-permute-start(bf16[48,128,128]{2,1,0:T(8,128)(2,1)} %fusion.18), channel_id=1, source_target_pairs={{0,8},{4,12},{1,9},{5,13},{2,10},{6,14},{3,11},{7,15}} | collective-permute-start | bytes 4718600 | tf_op jit(solution)/shard_map/ppermute | solution.py:220
  1116.8 33.8 %collective-permute-start.116 = (bf16[48,128,128]{2,1,0:T(8,128)(2,1)}, bf16[48,128,128]{2,1,0:T(8,128)(2,1)}, u32[]{:S(2)}, u32[]{:S(2)}) collective-permute-start(bf16[48,128,128]{2,1,0:T(8,128)(2,1)} %get-tuple-element.613), channel_id=1, source_target_pairs={{0,8},{4,12},{8,16},{12,20},{16,24},{20,28},{1,9},{5,13},{9,17},{1... | collective-permute-start | bytes 4718600 | tf_op jit(solution)/shard_map/ppermute | solution.py:220
  (207 other events, 2771.9 us)
